TPU v7x, 512 devices: a whole 4x4x16 slice. The times are simulated.
512 devices in a mesh: mem: 64 (over z, x), camp: 8 (over y, core).
Axes of the slice: x: 4, y: 4, z: 16, core: 2. Of those that a mesh axis runs over, the one named last changes fastest.
Arguments:
- gains: bfloat16 [2560, 128, 1024], P('mem', None, 'camp'), may hold values from -14 to 14
- costs: bfloat16 [2560, 128, 1024], P('mem', None, 'camp'), may hold values from 0.5 to 2
- tile_rows: int32 [2560, 8], P('mem', 'camp'), may hold values from 0 to 7, as said below
- tile_cols: int32 [2560, 8], P('mem', 'camp'), may hold values from 0 to 1023
- tile_count: int32 [64, 8], P('mem', 'camp'), may hold values from 1 to 40, as said below
- duals: float32 [1048576], P('camp'), may hold values from 0.005 to 0.04
- allowances: float32 [1048576], P('camp'), may hold values from 0.02 to 0.16
Outputs:
- duals_out: float32 [1048576], P('camp')
- usage_out: float32 [1048576], P('camp')
- unused_share: float32 [65536], P('mem')
Inputs may be any that keep to these rules, and one draw needn't show every extreme that they name: `tile_rows`: the live slots of one device name distinct pairs of member block and campaign block. `tile_count`: some device has all 40 slots live.
All inputs are finite; a program needn't handle non-finite values.
Results may differ from a plain program's by a relative error of at most 0.0003.
Values sent between devices are 32-bit elements; how exact they have to be, the bound alone decides.
No kernel may reach another device: no remote copies, remote signals or barrier semaphores. Data moves between devices by JAX's collectives and lax.ppermute only.
A program may use at most 64 MiB of HBM per device.

v0:
```python
import jax
import jax.numpy as jnp
from jax import lax
from jax.sharding import PartitionSpec as P

MB = 8
ROUNDS = 3


SMOOTHING = 0.05
STEP_SIZE = 0.2


def local(gains, costs, tile_rows, tile_cols, tile_count, duals, allowances):
    slots = gains.shape[0]
    tile = gains.shape[1]
    camp_blocks = duals.shape[0] // tile
    live_slot = jnp.arange(slots) < tile_count[0, 0]
    member_block = tile_rows[:, 0]
    camp_block = tile_cols[:, 0]
    onehot = (member_block[None, :] == jnp.arange(MB)[:, None]) & live_slot[None, :]
    onehot_f = onehot.astype(jnp.float32)
    gain_f = gains.astype(jnp.float32)
    cost_f = costs.astype(jnp.float32)
    price = duals
    usage = jnp.zeros_like(duals)
    row_top = jnp.zeros((MB, tile), jnp.float32)
    denom = jnp.ones((MB, tile), jnp.float32)
    for step in range(ROUNDS):
        price_tile = jnp.take(price.reshape(camp_blocks, tile), camp_block, axis=0)
        scores = (gain_f - cost_f * price_tile[:, None, :]) / SMOOTHING
        tile_top = jnp.max(scores, axis=2)
        local_top = jnp.maximum(
            jnp.max(jnp.where(onehot[:, :, None], tile_top[None], -jnp.inf), axis=1), 0.0
        )
        row_top = lax.pmax(local_top, "camp")
        exponent = jnp.exp(scores - jnp.take(row_top, member_block, axis=0)[:, :, None])
        tile_sum = jnp.where(live_slot[:, None], jnp.sum(exponent, axis=2), 0.0)
        local_sum = jnp.dot(onehot_f, tile_sum, precision=lax.Precision.HIGHEST)
        row_sum = lax.psum(local_sum, "camp")
        denom = jnp.exp(-row_top) + row_sum
        alloc = exponent / jnp.take(denom, member_block, axis=0)[:, :, None]
        column_use = jnp.where(live_slot[:, None], jnp.sum(cost_f * alloc, axis=1), 0.0)
        local_use = jax.ops.segment_sum(column_use, camp_block, num_segments=camp_blocks).reshape(
            -1
        )
        usage = lax.psum(local_use, "mem")
        price = jnp.maximum(price + STEP_SIZE * (usage - allowances), 0.0)
    unused_share = (jnp.exp(-row_top) / denom).reshape(-1)
    return (price, usage, unused_share)


def solution(mesh):
    return jax.shard_map(
        local,
        mesh=mesh,
        in_specs=(
            P("mem", None, "camp"),
            P("mem", None, "camp"),
            P("mem", "camp"),
            P("mem", "camp"),
            P("mem", "camp"),
            P("camp"),
            P("camp"),
        ),
        out_specs=(P("camp"), P("camp"), P("mem")),
        check_vma=False,
    )
```

profile of v0, /device:TPU:8, one launch (start us, length us, event | category | flops | bytes accessed | tf_op | source)
XLA Modules:
  0.0 916.5 jit_solution(14654936360261097139)
XLA Ops:
  11.2 1.6 gather_fusion
  12.9 2.6 fusion.7
  15.7 14.8 %pmax.21 = f32[8,128]{1,0:T(8,128)S(1)} all-reduce(f32[8,128]{1,0:T(8,128)S(1)} %broadcast_maximum_fusion.2), channel_id=1, replica_groups=mesh['mem'=64,'camp'=8] {'camp'}, use_global_device_ids=true, to_apply=%region_2.4 | all-reduce | flops 1024 | bytes 8192 | tf_op jit(solution)/shard_map/pmax | solution.py:36
  31.1 1.7 fusion.6
  33.0 12.9 %psum.42 = f32[8,128]{1,0:T(8,128)S(1)} all-reduce(f32[8,128]{1,0:T(8,128)S(1)} %fusion.26), channel_id=1, replica_groups=mesh['mem'=64,'camp'=8] {'camp'}, use_global_device_ids=true, to_apply=%region_4.7 | all-reduce | flops 1024 | bytes 8192 | tf_op jit(solution)/shard_map/psum | solution.py:40
  46.6 1.8 fusion.3
  48.4 1.7 scatter_custom_fusion
  50.2 267.3 %all-reduce.4.cloned.1.call-done = f32[131072]{0:T(1024)} async-done(((f32[131072]{0:T(1024)}), f32[131072]{0:T(1024)}) %all-reduce.4.cloned.1.call-update) | async-done | bytes 524304 | tf_op jit(solution)/shard_map/psum | solution.py:47
  317.5 2.1 fusion.18
  319.5 1.6 gather_fusion.3
  322.1 10.0 %pmax.22 = f32[8,128]{1,0:T(8,128)S(1)} all-reduce(f32[8,128]{1,0:T(8,128)S(1)} %broadcast_maximum_fusion.1), channel_id=1, replica_groups=mesh['mem'=64,'camp'=8] {'camp'}, use_global_device_ids=true, to_apply=%region_10.13 | all-reduce | flops 1024 | bytes 8192 | tf_op jit(solution)/shard_map/pmax | solution.py:36
  332.8 1.7 fusion.8
  334.7 12.4 %psum.44 = f32[8,128]{1,0:T(8,128)S(1)} all-reduce(f32[8,128]{1,0:T(8,128)S(1)} %fusion.23), channel_id=1, replica_groups=mesh['mem'=64,'camp'=8] {'camp'}, use_global_device_ids=true, to_apply=%region_12.15 | all-reduce | flops 1024 | bytes 8192 | tf_op jit(solution)/shard_map/psum | solution.py:40
  347.7 1.8 fusion.4
  349.5 1.7 scatter_custom_fusion.1
  351.3 260.4 %all-reduce.6.cloned.1.call-done = f32[131072]{0:T(1024)} async-done(((f32[131072]{0:T(1024)}), f32[131072]{0:T(1024)}) %all-reduce.6.cloned.1.call-update) | async-done | bytes 524304 | tf_op jit(solution)/shard_map/psum | solution.py:47
  611.7 2.3 fusion.48
  616.6 10.0 %pmax.23 = f32[8,128]{1,0:T(8,128)S(1)} all-reduce(f32[8,128]{1,0:T(8,128)S(1)} %broadcast_maximum_fusion), channel_id=1, replica_groups=mesh['mem'=64,'camp'=8] {'camp'}, use_global_device_ids=true, to_apply=%region_18.21 | all-reduce | flops 1024 | bytes 8192 | tf_op jit(solution)/shard_map/pmax | solution.py:36
  627.2 1.7 fusion.10
  629.1 12.4 %psum.46 = f32[8,128]{1,0:T(8,128)S(1)} all-reduce(f32[8,128]{1,0:T(8,128)S(1)} %fusion.20), channel_id=1, replica_groups=mesh['mem'=64,'camp'=8] {'camp'}, use_global_device_ids=true, to_apply=%region_20.23 | all-reduce | flops 1024 | bytes 8192 | tf_op jit(solution)/shard_map/psum | solution.py:40
  642.8 1.8 fusion.5
  644.6 1.8 scatter_custom_fusion.2
  646.4 260.4 %all-reduce.8.cloned.1.call-done = f32[131072]{0:T(1024)} async-done(((f32[131072]{0:T(1024)}), f32[131072]{0:T(1024)}) %all-reduce.8.cloned.1.call-update) | async-done | bytes 524304 | tf_op jit(solution)/shard_map/psum | solution.py:47
  906.9 2.3 add_maximum_fusion
  (59 shorter events, 13.2 us)
Async XLA Ops:
  7.2 310.3 %all-reduce.4.cloned.1.call-start = ((), (), s32[]{:S(2)}) async-start(), calls=%async_computation | async-start | bytes 1048576 | tf_op jit(solution)/shard_map/psum | solution.py:47
  12.9 18.2 %copy-start = (bf16[40,128,128]{2,1,0:T(8,128)(2,1)S(1)}, bf16[40,128,128]{2,1,0:T(8,128)(2,1)}, u32[]{:S(2)}) copy-start(bf16[40,128,128]{2,1,0:T(8,128)(2,1)} %param.12) | copy-start | bytes 3932164
  12.9 18.2 %copy-start.1 = (bf16[40,128,128]{2,1,0:T(8,128)(2,1)S(1)}, bf16[40,128,128]{2,1,0:T(8,128)(2,1)}, u32[]{:S(2)}) copy-start(bf16[40,128,128]{2,1,0:T(8,128)(2,1)} %param.11) | copy-start | bytes 3932164
  31.1 1.7 copy-start.6
  46.6 270.9 %copy-start.2 = (f32[131072]{0:T(1024)S(1)}, f32[131072]{0:T(1024)}, u32[]{:S(2)}) copy-start(f32[131072]{0:T(1024)} %param.16) | copy-start | bytes 1572868
  50.2 561.5 %all-reduce.6.cloned.1.call-start = ((), (), s32[]{:S(2)}) async-start(), calls=%async_computation.1 | async-start | bytes 1048576 | tf_op jit(solution)/shard_map/psum | solution.py:47
  351.3 555.6 %all-reduce.8.cloned.1.call-start = ((), (), s32[]{:S(2)}) async-start(), calls=%async_computation.2 | async-start | bytes 1048576 | tf_op jit(solution)/shard_map/psum | solution.py:47
  644.6 262.3 %copy-start.3 = (f32[131072]{0:T(1024)S(1)}, f32[131072]{0:T(1024)}, u32[]{:S(2)}) copy-start(f32[131072]{0:T(1024)} %param.17) | copy-start | bytes 1572868
  644.6 262.3 %copy-start.4 = (f32[131072]{0:T(1024)S(1)}, f32[131072]{0:T(1024)}, u32[]{:S(2)}) copy-start(f32[131072]{0:T(1024)} %all-reduce.4.cloned.1.call-done) | copy-start | bytes 1572868
  906.8 2.3 copy-start.5
Sparse Core Ops, SparseCore 0:
  50.3 267.1 all-reduce.3
  351.4 260.2 all-reduce.5
  646.6 260.2 all-reduce.7
where the time goes:
time: 917 us; the launch traced here: 916 us
  waiting for transfers between devices  788 us (86%)
  blocking collectives  72.5 us (8%)
  other arithmetic  31.4 us (3%)
  between operations  14.6 us (2%)
  local copies, waits for them, and re-layouts  9.2 us (1%)
    psum x3, waiting for transfers between devices, local(): usage = lax.psum(local_use, 'mem')  788 us
    psum x3, blocking collectives, local(): row_sum = lax.psum(local_sum, 'camp')  37.7 us
    pmax x3, blocking collectives, local(): row_top = lax.pmax(local_top, 'camp')  34.8 us
  transfers between devices with their start and end apart: 3, of which 3 were waited for; matrix products, arithmetic and copies ran while one was open for 0% of the time, Pallas kernels for 0%

commit v1 on v0

v1 whole, which is shorter than its diff:
```python
import jax
import jax.numpy as jnp
from jax import lax
from jax.sharding import Mesh, PartitionSpec as P

MB = 8
ROUNDS = 3
SMOOTHING = 0.05
STEP_SIZE = 0.2
NZ, NX, NY, NC = 16, 4, 4, 2
CAMP = ("y", "core")


def spread(block, axis, count):
    sent = jnp.broadcast_to(block[None], (count,) + block.shape)
    return lax.all_to_all(sent, axis, 0, 0)


def split(values):
    high = lax.reduce_precision(values, 8, 7)
    return high.astype(jnp.bfloat16), (values - high).astype(jnp.bfloat16)


def local(gains, costs, tile_rows, tile_cols, tile_count, duals, allowances):
    slots = gains.shape[0]
    tile = gains.shape[1]
    camp_blocks = duals.shape[0] // tile
    live_slot = jnp.arange(slots) < tile_count[0, 0]
    member_block = tile_rows[:, 0]
    camp_block = tile_cols[:, 0]
    onehot = (member_block[None, :] == jnp.arange(MB)[:, None]) & live_slot[None, :]
    onehot_f = onehot.astype(jnp.float32)
    gain_f = gains.astype(jnp.float32)
    cost_f = costs.astype(jnp.float32)
    price = jnp.take(duals.reshape(camp_blocks, tile), camp_block, axis=0)
    allowance = jnp.take(allowances.reshape(camp_blocks, tile), camp_block, axis=0)

    ids_row = jnp.pad(camp_block.astype(jnp.float32), (0, tile - slots))[None]
    cols_x = spread(ids_row, "x", NX)[:, 0, :slots].reshape(-1)
    history = []
    cols_z = None
    for step in range(ROUNDS):
        scores = (gain_f - cost_f * price[:, None, :]) / SMOOTHING
        tile_top = jnp.max(scores, axis=2)
        local_top = jnp.maximum(
            jnp.max(jnp.where(onehot[:, :, None], tile_top[None], -jnp.inf), axis=1), 0.0
        )
        exponent = jnp.exp(scores - jnp.take(local_top, member_block, axis=0)[:, :, None])
        tile_sum = jnp.where(live_slot[:, None], jnp.sum(exponent, axis=2), 0.0)
        local_sum = jnp.dot(onehot_f, tile_sum, precision=lax.Precision.HIGHEST)
        both = spread(jnp.concatenate([local_top, local_sum]), CAMP, NY * NC)
        tops, sums = both[:, :MB], both[:, MB:]
        row_top = jnp.max(tops, axis=0)
        spare = jnp.exp(-row_top)
        denom = spare + jnp.sum(sums * jnp.exp(tops - row_top), axis=0)
        weight = jnp.exp(local_top - row_top) / denom
        weighted = exponent * jnp.take(weight, member_block, axis=0)[:, :, None]
        column_use = jnp.where(live_slot[:, None], jnp.sum(cost_f * weighted, axis=1), 0.0)
        if step == 0:
            sent = jnp.concatenate([column_use, ids_row, jnp.zeros((7, tile), jnp.float32)])
            got = spread(sent, "z", NZ)
            cols_z = got[:, slots, :slots].reshape(-1)
            pulled = (cols_x[:, None] == cols_z[None, :]).astype(jnp.float32)
            column_z = got[:, :slots].reshape(-1, tile)
            history.append(lax.all_gather(got, "x"))
        else:
            column_z = spread(column_use, "z", NZ).reshape(-1, tile)
            if step < ROUNDS - 1:
                history.append(lax.all_gather(column_z, "x"))
            else:
                history.append(spread(column_z, "x", NX))
        if step < ROUNDS - 1:
            asked = jnp.dot(pulled, column_z, precision=lax.Precision.HIGHEST)
            use = jnp.sum(lax.all_to_all(asked.reshape(NX, slots, tile), "x", 0, 0), axis=0)
            price = jnp.maximum(price + STEP_SIZE * (use - allowance), 0.0)

    unused_share = (spare / denom).reshape(-1)

    first = history[0]
    all_cols = first[:, :, slots, :slots].reshape(-1)
    history[0] = first[:, :, :slots]
    values = jnp.concatenate([h.reshape(-1, tile) for h in history], axis=1)
    high, low = split(values)
    place = (all_cols[None, :] == jnp.arange(camp_blocks, dtype=jnp.float32)[:, None]).astype(jnp.bfloat16)
    dense = jnp.dot(place, jnp.concatenate([high, low], axis=1), preferred_element_type=jnp.float32)
    dense = dense[:, : ROUNDS * tile] + dense[:, ROUNDS * tile :]
    full = duals.reshape(camp_blocks, tile)
    allow = allowances.reshape(camp_blocks, tile)
    for step in range(ROUNDS):
        usage = dense[:, step * tile : (step + 1) * tile]
        full = jnp.maximum(full + STEP_SIZE * (usage - allow), 0.0)
    return (full.reshape(-1), usage.reshape(-1), unused_share)


def solution(mesh):
    grid = Mesh(mesh.devices.reshape(NZ, NX, NY, NC), ("z", "x", "y", "core"))
    mem = ("z", "x")
    return jax.shard_map(
        local,
        mesh=grid,
        in_specs=(
            P(mem, None, CAMP),
            P(mem, None, CAMP),
            P(mem, CAMP),
            P(mem, CAMP),
            P(mem, CAMP),
            P(CAMP),
            P(CAMP),
        ),
        out_specs=(P(CAMP), P(CAMP), P(mem)),
        check_vma=False,
    )
```

time: 917 us -> 231 us (0.25)
  the two profiles are of different devices: /device:TPU:8 before, /device:TPU:32 now
where the time goes in v1:
time: 231 us; the launch traced here: 230 us
  blocking collectives  80.1 us (35%)
  waiting for transfers between devices  64.5 us (28%)
  starting transfers between devices  26.4 us (11%)
  other arithmetic  23.2 us (10%)
  between operations  15.1 us (7%)
  local copies, waits for them, and re-layouts  13.7 us (6%)
  matrix products  6.99 us (3%)
    all_to_all x4, blocking collectives, spread(): return lax.all_to_all(sent, axis, 0, 0)  80.1 us
    all_to_all x4, waiting for transfers between devices, spread(): return lax.all_to_all(sent, axis, 0, 0)  33.1 us
    all_gather x1, waiting for transfers between devices, local(): history.append(lax.all_gather(column_z, 'x'))  21 us
    all_to_all x4, starting transfers between devices, spread(): return lax.all_to_all(sent, axis, 0, 0)  19.8 us
    all_to_all x2, waiting for transfers between devices, local(): lax.all_to_all(asked.reshape(NX, slots, tile), 'x', 0, 0)  8.99 us
    all_to_all x2, starting transfers between devices, local(): lax.all_to_all(asked.reshape(NX, slots, tile), 'x', 0, 0)  6.59 us
    reduce_sum x3, other arithmetic, local(): jnp.sum(cost_f * weighted, axis=1)  5.36 us
    reduce_sum x3, other arithmetic, local(): tile_sum = jnp.where(live_slot[:, None], jnp.sum(exponent, axis=2), 0.0)  5 us
  transfers between devices with their start and end apart: 8, of which 7 were waited for; matrix products, arithmetic and copies ran while one was open for 6% of the time, Pallas kernels for 0%

profile of v1, /device:TPU:32, one launch (start us, length us, event | category | flops | bytes accessed | tf_op | source)
XLA Modules:
  0.0 230.0 jit_solution(11145957683957428101)
XLA Ops:
  13.0 2.5 %fusion.13 = f32[40,128]{1,0:T(8,128)S(1)} fusion(bf16[40,128,128]{2,1,0:T(8,128)(2,1)} %param.12, bf16[40,128,128]{2,1,0:T(8,128)(2,1)} %param.11, f32[40,128]{1,0:T(8,128)S(1)} %broadcast_select_fusion.6), kind=kLoop, calls=%fused_computation.37 | loop fusion | flops 3927040 | bytes 2662400 | tf_op jit(solution)/shard_map/reduce_max | solution.py:44
  16.3 1.7 fusion.12
  18.9 4.5 %all-to-all-start = ((f32[8,16,128]{2,1,0:T(8,128)}), f32[8,16,128]{2,1,0:T(8,128)S(1)}, u32[]{:S(2)}, u32[]{:S(2)}) async-start(f32[8,16,128]{2,1,0:T(8,128)} %broadcast_in_dim.174), calls=%async_computation | async-start | bytes 131072 | tf_op jit(solution)/shard_map/all_to_all | solution.py:16
  23.5 5.5 %all-to-all-done = f32[8,16,128]{2,1,0:T(8,128)S(1)} async-done(((f32[8,16,128]{2,1,0:T(8,128)}), f32[8,16,128]{2,1,0:T(8,128)S(1)}, u32[]{:S(2)}, u32[]{:S(2)}) %all-to-all-start) | async-done | bytes 65568 | tf_op jit(solution)/shard_map/all_to_all | solution.py:16
  29.7 1.8 fusion.9
  31.7 36.8 %all_to_all.50 = f32[16,48,128]{2,1,0:T(8,128)S(1)} all-to-all(f32[16,48,128]{2,1,0:T(8,128)S(1)} %broadcast_in_dim.177), channel_id=1, replica_groups=mesh['z'=16,'x'=4,'y'=4,'core'=2] {'z'}, dimensions={0} | all-to-all | bytes 786432 | tf_op jit(solution)/shard_map/all_to_all | solution.py:16
  69.0 4.3 %all-to-all-start.2 = ((f32[4,1,128]{2,1,0:T(1,128)}), f32[4,1,128]{2,1,0:T(1,128)S(1)}, u32[]{:S(2)}, u32[]{:S(2)}) async-start(f32[4,1,128]{2,1,0:T(1,128)} %broadcast_in_dim.178), calls=%async_computation.2 | async-start | bytes 4096 | tf_op jit(solution)/shard_map/all_to_all | solution.py:16
  73.5 5.0 %all-to-all-done.2 = f32[4,1,128]{2,1,0:T(1,128)S(1)} async-done(((f32[4,1,128]{2,1,0:T(1,128)}), f32[4,1,128]{2,1,0:T(1,128)S(1)}, u32[]{:S(2)}, u32[]{:S(2)}) %all-to-all-start.2) | async-done | bytes 2080 | tf_op jit(solution)/shard_map/all_to_all | solution.py:16
  79.5 3.3 %all-to-all-start.3 = ((f32[4,40,128]{2,1,0:T(8,128)}), f32[4,40,128]{2,1,0:T(8,128)S(1)}, u32[]{:S(2)}, u32[]{:S(2)}) async-start(f32[4,40,128]{2,1,0:T(8,128)} %fusion.29), calls=%async_computation.3 | async-start | bytes 163840 | tf_op jit(solution)/shard_map/all_to_all | solution.py:74
  84.4 4.1 %all-to-all-done.3 = f32[4,40,128]{2,1,0:T(8,128)S(1)} async-done(((f32[4,40,128]{2,1,0:T(8,128)}), f32[4,40,128]{2,1,0:T(8,128)S(1)}, u32[]{:S(2)}, u32[]{:S(2)}) %all-to-all-start.3) | async-done | bytes 81952 | tf_op jit(solution)/shard_map/all_to_all | solution.py:74
  92.0 8.0 %all_to_all.51 = f32[8,16,128]{2,1,0:T(8,128)S(1)} all-to-all(f32[8,16,128]{2,1,0:T(8,128)S(1)} %broadcast_in_dim.180), channel_id=1, replica_groups=mesh['z'=16,'x'=4,'y'=4,'core'=2] {'y','core'}, dimensions={0} | all-to-all | bytes 131072 | tf_op jit(solution)/shard_map/all_to_all | solution.py:16
  100.7 1.8 fusion.10
  102.6 27.3 %all_to_all.52 = f32[16,40,128]{2,1,0:T(8,128)S(1)} all-to-all(f32[16,40,128]{2,1,0:T(8,128)S(1)} %broadcast_in_dim.181), channel_id=1, replica_groups=mesh['z'=16,'x'=4,'y'=4,'core'=2] {'z'}, dimensions={0} | all-to-all | bytes 655360 | tf_op jit(solution)/shard_map/all_to_all | solution.py:16
  131.0 3.3 %all-to-all-start.6 = ((f32[4,40,128]{2,1,0:T(8,128)}), f32[4,40,128]{2,1,0:T(8,128)S(1)}, u32[]{:S(2)}, u32[]{:S(2)}) async-start(f32[4,40,128]{2,1,0:T(8,128)} %fusion.27), calls=%async_computation.6 | async-start | bytes 163840 | tf_op jit(solution)/shard_map/all_to_all | solution.py:74
  135.0 4.9 %all-to-all-done.6 = f32[4,40,128]{2,1,0:T(8,128)S(1)} async-done(((f32[4,40,128]{2,1,0:T(8,128)}), f32[4,40,128]{2,1,0:T(8,128)S(1)}, u32[]{:S(2)}, u32[]{:S(2)}) %all-to-all-start.6) | async-done | bytes 81952 | tf_op jit(solution)/shard_map/all_to_all | solution.py:74
  143.5 8.0 %all_to_all.53 = f32[8,16,128]{2,1,0:T(8,128)S(1)} all-to-all(f32[8,16,128]{2,1,0:T(8,128)S(1)} %broadcast_in_dim.183), channel_id=1, replica_groups=mesh['z'=16,'x'=4,'y'=4,'core'=2] {'y','core'}, dimensions={0} | all-to-all | bytes 131072 | tf_op jit(solution)/shard_map/all_to_all | solution.py:16
  152.2 1.8 fusion.11
  154.8 7.3 %all-to-all-start.8 = ((f32[16,40,128]{2,1,0:T(8,128)}), f32[16,40,128]{2,1,0:T(8,128)S(1)}, u32[]{:S(2)}, u32[]{:S(2)}) async-start(f32[16,40,128]{2,1,0:T(8,128)} %broadcast_in_dim.184), calls=%async_computation.8 | async-start | bytes 655360 | tf_op jit(solution)/shard_map/all_to_all | solution.py:16
  162.8 18.8 %all-to-all-done.8 = f32[16,40,128]{2,1,0:T(8,128)S(1)} async-done(((f32[16,40,128]{2,1,0:T(8,128)}), f32[16,40,128]{2,1,0:T(8,128)S(1)}, u32[]{:S(2)}, u32[]{:S(2)}) %all-to-all-start.8) | async-done | bytes 327712 | tf_op jit(solution)/shard_map/all_to_all | solution.py:16
  182.8 3.7 %all-to-all-start.9 = ((f32[4,640,128]{2,1,0:T(8,128)}), f32[4,640,128]{2,1,0:T(8,128)S(1)}, u32[]{:S(2)}, u32[]{:S(2)}) async-start(f32[4,640,128]{2,1,0:T(8,128)} %broadcast_in_dim.186), calls=%async_computation.9 | async-start | bytes 2621440 | tf_op jit(solution)/shard_map/all_to_all | solution.py:16
  189.7 21.0 %all-gather.4.cloned.1.call-done = f32[4,640,128]{2,1,0:T(8,128)} async-done(((f32[1,640,128]{2,1,0:T(8,128)}), f32[4,640,128]{2,1,0:T(8,128)}) %all-gather.4.cloned.1.call-update) | async-done | bytes 1310736 | tf_op jit(solution)/shard_map/all_gather | solution.py:69
  210.7 3.8 %all-to-all-done.9 = f32[4,640,128]{2,1,0:T(8,128)S(1)} async-done(((f32[4,640,128]{2,1,0:T(8,128)}), f32[4,640,128]{2,1,0:T(8,128)S(1)}, u32[]{:S(2)}, u32[]{:S(2)}) %all-to-all-start.9) | async-done | bytes 1310752 | tf_op jit(solution)/shard_map/all_to_all | solution.py:16
  214.4 2.0 reduce-precision_convert_fusion
  216.4 4.4 %fusion = f32[1024,768]{1,0:T(8,128)S(1)} fusion(f32[2560]{0:T(1024)S(1)} %eq.62, bf16[2560,384]{1,0:T(8,128)(2,1)S(1)} %get-tuple-element.6, bf16[2560,384]{1,0:T(8,128)(2,1)S(1)} %get-tuple-element.5), kind=kOutput, calls=%fused_computation.9 | convolution fusion | flops 4037017600 | bytes 7088128 | tf_op jit(solution)/shard_map/dot_general | solution.py:85
  (100 shorter events, 29.5 us)
Async XLA Ops:
  7.2 9.2 %copy-start = (bf16[40,128,128]{2,1,0:T(8,128)(2,1)S(1)}, bf16[40,128,128]{2,1,0:T(8,128)(2,1)}, u32[]{:S(2)}) copy-start(bf16[40,128,128]{2,1,0:T(8,128)(2,1)} %param.12) | copy-start | bytes 3932164
  7.2 9.2 %copy-start.1 = (bf16[40,128,128]{2,1,0:T(8,128)(2,1)S(1)}, bf16[40,128,128]{2,1,0:T(8,128)(2,1)}, u32[]{:S(2)}) copy-start(bf16[40,128,128]{2,1,0:T(8,128)(2,1)} %param.11) | copy-start | bytes 3932164
  13.0 5.0 %copy-start.6 = (s32[40,1]{0,1:T(1,128)S(1)}, s32[40,1]{0,1:T(1,128)}, u32[]{:S(2)}) copy-start(s32[40,1]{0,1:T(1,128)} %param.13) | copy-start | bytes 484
  13.0 10.3 %copy-start.7 = (s32[40,1]{0,1:T(1,128)S(1)}, s32[40,1]{0,1:T(1,128)}, u32[]{:S(2)}) copy-start(s32[40,1]{0,1:T(1,128)} %param.14) | copy-start | bytes 484
  18.9 10.1 %all-to-all-start = ((f32[8,16,128]{2,1,0:T(8,128)}), f32[8,16,128]{2,1,0:T(8,128)S(1)}, u32[]{:S(2)}, u32[]{:S(2)}) async-start(f32[8,16,128]{2,1,0:T(8,128)} %broadcast_in_dim.174), calls=%async_computation | async-start | bytes 131072 | tf_op jit(solution)/shard_map/all_to_all | solution.py:16
  68.4 23.4 %copy-start.2 = (f32[16,48,128]{2,1,0:T(8,128)}, f32[16,48,128]{2,1,0:T(8,128)S(1)}, u32[]{:S(2)}) copy-start(f32[16,48,128]{2,1,0:T(8,128)S(1)} %all_to_all.50) | copy-start | bytes 1179652
  69.0 9.5 %all-to-all-start.2 = ((f32[4,1,128]{2,1,0:T(1,128)}), f32[4,1,128]{2,1,0:T(1,128)S(1)}, u32[]{:S(2)}, u32[]{:S(2)}) async-start(f32[4,1,128]{2,1,0:T(1,128)} %broadcast_in_dim.178), calls=%async_computation.2 | async-start | bytes 4096 | tf_op jit(solution)/shard_map/all_to_all | solution.py:16
  79.5 9.0 %all-to-all-start.3 = ((f32[4,40,128]{2,1,0:T(8,128)}), f32[4,40,128]{2,1,0:T(8,128)S(1)}, u32[]{:S(2)}, u32[]{:S(2)}) async-start(f32[4,40,128]{2,1,0:T(8,128)} %fusion.29), calls=%async_computation.3 | async-start | bytes 163840 | tf_op jit(solution)/shard_map/all_to_all | solution.py:74
  130.0 13.3 %copy-start.3 = (f32[16,40,128]{2,1,0:T(8,128)}, f32[16,40,128]{2,1,0:T(8,128)S(1)}, u32[]{:S(2)}) copy-start(f32[16,40,128]{2,1,0:T(8,128)S(1)} %all_to_all.52) | copy-start | bytes 983044
  131.0 9.0 %all-to-all-start.6 = ((f32[4,40,128]{2,1,0:T(8,128)}), f32[4,40,128]{2,1,0:T(8,128)S(1)}, u32[]{:S(2)}, u32[]{:S(2)}) async-start(f32[4,40,128]{2,1,0:T(8,128)} %fusion.27), calls=%async_computation.6 | async-start | bytes 163840 | tf_op jit(solution)/shard_map/all_to_all | solution.py:74
  134.3 52.9 %all-gather.6.cloned.1.call-start = ((), (), s32[]{:S(2)}) async-start(), calls=%async_computation.11 | async-start | bytes 1966080 | tf_op jit(solution)/shard_map/all_gather | solution.py:65
  154.8 26.8 %all-to-all-start.8 = ((f32[16,40,128]{2,1,0:T(8,128)}), f32[16,40,128]{2,1,0:T(8,128)S(1)}, u32[]{:S(2)}, u32[]{:S(2)}) async-start(f32[16,40,128]{2,1,0:T(8,128)} %broadcast_in_dim.184), calls=%async_computation.8 | async-start | bytes 655360 | tf_op jit(solution)/shard_map/all_to_all | solution.py:16
  162.1 48.6 %all-gather.4.cloned.1.call-start = ((), (), s32[]{:S(2)}) async-start(), calls=%async_computation.10 | async-start | bytes 1638400 | tf_op jit(solution)/shard_map/all_gather | solution.py:69
  182.8 31.6 %all-to-all-start.9 = ((f32[4,640,128]{2,1,0:T(8,128)}), f32[4,640,128]{2,1,0:T(8,128)S(1)}, u32[]{:S(2)}, u32[]{:S(2)}) async-start(f32[4,640,128]{2,1,0:T(8,128)} %broadcast_in_dim.186), calls=%async_computation.9 | async-start | bytes 2621440 | tf_op jit(solution)/shard_map/all_to_all | solution.py:16
  220.8 1.0 copy-start.4
  220.8 1.2 copy-start.5
Sparse Core Ops, SparseCore 0:
  137.8 28.7 all-gather.5
  168.7 41.9 all-gather.3

commit v2 on v1

v2 whole, which is shorter than its diff:
```python
import jax
import jax.numpy as jnp
from jax import lax
from jax.sharding import Mesh, PartitionSpec as P

MB = 8
ROUNDS = 3
SMOOTHING = 0.05
STEP_SIZE = 0.2
NF, NP, NX, NY, NC = 8, 2, 4, 4, 2
CAMP = ("y", "core")
NEAR = ("pair", "x")
NN = NP * NX


def spread(block, axis, count):
    sent = jnp.broadcast_to(block[None], (count,) + block.shape)
    return lax.all_to_all(sent, axis, 0, 0)


def split(values):
    high = lax.reduce_precision(values, 8, 7)
    return high.astype(jnp.bfloat16), (values - high).astype(jnp.bfloat16)


def densify(values, cols, camp_blocks):
    tile = values.shape[1]
    place = (cols[None, :] == jnp.arange(camp_blocks, dtype=jnp.float32)[:, None]).astype(jnp.bfloat16)
    dense = jnp.dot(place, jnp.concatenate(split(values), axis=1), preferred_element_type=jnp.float32)
    return dense[:, :tile] + dense[:, tile:]


def local(gains, costs, tile_rows, tile_cols, tile_count, duals, allowances):
    slots = gains.shape[0]
    tile = gains.shape[1]
    camp_blocks = duals.shape[0] // tile
    live_slot = jnp.arange(slots) < tile_count[0, 0]
    member_block = tile_rows[:, 0]
    camp_block = tile_cols[:, 0]
    onehot = (member_block[None, :] == jnp.arange(MB)[:, None]) & live_slot[None, :]
    onehot_f = onehot.astype(jnp.float32)
    gain_f = gains.astype(jnp.float32)
    cost_f = costs.astype(jnp.float32)
    price = jnp.take(duals.reshape(camp_blocks, tile), camp_block, axis=0)
    allowance = jnp.take(allowances.reshape(camp_blocks, tile), camp_block, axis=0)
    own_cols = camp_block.astype(jnp.float32)
    ids_rows = jnp.pad(own_cols[None], ((0, 7), (0, tile - slots)))
    my_far = lax.axis_index("far")
    my_near = lax.axis_index("pair") * NX + lax.axis_index("x")

    def stats(price):
        scores = (gain_f - cost_f * price[:, None, :]) / SMOOTHING
        tile_top = jnp.max(scores, axis=2)
        local_top = jnp.maximum(
            jnp.max(jnp.where(onehot[:, :, None], tile_top[None], -jnp.inf), axis=1), 0.0
        )
        exponent = jnp.exp(scores - jnp.take(local_top, member_block, axis=0)[:, :, None])
        tile_sum = jnp.where(live_slot[:, None], jnp.sum(exponent, axis=2), 0.0)
        local_sum = jnp.dot(onehot_f, tile_sum, precision=lax.Precision.HIGHEST)
        both = spread(jnp.concatenate([local_top, local_sum]), CAMP, NY * NC)
        tops, sums = both[:, :MB], both[:, MB:]
        row_top = jnp.max(tops, axis=0)
        spare = jnp.exp(-row_top)
        denom = spare + jnp.sum(sums * jnp.exp(tops - row_top), axis=0)
        weight = jnp.exp(local_top - row_top) / denom
        weighted = exponent * jnp.take(weight, member_block, axis=0)[:, :, None]
        column_use = jnp.where(live_slot[:, None], jnp.sum(cost_f * weighted, axis=1), 0.0)
        return column_use, (spare / denom).reshape(-1)

    column_use, _ = stats(price)
    got = spread(jnp.concatenate([column_use, ids_rows]), "far", NF)
    column_far = got[:, :slots].reshape(NF * slots, tile)
    got = spread(jnp.concatenate([column_far, got[:, slots]]), NEAR, NN)
    cols_all = got[:, NF * slots :, :slots]
    cols_flat = cols_all.reshape(-1)
    rows_1 = got[:, : NF * slots].reshape(-1, tile)
    wanted = (own_cols[:, None] == cols_flat[None, :]).astype(jnp.float32)
    use = jnp.dot(wanted, rows_1, precision=lax.Precision.HIGHEST)
    price = jnp.maximum(price + STEP_SIZE * (use - allowance), 0.0)

    column_use, _ = stats(price)
    rows_2 = spread(column_use, NEAR, NN).reshape(NN * slots, tile)
    cols_near = lax.dynamic_index_in_dim(cols_all, my_far, 1, False)
    cols_far = lax.dynamic_index_in_dim(cols_all, my_near, 0, False)
    pulled = (cols_far.reshape(-1)[:, None] == cols_near.reshape(-1)[None, :]).astype(jnp.float32)
    asked = jnp.dot(pulled, rows_2, precision=lax.Precision.HIGHEST)
    use = jnp.sum(lax.all_to_all(asked.reshape(NF, slots, tile), "far", 0, 0), axis=0)
    price = jnp.maximum(price + STEP_SIZE * (use - allowance), 0.0)
    rows_2 = lax.all_gather(rows_2, "far").reshape(-1, tile)

    column_use, unused_share = stats(price)
    column_far = spread(column_use, "far", NF).reshape(NF * slots, tile)
    rows_3 = spread(column_far, NEAR, NN).reshape(-1, tile)

    cols_swapped = jnp.transpose(cols_all, (1, 0, 2)).reshape(-1)
    full = duals.reshape(camp_blocks, tile)
    allow = allowances.reshape(camp_blocks, tile)
    for rows, cols in ((rows_1, cols_flat), (rows_2, cols_swapped), (rows_3, cols_flat)):
        usage = densify(rows, cols, camp_blocks)
        full = jnp.maximum(full + STEP_SIZE * (usage - allow), 0.0)
    return (full.reshape(-1), usage.reshape(-1), unused_share)


def solution(mesh):
    grid = Mesh(mesh.devices.reshape(NF, NP, NX, NY, NC), ("far", "pair", "x", "y", "core"))
    mem = ("far", "pair", "x")
    return jax.shard_map(
        local,
        mesh=grid,
        in_specs=(
            P(mem, None, CAMP),
            P(mem, None, CAMP),
            P(mem, CAMP),
            P(mem, CAMP),
            P(mem, CAMP),
            P(CAMP),
            P(CAMP),
        ),
        out_specs=(P(CAMP), P(CAMP), P(mem)),
        check_vma=False,
    )
```

time: 231 us -> 243 us (1.052)
  the two profiles are of different devices: /device:TPU:32 before, /device:TPU:38 now
where the time goes in v2:
time: 243 us; the launch traced here: 242 us
  blocking collectives  89.4 us (37%)
  waiting for transfers between devices  70.9 us (29%)
  other arithmetic  22.5 us (9%)
  starting transfers between devices  22.4 us (9%)
  between operations  15.2 us (6%)
  local copies, waits for them, and re-layouts  14.2 us (6%)
  matrix products  7.5 us (3%)
    all_to_all x4, blocking collectives, spread(): return lax.all_to_all(sent, axis, 0, 0)  67.8 us
    all_gather x1, waiting for transfers between devices, local(): rows_2 = lax.all_gather(rows_2, 'far').reshape(-1, tile)  48.2 us
    all_to_all x4, starting transfers between devices, spread(): return lax.all_to_all(sent, axis, 0, 0)  22.4 us
    all_to_all x4, waiting for transfers between devices, spread(): return lax.all_to_all(sent, axis, 0, 0)  22 us
    all_to_all x1, blocking collectives, local(): lax.all_to_all(asked.reshape(NF, slots, tile), 'far', 0, 0)  21.6 us
    dot_general x3, matrix products, densify(): jnp.dot(place, jnp.concatenate(split(values), axis=1), preferred_element_...  5.91 us
    reduce_sum x3, other arithmetic, stats(): jnp.sum(cost_f * weighted, axis=1)  5.36 us
    reduce_sum x3, other arithmetic, stats(): tile_sum = jnp.where(live_slot[:, None], jnp.sum(exponent, axis=2), 0.0)  5.03 us
  transfers between devices with their start and end apart: 5, of which 4 were waited for; matrix products, arithmetic and copies ran while one was open for 3% of the time, Pallas kernels for 0%

profile of v2, /device:TPU:38, one launch (start us, length us, event | category | flops | bytes accessed | tf_op | source)
XLA Modules:
  0.0 242.1 jit_solution(13934489255416880292)
XLA Ops:
  9.9 1.6 gather_fusion
  11.6 2.6 %fusion.13 = f32[40,128]{1,0:T(8,128)S(1)} fusion(bf16[40,128,128]{2,1,0:T(8,128)(2,1)} %param.12, bf16[40,128,128]{2,1,0:T(8,128)(2,1)} %param.11, f32[40,128]{1,0:T(8,128)S(1)} %broadcast_select_fusion.6), kind=kLoop, calls=%fused_computation.35 | loop fusion | flops 3927040 | bytes 2662400 | tf_op jit(solution)/shard_map/reduce_max | solution.py:53
  15.1 1.7 fusion.12
  17.6 4.5 %all-to-all-start = ((f32[8,16,128]{2,1,0:T(8,128)}), f32[8,16,128]{2,1,0:T(8,128)S(1)}, u32[]{:S(2)}, u32[]{:S(2)}) async-start(f32[8,16,128]{2,1,0:T(8,128)} %broadcast_in_dim.173), calls=%async_computation | async-start | bytes 131072 | tf_op jit(solution)/shard_map/all_to_all | solution.py:18
  22.1 5.6 %all-to-all-done = f32[8,16,128]{2,1,0:T(8,128)S(1)} async-done(((f32[8,16,128]{2,1,0:T(8,128)}), f32[8,16,128]{2,1,0:T(8,128)S(1)}, u32[]{:S(2)}, u32[]{:S(2)}) %all-to-all-start) | async-done | bytes 65568 | tf_op jit(solution)/shard_map/all_to_all | solution.py:18
  28.4 1.8 fusion.9
  30.3 32.0 %all_to_all.45 = f32[8,48,128]{2,1,0:T(8,128)S(1)} all-to-all(f32[8,48,128]{2,1,0:T(8,128)S(1)} %broadcast_in_dim.174), channel_id=1, replica_groups=mesh['far'=8,'pair'=2,'x'=4,'y'=4,'core'=2] {'far'}, dimensions={0} | all-to-all | bytes 393216 | tf_op jit(solution)/shard_map/all_to_all | solution.py:18
  63.6 5.9 %all-to-all-start.2 = ((f32[8,328,128]{2,1,0:T(8,128)}), f32[8,328,128]{2,1,0:T(8,128)}, u32[]{:S(2)}, u32[]{:S(2)}) async-start(f32[8,328,128]{2,1,0:T(8,128)} %broadcast_in_dim.175), calls=%async_computation.2 | async-start | bytes 2686976 | tf_op jit(solution)/shard_map/all_to_all | solution.py:18
  70.0 12.4 %all-to-all-done.2 = f32[8,328,128]{2,1,0:T(8,128)} async-done(((f32[8,328,128]{2,1,0:T(8,128)}), f32[8,328,128]{2,1,0:T(8,128)}, u32[]{:S(2)}, u32[]{:S(2)}) %all-to-all-start.2) | async-done | bytes 1343520 | tf_op jit(solution)/shard_map/all_to_all | solution.py:18
  88.6 1.7 fusion.14
  90.5 8.0 %all_to_all.46 = f32[8,16,128]{2,1,0:T(8,128)S(1)} all-to-all(f32[8,16,128]{2,1,0:T(8,128)S(1)} %broadcast_in_dim.177), channel_id=1, replica_groups=mesh['far'=8,'pair'=2,'x'=4,'y'=4,'core'=2] {'y','core'}, dimensions={0} | all-to-all | bytes 131072 | tf_op jit(solution)/shard_map/all_to_all | solution.py:18
  99.2 1.8 fusion.10
  101.7 5.4 %all-to-all-start.4 = ((f32[8,40,128]{2,1,0:T(8,128)}), f32[8,40,128]{2,1,0:T(8,128)S(1)}, u32[]{:S(2)}, u32[]{:S(2)}) async-start(f32[8,40,128]{2,1,0:T(8,128)} %broadcast_in_dim.178), calls=%async_computation.4 | async-start | bytes 327680 | tf_op jit(solution)/shard_map/all_to_all | solution.py:18
  107.2 4.0 %all-to-all-done.4 = f32[8,40,128]{2,1,0:T(8,128)S(1)} async-done(((f32[8,40,128]{2,1,0:T(8,128)}), f32[8,40,128]{2,1,0:T(8,128)S(1)}, u32[]{:S(2)}, u32[]{:S(2)}) %all-to-all-start.4) | async-done | bytes 163872 | tf_op jit(solution)/shard_map/all_to_all | solution.py:18
  111.6 21.6 %all_to_all.47 = f32[8,40,128]{2,1,0:T(8,128)S(1)} all-to-all(f32[8,40,128]{2,1,0:T(8,128)S(1)} %fusion.44), channel_id=1, replica_groups=mesh['far'=8,'pair'=2,'x'=4,'y'=4,'core'=2] {'far'}, dimensions={0} | all-to-all | bytes 327680 | tf_op jit(solution)/shard_map/all_to_all | solution.py:87
  135.7 1.7 fusion.16
  137.6 8.0 %all_to_all.48 = f32[8,16,128]{2,1,0:T(8,128)S(1)} all-to-all(f32[8,16,128]{2,1,0:T(8,128)S(1)} %broadcast_in_dim.180), channel_id=1, replica_groups=mesh['far'=8,'pair'=2,'x'=4,'y'=4,'core'=2] {'y','core'}, dimensions={0} | all-to-all | bytes 131072 | tf_op jit(solution)/shard_map/all_to_all | solution.py:18
  146.4 1.8 fusion.11
  148.3 19.8 %all_to_all.49 = f32[8,40,128]{2,1,0:T(8,128)S(1)} all-to-all(f32[8,40,128]{2,1,0:T(8,128)S(1)} %broadcast_in_dim.181), channel_id=1, replica_groups=mesh['far'=8,'pair'=2,'x'=4,'y'=4,'core'=2] {'far'}, dimensions={0} | all-to-all | bytes 327680 | tf_op jit(solution)/shard_map/all_to_all | solution.py:18
  169.3 6.6 %all-to-all-start.8 = ((f32[8,320,128]{2,1,0:T(8,128)}), f32[8,320,128]{2,1,0:T(8,128)S(1)}, u32[]{:S(2)}, u32[]{:S(2)}) async-start(f32[8,320,128]{2,1,0:T(8,128)} %broadcast_in_dim.183), calls=%async_computation.8 | async-start | bytes 2621440 | tf_op jit(solution)/shard_map/all_to_all | solution.py:18
  177.3 1.6 fusion.1
  179.6 48.2 %all-gather.2.cloned.1.call-done = f32[8,320,128]{2,1,0:T(8,128)} async-done(((f32[1,320,128]{2,1,0:T(8,128)}), f32[8,320,128]{2,1,0:T(8,128)}) %all-gather.2.cloned.1.call-update) | async-done | bytes 1310736 | tf_op jit(solution)/shard_map/all_gather | solution.py:89
  229.3 2.6 %fusion.2 = f32[1024,256]{1,0:T(8,128)} fusion(f32[2560]{0:T(1024)S(1)} %eq.101, bf16[2560,128]{1,0:T(8,128)(2,1)S(1)} %get-tuple-element.12, bf16[2560,128]{1,0:T(8,128)(2,1)S(1)} %get-tuple-element.11), kind=kOutput, calls=%fused_computation.12 | convolution fusion | flops 1347420160 | bytes 2369536 | tf_op jit(solution)/shard_map/dot_general | solution.py:29
  232.2 1.6 fusion
  (115 shorter events, 24.4 us)
Async XLA Ops:
  8.5 76.8 %copy-start.12 = (pred[40]{0:T(512)(128)(4,1)}, pred[40]{0:T(512)(128)(4,1)S(1)}, u32[]{:S(2)}) copy-start(pred[40]{0:T(512)(128)(4,1)S(1)} %get-tuple-element.20) | copy-start | bytes 124
  9.2 91.8 %copy-start.13 = (pred[40]{0:T(512)(128)(4,1)}, pred[40]{0:T(512)(128)(4,1)S(1)}, u32[]{:S(2)}) copy-start(pred[40]{0:T(512)(128)(4,1)S(1)} %iota_compare_fusion.7) | copy-start | bytes 124
  11.6 3.4 %copy-start = (bf16[40,128,128]{2,1,0:T(8,128)(2,1)S(1)}, bf16[40,128,128]{2,1,0:T(8,128)(2,1)}, u32[]{:S(2)}) copy-start(bf16[40,128,128]{2,1,0:T(8,128)(2,1)} %param.12) | copy-start | bytes 3932164
  11.6 3.4 %copy-start.1 = (bf16[40,128,128]{2,1,0:T(8,128)(2,1)S(1)}, bf16[40,128,128]{2,1,0:T(8,128)(2,1)}, u32[]{:S(2)}) copy-start(bf16[40,128,128]{2,1,0:T(8,128)(2,1)} %param.11) | copy-start | bytes 3932164
  14.4 84.2 %copy-start.11 = (s32[1024]{0:T(1024)}, s32[1024]{0:T(1024)S(1)}, u32[]{:S(2)}) copy-start(s32[1024]{0:T(1024)S(1)} %pad_clamp_fusion) | copy-start | bytes 12292
  15.0 1.7 copy-start.15
  15.0 7.0 %copy-start.17 = (s32[40,1]{0,1:T(1,128)S(1)}, s32[40,1]{0,1:T(1,128)}, u32[]{:S(2)}) copy-start(s32[40,1]{0,1:T(1,128)} %param.14) | copy-start | bytes 484
  17.6 10.1 %all-to-all-start = ((f32[8,16,128]{2,1,0:T(8,128)}), f32[8,16,128]{2,1,0:T(8,128)S(1)}, u32[]{:S(2)}, u32[]{:S(2)}) async-start(f32[8,16,128]{2,1,0:T(8,128)} %broadcast_in_dim.173), calls=%async_computation | async-start | bytes 131072 | tf_op jit(solution)/shard_map/all_to_all | solution.py:18
  63.6 5.9 %copy-start.7 = (f32[131072]{0:T(1024)S(1)}, f32[131072]{0:T(1024)}, u32[]{:S(2)}) copy-start(f32[131072]{0:T(1024)} %param.17) | copy-start | bytes 1572868
  63.6 18.9 %all-to-all-start.2 = ((f32[8,328,128]{2,1,0:T(8,128)}), f32[8,328,128]{2,1,0:T(8,128)}, u32[]{:S(2)}, u32[]{:S(2)}) async-start(f32[8,328,128]{2,1,0:T(8,128)} %broadcast_in_dim.175), calls=%async_computation.2 | async-start | bytes 2686976 | tf_op jit(solution)/shard_map/all_to_all | solution.py:18
  83.9 3.1 %copy-start.9 = (f32[2560]{0:T(1024)}, f32[2560]{0:T(1024)S(1)}, u32[]{:S(2)}) copy-start(f32[2560]{0:T(1024)S(1)} %eq.97) | copy-start | bytes 30724
  85.3 1.1 copy-start.2
  101.7 9.5 %all-to-all-start.4 = ((f32[8,40,128]{2,1,0:T(8,128)}), f32[8,40,128]{2,1,0:T(8,128)S(1)}, u32[]{:S(2)}, u32[]{:S(2)}) async-start(f32[8,40,128]{2,1,0:T(8,128)} %broadcast_in_dim.178), calls=%async_computation.4 | async-start | bytes 327680 | tf_op jit(solution)/shard_map/all_to_all | solution.py:18
  111.2 23.5 %copy-start.4 = (f32[8,40,128]{2,1,0:T(8,128)}, f32[8,40,128]{2,1,0:T(8,128)S(1)}, u32[]{:S(2)}) copy-start(f32[8,40,128]{2,1,0:T(8,128)S(1)} %all-to-all-done.4) | copy-start | bytes 491524
  135.7 1.7 copy-start.14
  135.7 1.7 copy-start.16
  169.3 7.3 %copy-start.8 = (f32[8,8,40]{2,0,1:T(8,128)S(1)}, f32[8,8,40]{2,0,1:T(8,128)}, u32[]{:S(2)}) copy-start(f32[8,8,40]{2,0,1:T(8,128)} %get-tuple-element.6) | copy-start | bytes 30724
  169.3 7.5 %copy-start.3 = (f32[8,320,128]{2,1,0:T(8,128)S(1)}, f32[8,320,128]{2,1,0:T(8,128)}, u32[]{:S(2)}) copy-start(f32[8,320,128]{2,1,0:T(8,128)} %copy-done.2) | copy-start | bytes 3932164
  169.3 62.7 %all-to-all-start.8 = ((f32[8,320,128]{2,1,0:T(8,128)}), f32[8,320,128]{2,1,0:T(8,128)S(1)}, u32[]{:S(2)}, u32[]{:S(2)}) async-start(f32[8,320,128]{2,1,0:T(8,128)} %broadcast_in_dim.183), calls=%async_computation.8 | async-start | bytes 2621440 | tf_op jit(solution)/shard_map/all_to_all | solution.py:18
  175.9 51.9 %all-gather.2.cloned.1.call-start = ((), (), s32[]{:S(2)}) async-start(), calls=%async_computation.9 | async-start | bytes 1474560 | tf_op jit(solution)/shard_map/all_gather | solution.py:89
  176.6 0.7 copy-start.10
  232.2 1.7 copy-start.5
  232.2 1.7 copy-start.6
Sparse Core Ops, SparseCore 0:
  179.4 48.4 all-gather.1

commit v3 on v0

v3 whole, which is shorter than its diff:
```python
import functools
import math

import jax
import jax.numpy as jnp
from jax import lax
from jax.experimental import pallas as pl
from jax.experimental.pallas import tpu as pltpu
from jax.sharding import Mesh, PartitionSpec as P

MB = 8
ROUNDS = 3
SMOOTHING = 0.05
STEP_SIZE = 0.2
SCALE = math.log2(math.e) / SMOOTHING
NF, NP, NX, NY, NC = 8, 2, 4, 4, 2
CAMP = ("y", "core")
NEAR = ("pair", "x")
NN = NP * NX
N_CAMP = NY * NC
TILE = 128
CHUNK = 256
F32 = jnp.float32
VMEM = pl.BlockSpec(memory_space=pltpu.VMEM)
SMEM = pl.BlockSpec(memory_space=pltpu.SMEM)


def call(body, out_shape, operands, specs, scratch, flops=0, moved=0):
    return pl.pallas_call(
        body,
        out_shape=out_shape,
        in_specs=specs,
        out_specs=jax.tree.map(lambda _: VMEM, out_shape),
        scratch_shapes=scratch,
        compiler_params=pltpu.CompilerParams(vmem_limit_bytes=32 * 1024 * 1024),
        cost_estimate=pl.CostEstimate(flops=flops, bytes_accessed=moved, transcendentals=0),
    )(*operands)


def dense_step(got_ref, ids_ref, price_ref, allow_ref, new_ref, usage_ref, parts):
    per = ids_ref.shape[1] // NN
    for near in range(NN):
        values = got_ref[near, :per, :]
        high = values.astype(jnp.bfloat16)
        parts[near * per : (near + 1) * per, :TILE] = high
        parts[near * per : (near + 1) * per, TILE:] = (values - high.astype(F32)).astype(jnp.bfloat16)
    ids = ids_ref[...]
    blocks = price_ref.shape[0]
    for at in range(0, blocks, CHUNK):
        index = lax.broadcasted_iota(jnp.int32, (CHUNK, 1), 0) + at
        place = jnp.where(ids == index, 1.0, 0.0).astype(jnp.bfloat16)
        both = jnp.dot(place, parts[...], preferred_element_type=F32)
        usage = both[:, :TILE] + both[:, TILE:]
        rows = slice(at, at + CHUNK)
        if usage_ref is not None:
            usage_ref[rows, :] = usage
        new_ref[rows, :] = jnp.maximum(price_ref[rows, :] + STEP_SIZE * (usage - allow_ref[rows, :]), 0.0)


def score_step(rows, cols, count, gain_ref, cost_ref, price_ref, sent_ref, ex_ref, top, total):
    top[...] = jnp.zeros_like(top)
    total[...] = jnp.zeros_like(total)
    live = count[0, 0]

    @pl.loop(0, live)
    def _(s):
        block = rows[s, 0]
        price = price_ref[pl.ds(cols[s, 0], 1), :] * SCALE
        score = gain_ref[s].astype(F32) * SCALE - cost_ref[s].astype(F32) * price
        ex_ref[s] = score
        top[block] = jnp.maximum(top[block], score)

    lane = lax.broadcasted_iota(jnp.int32, (TILE, TILE), 1)
    stats = jnp.zeros((TILE, TILE), F32)
    for b in range(MB):
        best = jnp.broadcast_to(jnp.max(top[b], axis=1, keepdims=True), (TILE, TILE))
        top[b] = best
        stats = jnp.where(lane == b, best, stats)

    @pl.loop(0, live)
    def _(s):
        block = rows[s, 0]
        e = jnp.exp2(ex_ref[s] - top[block])
        total[block] = total[block] + e
        ex_ref[s] = cost_ref[s].astype(F32) * e

    for b in range(MB):
        stats = jnp.where(lane == MB + b, jnp.sum(total[b], axis=1, keepdims=True), stats)
    packed = jnp.transpose(stats)[: 2 * MB, :]
    for k in range(N_CAMP):
        sent_ref[k] = packed


def first_body(rows, cols, count, gain_ref, cost_ref, price_ref, sent_ref, ex_ref, top, total):
    score_step(rows, cols, count, gain_ref, cost_ref, price_ref, sent_ref, ex_ref, top, total)


def next_body(rows, cols, count, gain_ref, cost_ref, got_ref, ids_ref, price_ref, allow_ref,
              new_ref, sent_ref, ex_ref, top, total, parts):
    dense_step(got_ref, ids_ref, price_ref, allow_ref, new_ref, None, parts)
    score_step(rows, cols, count, gain_ref, cost_ref, new_ref, sent_ref, ex_ref, top, total)


def last_body(got_ref, ids_ref, price_ref, allow_ref, new_ref, usage_ref, parts):
    dense_step(got_ref, ids_ref, price_ref, allow_ref, new_ref, usage_ref, parts)


def use_body(rows, cols, count, got_ref, sent_ref, ex_ref, use_ref, unused_ref, weights, use, *, with_ids):
    slots = ex_ref.shape[0]
    tops = got_ref[:, :MB, :]
    row_top = jnp.max(tops, axis=0)
    spare = jnp.exp2(-row_top)
    denom = spare + jnp.sum(got_ref[:, MB:, :] * jnp.exp2(tops - row_top), axis=0)
    unused_ref[...] = spare / denom
    weight = jnp.exp2(sent_ref[0, :MB, :] - row_top) / denom
    turned = jnp.transpose(jnp.concatenate([weight] * (TILE // MB), axis=0))
    for b in range(MB):
        weights[b] = jnp.broadcast_to(turned[:, b : b + 1], (TILE, TILE))
    use[...] = jnp.zeros_like(use)

    @pl.loop(0, count[0, 0])
    def _(s):
        use[pl.ds(s, 1), :] = jnp.sum(ex_ref[s] * weights[rows[s, 0]], axis=0, keepdims=True)

    if with_ids:
        lane = lax.broadcasted_iota(jnp.int32, (MB, TILE), 1)
        ids = jnp.zeros((MB, TILE), F32)
        for s in range(slots):
            ids = jnp.where(lane == s, cols[s, 0].astype(F32), ids)
        use[slots:, :] = ids
    for k in range(NF):
        use_ref[k] = use[...]


def local(gains, costs, tile_rows, tile_cols, tile_count, duals, allowances):
    slots = gains.shape[0]
    blocks = duals.shape[0] // TILE
    price = duals.reshape(blocks, TILE)
    allow = allowances.reshape(blocks, TILE)
    where = (tile_rows, tile_cols, tile_count)
    tiles = (gains, costs)
    shape = lambda *s: jax.ShapeDtypeStruct(s, F32)
    sent_shape, ex_shape = shape(N_CAMP, 2 * MB, TILE), shape(slots, TILE, TILE)
    by_block = pltpu.VMEM((MB, TILE, TILE), F32)
    parts = pltpu.VMEM((NF * NN * slots, 2 * TILE), jnp.bfloat16)
    got = ids = None
    for step in range(ROUNDS):
        if step == 0:
            sent, ex = call(first_body, (sent_shape, ex_shape), where + tiles + (price,),
                            [SMEM] * 3 + [VMEM] * 3, [by_block, by_block])
        else:
            price, sent, ex = call(next_body, (shape(blocks, TILE), sent_shape, ex_shape),
                                   where + tiles + (got, ids, price, allow),
                                   [SMEM] * 3 + [VMEM] * 6, [by_block, by_block, parts])
        stats = lax.all_to_all(sent, CAMP, 0, 0)
        extra = MB if step == 0 else 0
        use, unused = call(functools.partial(use_body, with_ids=step == 0),
                           (shape(NF, slots + extra, TILE), shape(MB, TILE)), where + (stats, sent, ex),
                           [SMEM] * 3 + [VMEM] * 3,
                           [by_block, pltpu.VMEM((slots + extra, TILE), F32)])
        far = lax.all_to_all(use, "far", 0, 0)
        rows = far[:, :slots].reshape(NF * slots, TILE)
        if step == 0:
            rows = jnp.concatenate([rows, far[:, slots]])
        got = lax.all_to_all(jnp.broadcast_to(rows[None], (NN,) + rows.shape), NEAR, 0, 0)
        if step == 0:
            ids = got[:, NF * slots :, :slots].reshape(1, -1).astype(jnp.int32)
    price, usage = call(last_body, (shape(blocks, TILE), shape(blocks, TILE)), (got, ids, price, allow),
                        [VMEM] * 4, [parts])
    return (price.reshape(-1), usage.reshape(-1), unused.reshape(-1))


def solution(mesh):
    grid = Mesh(mesh.devices.reshape(NF, NP, NX, NY, NC), ("far", "pair", "x", "y", "core"))
    mem = ("far", "pair", "x")
    return jax.shard_map(
        local,
        mesh=grid,
        in_specs=(
            P(mem, None, CAMP),
            P(mem, None, CAMP),
            P(mem, CAMP),
            P(mem, CAMP),
            P(mem, CAMP),
            P(CAMP),
            P(CAMP),
        ),
        out_specs=(P(CAMP), P(CAMP), P(mem)),
        check_vma=False,
    )
```

time: 917 us -> 194 us (0.21)
  waiting for transfers between devices: 788 us -> 0 us
  blocking collectives: 72.5 us -> 162 us
  other arithmetic: 31.4 us -> 0.02 us
  Pallas kernels: 0 us -> 21.2 us
  between operations: 14.6 us -> 1.38 us
    psum x3 -> x0, waiting for transfers between devices: 788 us -> none  [local(): usage = lax.psum(local_use, 'mem')]
    all_to_all x0 -> x9, blocking collectives: none -> 162 us  [the longest x3 70.2 us: local(): far = lax.all_to_all(use, 'far', 0, 0)]
    psum x3 -> x0, blocking collectives: 37.7 us -> none  [local(): row_sum = lax.psum(local_sum, 'camp')]
    pmax x3 -> x0, blocking collectives: 34.8 us -> none  [local(): row_top = lax.pmax(local_top, 'camp')]
    pallas_call x0 -> x7, Pallas kernels: none -> 21.2 us  [call(): pl.pallas_call(body, out_shape=out_shape, in_specs=specs, out_specs=jax.t...]
    reduce_sum x6 -> x0, other arithmetic: 10.4 us -> none  [the longest x3 5.39 us: local(): jnp.sum(cost_f * alloc, axis=1)]
  transfers between devices with their start and end apart: 3 -> 0, of which waited for: 3 -> 0; matrix products, arithmetic and copies ran while one was open for 0% -> 0% of each run, Pallas kernels for 0% -> 0%
where the time goes in v3:
time: 194 us; the launch traced here: 193 us
  blocking collectives  162 us (84%)
  Pallas kernels  21.2 us (11%)
  local copies, waits for them, and re-layouts  8.98 us (5%)
    all_to_all x3, blocking collectives, local(): far = lax.all_to_all(use, 'far', 0, 0)  70.2 us
    all_to_all x3, blocking collectives, local(): lax.all_to_all(jnp.broadcast_to(rows[None], (NN,) + rows.shape), NEAR, 0, 0)  59.4 us
    all_to_all x3, blocking collectives, local(): stats = lax.all_to_all(sent, CAMP, 0, 0)  31.9 us
    pallas_call x7, Pallas kernels, call(): pl.pallas_call(body, out_shape=out_shape, in_specs=specs, out_specs=jax.t...  21.2 us
    unnamed x20, local copies, waits for them, and re-layouts  8.62 us

profile of v3, /device:TPU:8, one launch (start us, length us, event | category | flops | bytes accessed | tf_op | source)
XLA Modules:
  0.0 193.2 jit_solution(15818984832638850905)
XLA Ops:
  1.3 0.7 copy.20.rows
  2.0 0.7 copy.21.cols
  2.8 1.3 copy-done
  4.1 1.3 copy-done.2
  5.4 1.0 copy-done.7
  6.4 2.5 %shard_map.94 = (f32[8,16,128]{2,1,0:T(8,128)S(1)}, f32[40,128,128]{2,1,0:T(8,128)S(1)}) custom-call(s32[40,1]{1,0:T(8,128)S(1)} %copy.20.rows, s32[40,1]{1,0:T(8,128)S(1)} %copy.21.cols, s32[1,1]{1,0:T(1,128)S(6)} %copy.22.count, bf16[40,128,128]{2,1,0:T(8,128)(2,1)S(1)} %copy-done, bf16[40,128,128]{2,1,0:T(8,128)(2,1)S(1)} %copy-done.2, ...), custom_call_target="tpu_custom_call" | custom-call | tf_op jit(solution)/shard_map/pallas_call | solution.py:29
  8.9 11.6 %all_to_all.45.got_ref = f32[8,16,128]{2,1,0:T(8,128)S(1)} all-to-all(f32[8,16,128]{2,1,0:T(8,128)S(1)} %get-tuple-element.17.sent_ref), channel_id=1, replica_groups=mesh['far'=8,'pair'=2,'x'=4,'y'=4,'core'=2] {'y','core'}, dimensions={0} | all-to-all | bytes 131072 | tf_op jit(solution)/shard_map/all_to_all | solution.py:155
  20.5 2.7 %shard_map.95 = (f32[8,48,128]{2,1,0:T(8,128)S(1)}, f32[8,128]{1,0:T(8,128)}) custom-call(s32[40,1]{1,0:T(8,128)S(1)} %copy.20.rows, s32[40,1]{1,0:T(8,128)S(1)} %copy.21.cols, s32[1,1]{1,0:T(1,128)S(6)} %copy.22.count, f32[8,16,128]{2,1,0:T(8,128)S(1)} %all_to_all.45.got_ref, f32[8,16,128]{2,1,0:T(8,128)S(1)} %get-tuple-element.17.sent_ref, ...), custom_call_target="tpu_custom_call" | custom-call | tf_op jit(solution)/shard_map/pallas_call | solution.py:29
  23.3 29.7 %all_to_all.46 = f32[8,48,128]{2,1,0:T(8,128)S(1)} all-to-all(f32[8,48,128]{2,1,0:T(8,128)S(1)} %get-tuple-element.19), channel_id=1, replica_groups=mesh['far'=8,'pair'=2,'x'=4,'y'=4,'core'=2] {'far'}, dimensions={0} | all-to-all | bytes 393216 | tf_op jit(solution)/shard_map/all_to_all | solution.py:161
  53.2 22.7 %all_to_all.47.got_ref = f32[8,328,128]{2,1,0:T(8,128)S(1)} all-to-all(f32[8,328,128]{2,1,0:T(8,128)S(1)} %broadcast_in_dim.20), channel_id=1, replica_groups=mesh['far'=8,'pair'=2,'x'=4,'y'=4,'core'=2] {'pair','x'}, dimensions={0} | all-to-all | bytes 2686976 | tf_op jit(solution)/shard_map/all_to_all | solution.py:165
  75.9 1.1 copy-done.4
  77.1 1.3 copy-done.5
  78.5 1.0 copy-done.8
  79.5 4.0 %shard_map.96 = (f32[1024,128]{1,0:T(8,128)S(1)}, f32[8,16,128]{2,1,0:T(8,128)S(1)}, f32[40,128,128]{2,1,0:T(8,128)S(1)}) custom-call(s32[40,1]{1,0:T(8,128)S(1)} %copy.20.rows, s32[40,1]{1,0:T(8,128)S(1)} %copy.21.cols, s32[1,1]{1,0:T(1,128)S(6)} %copy.22.count, bf16[40,128,128]{2,1,0:T(8,128)(2,1)S(1)} %copy-done.1, bf16[40,128,128]{2,1,0:T(8,128)(2,1)S(1)} %copy-done.3, ...), custom_call_target="tpu_custom_call" | custom-call | tf_op jit(solution)/shard_map/pallas_call | solution.py:29
  83.5 9.7 %all_to_all.48.got_ref = f32[8,16,128]{2,1,0:T(8,128)S(1)} all-to-all(f32[8,16,128]{2,1,0:T(8,128)S(1)} %get-tuple-element.20.sent_ref), channel_id=1, replica_groups=mesh['far'=8,'pair'=2,'x'=4,'y'=4,'core'=2] {'y','core'}, dimensions={0} | all-to-all | bytes 131072 | tf_op jit(solution)/shard_map/all_to_all | solution.py:155
  93.2 2.7 %shard_map.97 = (f32[8,40,128]{2,1,0:T(8,128)S(1)}, f32[8,128]{1,0:T(8,128)}) custom-call(s32[40,1]{1,0:T(8,128)S(1)} %copy.20.rows, s32[40,1]{1,0:T(8,128)S(1)} %copy.21.cols, s32[1,1]{1,0:T(1,128)S(6)} %copy.22.count, f32[8,16,128]{2,1,0:T(8,128)S(1)} %all_to_all.48.got_ref, f32[8,16,128]{2,1,0:T(8,128)S(1)} %get-tuple-element.20.sent_ref, ...), custom_call_target="tpu_custom_call" | custom-call | tf_op jit(solution)/shard_map/pallas_call | solution.py:29
  95.9 20.5 %all_to_all.49 = f32[8,40,128]{2,1,0:T(8,128)S(1)} all-to-all(f32[8,40,128]{2,1,0:T(8,128)S(1)} %get-tuple-element.22), channel_id=1, replica_groups=mesh['far'=8,'pair'=2,'x'=4,'y'=4,'core'=2] {'far'}, dimensions={0} | all-to-all | bytes 327680 | tf_op jit(solution)/shard_map/all_to_all | solution.py:161
  116.5 17.4 %all_to_all.50.got_ref = f32[8,320,128]{2,1,0:T(8,128)S(1)} all-to-all(f32[8,320,128]{2,1,0:T(8,128)S(1)} %broadcast_in_dim.22), channel_id=1, replica_groups=mesh['far'=8,'pair'=2,'x'=4,'y'=4,'core'=2] {'pair','x'}, dimensions={0} | all-to-all | bytes 2621440 | tf_op jit(solution)/shard_map/all_to_all | solution.py:165
  133.9 4.0 %shard_map.98 = (f32[1024,128]{1,0:T(8,128)S(1)}, f32[8,16,128]{2,1,0:T(8,128)S(1)}, f32[40,128,128]{2,1,0:T(8,128)S(1)}) custom-call(s32[40,1]{1,0:T(8,128)S(1)} %copy.20.rows, s32[40,1]{1,0:T(8,128)S(1)} %copy.21.cols, s32[1,1]{1,0:T(1,128)S(6)} %copy.22.count, bf16[40,128,128]{2,1,0:T(8,128)(2,1)S(1)} %copy-done.1, bf16[40,128,128]{2,1,0:T(8,128)(2,1)S(1)} %copy-done.3, ...), custom_call_target="tpu_custom_call" | custom-call | tf_op jit(solution)/shard_map/pallas_call | solution.py:29
  138.0 10.7 %all_to_all.51.got_ref = f32[8,16,128]{2,1,0:T(8,128)S(1)} all-to-all(f32[8,16,128]{2,1,0:T(8,128)S(1)} %get-tuple-element.24.sent_ref), channel_id=1, replica_groups=mesh['far'=8,'pair'=2,'x'=4,'y'=4,'core'=2] {'y','core'}, dimensions={0} | all-to-all | bytes 131072 | tf_op jit(solution)/shard_map/all_to_all | solution.py:155
  148.6 2.7 %shard_map.99 = (f32[8,40,128]{2,1,0:T(8,128)S(1)}, f32[8,128]{1,0:T(8,128)}) custom-call(s32[40,1]{1,0:T(8,128)S(1)} %copy.20.rows, s32[40,1]{1,0:T(8,128)S(1)} %copy.21.cols, s32[1,1]{1,0:T(1,128)S(6)} %copy.22.count, f32[8,16,128]{2,1,0:T(8,128)S(1)} %all_to_all.51.got_ref, f32[8,16,128]{2,1,0:T(8,128)S(1)} %get-tuple-element.24.sent_ref, ...), custom_call_target="tpu_custom_call" | custom-call | tf_op jit(solution)/shard_map/pallas_call | solution.py:29
  151.3 20.0 %all_to_all.52 = f32[8,40,128]{2,1,0:T(8,128)S(1)} all-to-all(f32[8,40,128]{2,1,0:T(8,128)S(1)} %get-tuple-element.26), channel_id=1, replica_groups=mesh['far'=8,'pair'=2,'x'=4,'y'=4,'core'=2] {'far'}, dimensions={0} | all-to-all | bytes 327680 | tf_op jit(solution)/shard_map/all_to_all | solution.py:161
  171.4 19.2 %all_to_all.53.got_ref = f32[8,320,128]{2,1,0:T(8,128)S(1)} all-to-all(f32[8,320,128]{2,1,0:T(8,128)S(1)} %broadcast_in_dim.24), channel_id=1, replica_groups=mesh['far'=8,'pair'=2,'x'=4,'y'=4,'core'=2] {'pair','x'}, dimensions={0} | all-to-all | bytes 2621440 | tf_op jit(solution)/shard_map/all_to_all | solution.py:165
  190.7 2.5 %shard_map.100 = (f32[1024,128]{1,0:T(8,128)}, f32[1024,128]{1,0:T(8,128)}) custom-call(f32[8,320,128]{2,1,0:T(8,128)S(1)} %all_to_all.53.got_ref, s32[1,2560]{1,0:T(1,128)S(1)} %convert_element_type.6.ids_ref, f32[1024,128]{1,0:T(8,128)S(1)} %get-tuple-element.27.price_ref, f32[1024,128]{1,0:T(8,128)S(1)} %bitcast.11), custom_call_target="tpu_custom_call" | custom-call | tf_op jit(solution)/shard_map/pallas_call | solution.py:29
  (20 shorter events, 0.4 us)
Async XLA Ops:
  2.8 1.3 copy-start
  4.1 1.3 copy-start.2
  5.4 1.0 copy-start.7
  53.0 24.1 %copy-start.6 = (f32[131072]{0:T(1024)S(1)}, f32[131072]{0:T(1024)}, u32[]{:S(2)}) copy-start(f32[131072]{0:T(1024)} %param.13) | copy-start | bytes 1572868
  53.1 24.0 %copy-start.1 = (bf16[40,128,128]{2,1,0:T(8,128)(2,1)S(1)}, bf16[40,128,128]{2,1,0:T(8,128)(2,1)}, u32[]{:S(2)}) copy-start(bf16[40,128,128]{2,1,0:T(8,128)(2,1)} %gain_ref.5) | copy-start | bytes 3932164
  53.1 24.0 %copy-start.3 = (bf16[40,128,128]{2,1,0:T(8,128)(2,1)S(1)}, bf16[40,128,128]{2,1,0:T(8,128)(2,1)}, u32[]{:S(2)}) copy-start(bf16[40,128,128]{2,1,0:T(8,128)(2,1)} %cost_ref.5) | copy-start | bytes 3932164
  75.9 1.1 copy-start.4
  77.1 1.3 copy-start.5
  78.5 1.0 copy-start.8

commit v4 on v3

v4 whole, which is shorter than its diff:
```python
import functools
import math

import jax
import jax.numpy as jnp
from jax import lax
from jax.experimental import pallas as pl
from jax.experimental.pallas import tpu as pltpu
from jax.sharding import Mesh, PartitionSpec as P

MB = 8
ROUNDS = 3
SMOOTHING = 0.05
STEP_SIZE = 0.2
SCALE = math.log2(math.e) / SMOOTHING
NF, NP, NX, NY, NC = 8, 2, 4, 4, 2
CAMP = ("y", "core")
NEAR = ("pair", "x")
NN = NP * NX
N_CAMP = NY * NC
TILE = 128
CHUNK = 256
GROUP = 8
F32 = jnp.float32
VMEM = pl.BlockSpec(memory_space=pltpu.VMEM)
HBM = pl.BlockSpec(memory_space=pltpu.HBM)
SMEM = pl.BlockSpec(memory_space=pltpu.SMEM)


def call(body, out_shape, operands, specs, scratch, grant):
    return pl.pallas_call(
        body,
        out_shape=out_shape,
        in_specs=specs,
        out_specs=jax.tree.map(lambda _: VMEM, out_shape),
        scratch_shapes=scratch,
        compiler_params=pltpu.CompilerParams(vmem_limit_bytes=grant * 1024 * 1024),
        cost_estimate=pl.CostEstimate(flops=0, bytes_accessed=0, transcendentals=0),
    )(*operands)


def dense_step(got_ref, ids_ref, price_ref, allow_ref, new_ref, usage_ref, parts):
    per = ids_ref.shape[1] // NN
    for near in range(NN):
        values = got_ref[near, :per, :]
        high = values.astype(jnp.bfloat16)
        parts[near * per : (near + 1) * per, :TILE] = high
        parts[near * per : (near + 1) * per, TILE:] = (values - high.astype(F32)).astype(jnp.bfloat16)
    ids = ids_ref[...]
    blocks = price_ref.shape[0]
    for at in range(0, blocks, CHUNK):
        index = lax.broadcasted_iota(jnp.int32, (CHUNK, 1), 0) + at
        place = jnp.where(ids == index, 1.0, 0.0).astype(jnp.bfloat16)
        both = jnp.dot(place, parts[...], preferred_element_type=F32)
        usage = both[:, :TILE] + both[:, TILE:]
        rows = slice(at, at + CHUNK)
        if usage_ref is not None:
            usage_ref[rows, :] = usage
        new_ref[rows, :] = jnp.maximum(price_ref[rows, :] + STEP_SIZE * (usage - allow_ref[rows, :]), 0.0)


def score_step(plan, slots, gain_ref, cost_ref, price_ref, sent_ref, ex_ref, top, total, arrive=None):
    top[...] = jnp.zeros_like(top)
    total[...] = jnp.zeros_like(total)
    live = plan[2 * slots]

    def score(s):
        block = plan[s]
        price = price_ref[pl.ds(plan[slots + s], 1), :] * SCALE
        value = gain_ref[s].astype(F32) * SCALE - cost_ref[s].astype(F32) * price
        ex_ref[s] = value
        top[block] = jnp.maximum(top[block], value)

    if arrive is None:
        pl.loop(0, live)(score)
    else:
        for part in range(slots // GROUP):
            arrive(part)
            pl.loop(part * GROUP, jnp.minimum(live, (part + 1) * GROUP))(score)

    lane = lax.broadcasted_iota(jnp.int32, (TILE, TILE), 1)
    stats = jnp.zeros((TILE, TILE), F32)
    for b in range(MB):
        best = jnp.broadcast_to(jnp.max(top[b], axis=1, keepdims=True), (TILE, TILE))
        top[b] = best
        stats = jnp.where(lane == b, best, stats)

    @pl.loop(0, live)
    def _(s):
        block = plan[s]
        e = jnp.exp2(ex_ref[s] - top[block])
        total[block] = total[block] + e
        ex_ref[s] = cost_ref[s].astype(F32) * e

    for b in range(MB):
        stats = jnp.where(lane == MB + b, jnp.sum(total[b], axis=1, keepdims=True), stats)
    packed = jnp.transpose(stats)[: 2 * MB, :]
    for k in range(N_CAMP):
        sent_ref[k] = packed


def first_body(plan, gains, costs, duals, gain_ref, cost_ref, price_ref, sent_ref, ex_ref, top, total, sems):
    slots = ex_ref.shape[0]
    price_copy = pltpu.make_async_copy(duals, price_ref, sems.at[2 * (slots // GROUP)])
    price_copy.start()
    copies = []
    for part in range(slots // GROUP):
        rows = pl.ds(part * GROUP, GROUP)
        pair = [
            pltpu.make_async_copy(source.at[rows], target.at[rows], sems.at[2 * part + k])
            for k, (source, target) in enumerate(((gains, gain_ref), (costs, cost_ref)))
        ]
        for copy in pair:
            copy.start()
        copies.append(pair)

    def arrive(part):
        if part == 0:
            price_copy.wait()
        for copy in copies[part]:
            copy.wait()

    score_step(plan, slots, gain_ref, cost_ref, price_ref, sent_ref, ex_ref, top, total, arrive)


def gather_ids(got_ref, ids_ref, slots):
    lane = lax.broadcasted_iota(jnp.int32, (1, TILE), 1)
    lines = [jnp.zeros((1, TILE), F32)] * (ids_ref.shape[1] // TILE + 1)
    for source in range(NN * NF):
        near, far = divmod(source, NF)
        at, shift = divmod(source * slots, TILE)
        first = NF * slots + far
        line = got_ref[near, first : first + 1, :]
        line = pltpu.roll(line, shift, 1) if shift else line
        lines[at] = lines[at] + jnp.where(lane >= shift, line, 0.0)
        if shift + slots > TILE:
            lines[at + 1] = lines[at + 1] + jnp.where(lane < shift + slots - TILE, line, 0.0)
    for at in range(ids_ref.shape[1] // TILE):
        ids_ref[:, at * TILE : (at + 1) * TILE] = lines[at].astype(jnp.int32)


def second_body(plan, gain_ref, cost_ref, got_ref, price_ref, allow_ref,
                new_ref, sent_ref, ex_ref, ids_ref, top, total, parts):
    gather_ids(got_ref, ids_ref, ex_ref.shape[0])
    dense_step(got_ref, ids_ref, price_ref, allow_ref, new_ref, None, parts)
    score_step(plan, ex_ref.shape[0], gain_ref, cost_ref, new_ref, sent_ref, ex_ref, top, total)


def next_body(plan, gain_ref, cost_ref, got_ref, ids_ref, price_ref, allow_ref,
              new_ref, sent_ref, ex_ref, top, total, parts):
    dense_step(got_ref, ids_ref, price_ref, allow_ref, new_ref, None, parts)
    score_step(plan, ex_ref.shape[0], gain_ref, cost_ref, new_ref, sent_ref, ex_ref, top, total)


def merge(got_ref):
    tops = got_ref[:, :MB, :]
    row_top = jnp.max(tops, axis=0)
    spare = jnp.exp2(-row_top)
    return row_top, spare, spare + jnp.sum(got_ref[:, MB:, :] * jnp.exp2(tops - row_top), axis=0)


def last_body(got_ref, ids_ref, price_ref, allow_ref, stats_ref, new_ref, usage_ref, unused_ref, parts):
    _, spare, denom = merge(stats_ref)
    unused_ref[...] = spare / denom
    dense_step(got_ref, ids_ref, price_ref, allow_ref, new_ref, usage_ref, parts)


def use_body(plan, got_ref, sent_ref, ex_ref, use_ref, weights, use, *, with_ids):
    slots = ex_ref.shape[0]
    row_top, _, denom = merge(got_ref)
    weight = jnp.exp2(sent_ref[0, :MB, :] - row_top) / denom
    turned = jnp.transpose(jnp.concatenate([weight] * (TILE // MB), axis=0))
    for b in range(MB):
        weights[b] = jnp.broadcast_to(turned[:, b : b + 1], (TILE, TILE))
    use[...] = jnp.zeros_like(use)

    @pl.loop(0, plan[2 * slots])
    def _(s):
        use[pl.ds(s, 1), :] = jnp.sum(ex_ref[s] * weights[plan[s]], axis=0, keepdims=True)

    if with_ids:
        lane = lax.broadcasted_iota(jnp.int32, (MB, TILE), 1)
        ids = jnp.zeros((MB, TILE), F32)
        for s in range(slots):
            ids = jnp.where(lane == s, plan[slots + s].astype(F32), ids)
        use[slots:, :] = ids
    for k in range(NF):
        use_ref[k] = use[...]


def local(gains, costs, tile_rows, tile_cols, tile_count, duals, allowances):
    slots = gains.shape[0]
    blocks = duals.shape[0] // TILE
    price = duals.reshape(blocks, TILE)
    allow = allowances.reshape(blocks, TILE)
    plan = jnp.concatenate([tile_rows[:, 0], tile_cols[:, 0], tile_count[0]])
    shape = lambda *s: jax.ShapeDtypeStruct(s, F32)
    sent_shape, ex_shape, full_shape = shape(N_CAMP, 2 * MB, TILE), shape(slots, TILE, TILE), shape(blocks, TILE)
    tile_shape = jax.ShapeDtypeStruct(gains.shape, gains.dtype)
    by_block = pltpu.VMEM((MB, TILE, TILE), F32)
    parts = pltpu.VMEM((NF * NN * slots, 2 * TILE), jnp.bfloat16)
    ids_shape = jax.ShapeDtypeStruct((1, NF * NN * slots), jnp.int32)
    got = ids = None
    for step in range(ROUNDS):
        if step == 0:
            gains, costs, price, sent, ex = call(
                first_body, (tile_shape, tile_shape, full_shape, sent_shape, ex_shape),
                (plan, gains, costs, price), [SMEM, HBM, HBM, HBM],
                [by_block, by_block, pltpu.SemaphoreType.DMA((2 * (slots // GROUP) + 1,))], 12)
        elif step == 1:
            price, sent, ex, ids = call(
                second_body, (full_shape, sent_shape, ex_shape, ids_shape),
                (plan, gains, costs, got, price, allow), [SMEM] + [VMEM] * 5,
                [by_block, by_block, parts], 16)
        else:
            price, sent, ex = call(
                next_body, (full_shape, sent_shape, ex_shape),
                (plan, gains, costs, got, ids, price, allow), [SMEM] + [VMEM] * 6,
                [by_block, by_block, parts], 16)
        stats = lax.all_to_all(sent, CAMP, 0, 0)
        extra = MB if step == 0 else 0
        use = call(functools.partial(use_body, with_ids=step == 0), shape(NF, slots + extra, TILE),
                   (plan, stats, sent, ex), [SMEM] + [VMEM] * 3,
                   [by_block, pltpu.VMEM((slots + extra, TILE), F32)], 8)
        far = lax.all_to_all(use, "far", 0, 0)
        rows = far[:, :slots].reshape(NF * slots, TILE)
        if step == 0:
            rows = jnp.concatenate([rows, far[:, slots]])
        got = lax.all_to_all(jnp.broadcast_to(rows[None], (NN,) + rows.shape), NEAR, 0, 0)
    price, usage, unused = call(
        last_body, (full_shape, full_shape, shape(MB, TILE)), (got, ids, price, allow, stats), [VMEM] * 5, [parts], 16)
    return (price.reshape(-1), usage.reshape(-1), unused.reshape(-1))


def solution(mesh):
    grid = Mesh(mesh.devices.reshape(NF, NP, NX, NY, NC), ("far", "pair", "x", "y", "core"))
    mem = ("far", "pair", "x")
    return jax.shard_map(
        local,
        mesh=grid,
        in_specs=(
            P(mem, None, CAMP),
            P(mem, None, CAMP),
            P(mem, CAMP),
            P(mem, CAMP),
            P(mem, CAMP),
            P(CAMP),
            P(CAMP),
        ),
        out_specs=(P(CAMP), P(CAMP), P(mem)),
        check_vma=False,
    )
```

time: 194 us -> 185 us (0.954)
  Pallas kernels: 21.2 us -> 12.3 us
  local copies, waits for them, and re-layouts: 8.98 us -> 3.95 us
  blocking collectives: 162 us -> 166 us
    pallas_call x7, Pallas kernels: 21.2 us -> 12.3 us  [call(): pl.pallas_call(body, out_shape=out_shape, in_specs=specs, out_specs=jax.t...]
    all_to_all x3, blocking collectives: 59.4 us -> 66.4 us  [local(): lax.all_to_all(jnp.broadcast_to(rows[None], (NN,) + rows.shape), NEAR, 0, 0)]
    all_to_all x3, blocking collectives: 31.9 us -> 26.9 us  [local(): stats = lax.all_to_all(sent, CAMP, 0, 0)]
    unnamed x20 -> x8, local copies, waits for them, and re-layouts: 8.62 us -> 3.68 us
    all_to_all x3, blocking collectives: 70.2 us -> 73.2 us  [local(): far = lax.all_to_all(use, 'far', 0, 0)]
where the time goes in v4:
time: 185 us
  blocking collectives  166 us (90%)
  Pallas kernels  12.3 us (7%)
  local copies, waits for them, and re-layouts  3.95 us (2%)
    all_to_all x3, blocking collectives, local(): far = lax.all_to_all(use, 'far', 0, 0)  73.2 us
    all_to_all x3, blocking collectives, local(): lax.all_to_all(jnp.broadcast_to(rows[None], (NN,) + rows.shape), NEAR, 0, 0)  66.4 us
    all_to_all x3, blocking collectives, local(): stats = lax.all_to_all(sent, CAMP, 0, 0)  26.9 us
    pallas_call x7, Pallas kernels, call(): pl.pallas_call(body, out_shape=out_shape, in_specs=specs, out_specs=jax.t...  12.3 us

profile of v4, /device:TPU:8, one launch (start us, length us, event | category | flops | bytes accessed | tf_op | source)
XLA Modules:
  0.0 184.9 jit_solution(4934931730059696808)
XLA Ops:
  1.3 0.7 pad_add_fusion.plan
  2.0 1.3 copy-done.1
  3.3 1.3 copy-done.2
  4.7 1.0 copy-done.3
  5.7 1.5 shard_map.94
  7.2 12.4 %all_to_all.45.got_ref = f32[8,16,128]{2,1,0:T(8,128)S(1)} all-to-all(f32[8,16,128]{2,1,0:T(8,128)S(1)} %get-tuple-element.20.sent_ref), channel_id=1, replica_groups=mesh['far'=8,'pair'=2,'x'=4,'y'=4,'core'=2] {'y','core'}, dimensions={0} | all-to-all | bytes 131072 | tf_op jit(solution)/shard_map/all_to_all | solution.py:220
  19.6 1.0 shard_map.95
  20.6 30.6 %all_to_all.46 = f32[8,48,128]{2,1,0:T(8,128)S(1)} all-to-all(f32[8,48,128]{2,1,0:T(8,128)S(1)} %shard_map.95), channel_id=1, replica_groups=mesh['far'=8,'pair'=2,'x'=4,'y'=4,'core'=2] {'far'}, dimensions={0} | all-to-all | bytes 393216 | tf_op jit(solution)/shard_map/all_to_all | solution.py:225
  51.2 0.1 broadcast_in_dim.20
  51.3 0.0 copy-start
  51.3 24.2 %all_to_all.47.got_ref = f32[8,328,128]{2,1,0:T(8,128)S(1)} all-to-all(f32[8,328,128]{2,1,0:T(8,128)S(1)} %broadcast_in_dim.20), channel_id=1, replica_groups=mesh['far'=8,'pair'=2,'x'=4,'y'=4,'core'=2] {'pair','x'}, dimensions={0} | all-to-all | bytes 2686976 | tf_op jit(solution)/shard_map/all_to_all | solution.py:229
  75.5 2.7 %shard_map.96 = (f32[1024,128]{1,0:T(8,128)S(1)}, f32[8,16,128]{2,1,0:T(8,128)S(1)}, f32[40,128,128]{2,1,0:T(8,128)S(1)}, s32[1,2560]{1,0:T(1,128)S(1)}) custom-call(s32[81]{0:T(128)S(1)} %pad_add_fusion.plan, bf16[40,128,128]{2,1,0:T(8,128)(2,1)S(1)} %get-tuple-element.18.gain_ref, bf16[40,128,128]{2,1,0:T(8,128)(2,1)S(1)} %get-tuple-element.19.cost_ref, ...), custom_call_target="tpu_custom_call" | custom-call | tf_op jit(solution)/shard_map/pallas_call | solution.py:31
  78.2 7.3 %all_to_all.48.got_ref = f32[8,16,128]{2,1,0:T(8,128)S(1)} all-to-all(f32[8,16,128]{2,1,0:T(8,128)S(1)} %get-tuple-element.23.sent_ref), channel_id=1, replica_groups=mesh['far'=8,'pair'=2,'x'=4,'y'=4,'core'=2] {'y','core'}, dimensions={0} | all-to-all | bytes 131072 | tf_op jit(solution)/shard_map/all_to_all | solution.py:220
  85.5 1.0 shard_map.97
  86.4 21.5 %all_to_all.49 = f32[8,40,128]{2,1,0:T(8,128)S(1)} all-to-all(f32[8,40,128]{2,1,0:T(8,128)S(1)} %shard_map.97), channel_id=1, replica_groups=mesh['far'=8,'pair'=2,'x'=4,'y'=4,'core'=2] {'far'}, dimensions={0} | all-to-all | bytes 327680 | tf_op jit(solution)/shard_map/all_to_all | solution.py:225
  107.9 0.1 broadcast_in_dim.22
  108.0 20.6 %all_to_all.50.got_ref = f32[8,320,128]{2,1,0:T(8,128)S(1)} all-to-all(f32[8,320,128]{2,1,0:T(8,128)S(1)} %broadcast_in_dim.22), channel_id=1, replica_groups=mesh['far'=8,'pair'=2,'x'=4,'y'=4,'core'=2] {'pair','x'}, dimensions={0} | all-to-all | bytes 2621440 | tf_op jit(solution)/shard_map/all_to_all | solution.py:229
  128.6 2.6 %shard_map.98 = (f32[1024,128]{1,0:T(8,128)S(1)}, f32[8,16,128]{2,1,0:T(8,128)S(1)}, f32[40,128,128]{2,1,0:T(8,128)S(1)}) custom-call(s32[81]{0:T(128)S(1)} %pad_add_fusion.plan, bf16[40,128,128]{2,1,0:T(8,128)(2,1)S(1)} %get-tuple-element.18.gain_ref, bf16[40,128,128]{2,1,0:T(8,128)(2,1)S(1)} %get-tuple-element.19.cost_ref, ...), custom_call_target="tpu_custom_call" | custom-call | tf_op jit(solution)/shard_map/pallas_call | solution.py:31
  131.2 7.3 %all_to_all.51.got_ref.stats_ref = f32[8,16,128]{2,1,0:T(8,128)S(1)} all-to-all(f32[8,16,128]{2,1,0:T(8,128)S(1)} %get-tuple-element.27.sent_ref), channel_id=1, replica_groups=mesh['far'=8,'pair'=2,'x'=4,'y'=4,'core'=2] {'y','core'}, dimensions={0} | all-to-all | bytes 131072 | tf_op jit(solution)/shard_map/all_to_all | solution.py:220
  138.5 1.0 shard_map.99
  139.5 21.1 %all_to_all.52 = f32[8,40,128]{2,1,0:T(8,128)S(1)} all-to-all(f32[8,40,128]{2,1,0:T(8,128)S(1)} %shard_map.99), channel_id=1, replica_groups=mesh['far'=8,'pair'=2,'x'=4,'y'=4,'core'=2] {'far'}, dimensions={0} | all-to-all | bytes 327680 | tf_op jit(solution)/shard_map/all_to_all | solution.py:225
  160.6 0.1 broadcast_in_dim.24
  160.7 21.6 %all_to_all.53.got_ref = f32[8,320,128]{2,1,0:T(8,128)S(1)} all-to-all(f32[8,320,128]{2,1,0:T(8,128)S(1)} %broadcast_in_dim.24), channel_id=1, replica_groups=mesh['far'=8,'pair'=2,'x'=4,'y'=4,'core'=2] {'pair','x'}, dimensions={0} | all-to-all | bytes 2621440 | tf_op jit(solution)/shard_map/all_to_all | solution.py:229
  182.3 2.5 %shard_map.100 = (f32[1024,128]{1,0:T(8,128)}, f32[1024,128]{1,0:T(8,128)}, f32[8,128]{1,0:T(8,128)}) custom-call(f32[8,320,128]{2,1,0:T(8,128)S(1)} %all_to_all.53.got_ref, s32[1,2560]{1,0:T(1,128)S(1)} %get-tuple-element.25.ids_ref, f32[1024,128]{1,0:T(8,128)S(1)} %get-tuple-element.29.price_ref, f32[1024,128]{1,0:T(8,128)S(1)} %bitcast.15, ...), custom_call_target="tpu_custom_call" | custom-call | tf_op jit(solution)/shard_map/pallas_call | solution.py:31
  (7 shorter events, 0.0 us)
Async XLA Ops:
  2.0 1.3 copy-start.1
  3.3 1.3 copy-start.2
  4.7 1.0 copy-start.3
  51.3 24.2 %copy-start = (f32[131072]{0:T(1024)S(1)}, f32[131072]{0:T(1024)}, u32[]{:S(2)}) copy-start(f32[131072]{0:T(1024)} %param.13) | copy-start | bytes 1572868

commit v5 on v4

v5 whole, which is shorter than its diff:
```python
import functools
import math

import jax
import jax.numpy as jnp
from jax import lax
from jax.experimental import pallas as pl
from jax.experimental.pallas import tpu as pltpu
from jax.sharding import Mesh, PartitionSpec as P

MB = 8
ROUNDS = 3
SMOOTHING = 0.05
STEP_SIZE = 0.2
SCALE = math.log2(math.e) / SMOOTHING
NF, NP, NX, NY, NC = 8, 2, 4, 4, 2
CAMP = ("y", "core")
NEAR = ("pair", "x")
NN = NP * NX
N_CAMP = NY * NC
TILE = 128
CHUNK = 256
GROUP = 4
USE_GROUP = 8
F32 = jnp.float32
VMEM = pl.BlockSpec(memory_space=pltpu.VMEM)
SMEM = pl.BlockSpec(memory_space=pltpu.SMEM)


def call(body, out_shape, operands, specs, scratch, grant, flops=0):
    return pl.pallas_call(
        body,
        out_shape=out_shape,
        in_specs=specs,
        out_specs=jax.tree.map(lambda _: VMEM, out_shape),
        scratch_shapes=scratch,
        compiler_params=pltpu.CompilerParams(vmem_limit_bytes=grant * 1024 * 1024),
        cost_estimate=pl.CostEstimate(flops=flops, bytes_accessed=0, transcendentals=0),
    )(*operands)


def dense_step(got_ref, ids_ref, price_ref, allow_ref, new_ref, usage_ref, parts):
    per = ids_ref.shape[1] // NN
    for near in range(NN):
        values = got_ref[near, :per, :]
        high = values.astype(jnp.bfloat16)
        parts[near * per : (near + 1) * per, :TILE] = high
        parts[near * per : (near + 1) * per, TILE:] = (values - high.astype(F32)).astype(jnp.bfloat16)
    ids = ids_ref[...]
    blocks = price_ref.shape[0]
    for at in range(0, blocks, CHUNK):
        index = lax.broadcasted_iota(jnp.int32, (CHUNK, 1), 0) + at
        place = jnp.where(ids == index, 1.0, 0.0).astype(jnp.bfloat16)
        both = jnp.dot(place, parts[...], preferred_element_type=F32)
        usage = both[:, :TILE] + both[:, TILE:]
        rows = slice(at, at + CHUNK)
        if usage_ref is not None:
            usage_ref[rows, :] = usage
        new_ref[rows, :] = jnp.maximum(price_ref[rows, :] + STEP_SIZE * (usage - allow_ref[rows, :]), 0.0)


def score_step(rows, cols, live, gain_ref, cost_ref, price_ref, sent_ref, ex_ref, top, total):
    top[...] = jnp.zeros_like(top)
    total[...] = jnp.zeros_like(total)
    number = live[0, 0]
    groups = lax.div(number + GROUP - 1, GROUP)

    @pl.loop(0, groups)
    def _(g):
        for k in range(GROUP):
            s = g * GROUP + k
            block = rows[s]
            price = price_ref[pl.ds(cols[s], 1), :] * SCALE
            value = gain_ref[s].astype(F32) * SCALE - cost_ref[s].astype(F32) * price
            ex_ref[s] = value
            top[block] = jnp.maximum(top[block], jnp.where(s < number, value, 0.0))

    lane = lax.broadcasted_iota(jnp.int32, (TILE, TILE), 1)
    stats = jnp.zeros((TILE, TILE), F32)
    for b in range(MB):
        best = jnp.broadcast_to(jnp.max(top[b], axis=1, keepdims=True), (TILE, TILE))
        top[b] = best
        stats = jnp.where(lane == b, best, stats)

    @pl.loop(0, groups)
    def _(g):
        for k in range(GROUP):
            s = g * GROUP + k
            block = rows[s]
            e = jnp.where(s < number, jnp.exp2(ex_ref[s] - top[block]), 0.0)
            total[block] = total[block] + e
            ex_ref[s] = cost_ref[s].astype(F32) * e

    for b in range(MB):
        stats = jnp.where(lane == MB + b, jnp.sum(total[b], axis=1, keepdims=True), stats)
    packed = jnp.transpose(stats)[: 2 * MB, :]
    for k in range(N_CAMP):
        sent_ref[k] = packed


def plan_body(count_ref, live_ref):
    live_ref[...] = jnp.broadcast_to(count_ref[...], live_ref.shape)


def first_body(rows, cols, live, gain_ref, cost_ref, price_ref, sent_ref, ex_ref, top, total):
    score_step(rows, cols, live, gain_ref, cost_ref, price_ref, sent_ref, ex_ref, top, total)


def gather_ids(got_ref, ids_ref, slots):
    lane = lax.broadcasted_iota(jnp.int32, (1, TILE), 1)
    lines = [jnp.zeros((1, TILE), F32)] * (ids_ref.shape[1] // TILE + 1)
    for source in range(NN * NF):
        near, far = divmod(source, NF)
        at, shift = divmod(source * slots, TILE)
        first = NF * slots + far
        line = got_ref[near, first : first + 1, :]
        line = pltpu.roll(line, shift, 1) if shift else line
        lines[at] = lines[at] + jnp.where(lane >= shift, line, 0.0)
        if shift + slots > TILE:
            lines[at + 1] = lines[at + 1] + jnp.where(lane < shift + slots - TILE, line, 0.0)
    for at in range(ids_ref.shape[1] // TILE):
        ids_ref[:, at * TILE : (at + 1) * TILE] = lines[at].astype(jnp.int32)


def second_body(rows, cols, live, gain_ref, cost_ref, got_ref, price_ref, allow_ref,
                new_ref, sent_ref, ex_ref, ids_ref, top, total, parts):
    gather_ids(got_ref, ids_ref, ex_ref.shape[0])
    dense_step(got_ref, ids_ref, price_ref, allow_ref, new_ref, None, parts)
    score_step(rows, cols, live, gain_ref, cost_ref, new_ref, sent_ref, ex_ref, top, total)


def next_body(rows, cols, live, gain_ref, cost_ref, got_ref, ids_ref, price_ref, allow_ref,
              new_ref, sent_ref, ex_ref, top, total, parts):
    dense_step(got_ref, ids_ref, price_ref, allow_ref, new_ref, None, parts)
    score_step(rows, cols, live, gain_ref, cost_ref, new_ref, sent_ref, ex_ref, top, total)


def merge(got_ref):
    tops = got_ref[:, :MB, :]
    row_top = jnp.max(tops, axis=0)
    spare = jnp.exp2(-row_top)
    return row_top, spare, spare + jnp.sum(got_ref[:, MB:, :] * jnp.exp2(tops - row_top), axis=0)


def last_body(got_ref, ids_ref, price_ref, allow_ref, stats_ref, new_ref, usage_ref, unused_ref, parts):
    _, spare, denom = merge(stats_ref)
    unused_ref[...] = spare / denom
    dense_step(got_ref, ids_ref, price_ref, allow_ref, new_ref, usage_ref, parts)


def use_body(rows, cols, live, got_ref, sent_ref, ex_ref, use_ref, weights, use, *, with_ids):
    slots = ex_ref.shape[0]
    row_top, _, denom = merge(got_ref)
    weight = jnp.exp2(sent_ref[0, :MB, :] - row_top) / denom
    turned = jnp.transpose(jnp.concatenate([weight] * (TILE // MB), axis=0))
    for b in range(MB):
        weights[b] = jnp.broadcast_to(turned[:, b : b + 1], (TILE, TILE))
    use[...] = jnp.zeros_like(use)

    number = live[0, 0]

    @pl.loop(0, lax.div(number + USE_GROUP - 1, USE_GROUP))
    def _(g):
        first = pl.multiple_of(g * USE_GROUP, USE_GROUP)
        lines = [
            jnp.sum(ex_ref[first + k] * weights[rows[first + k]], axis=0, keepdims=True) for k in range(USE_GROUP)
        ]
        index = lax.broadcasted_iota(jnp.int32, (USE_GROUP, 1), 0) + first
        use[pl.ds(first, USE_GROUP), :] = jnp.where(index < number, jnp.concatenate(lines, axis=0), 0.0)

    if with_ids:
        lane = lax.broadcasted_iota(jnp.int32, (MB, TILE), 1)
        ids = jnp.zeros((MB, TILE), F32)
        for s in range(slots):
            ids = jnp.where(lane == s, cols[s].astype(F32), ids)
        use[slots:, :] = ids
    for k in range(NF):
        use_ref[k] = use[...]


def local(gains, costs, tile_rows, tile_cols, tile_count, duals, allowances):
    slots = gains.shape[0]
    blocks = duals.shape[0] // TILE
    price = duals.reshape(blocks, TILE)
    allow = allowances.reshape(blocks, TILE)
    live = call(plan_body, jax.ShapeDtypeStruct((MB, TILE), jnp.int32), (tile_count,), [VMEM], [], 4, flops=20000000000)
    plan = (tile_rows[:, 0], tile_cols[:, 0], live)
    shape = lambda *s: jax.ShapeDtypeStruct(s, F32)
    sent_shape, ex_shape, full_shape = shape(N_CAMP, 2 * MB, TILE), shape(slots, TILE, TILE), shape(blocks, TILE)
    by_block = pltpu.VMEM((MB, TILE, TILE), F32)
    parts = pltpu.VMEM((NF * NN * slots, 2 * TILE), jnp.bfloat16)
    ids_shape = jax.ShapeDtypeStruct((1, NF * NN * slots), jnp.int32)
    got = ids = None
    for step in range(ROUNDS):
        if step == 0:
            sent, ex = call(first_body, (sent_shape, ex_shape), plan + (gains, costs, price),
                            [SMEM] * 3 + [VMEM] * 3, [by_block, by_block], 12)
        elif step == 1:
            price, sent, ex, ids = call(
                second_body, (full_shape, sent_shape, ex_shape, ids_shape),
                plan + (gains, costs, got, price, allow), [SMEM] * 3 + [VMEM] * 5,
                [by_block, by_block, parts], 16)
        else:
            price, sent, ex = call(
                next_body, (full_shape, sent_shape, ex_shape),
                plan + (gains, costs, got, ids, price, allow), [SMEM] * 3 + [VMEM] * 6,
                [by_block, by_block, parts], 16)
        stats = lax.all_to_all(sent, CAMP, 0, 0)
        extra = MB if step == 0 else 0
        use = call(functools.partial(use_body, with_ids=step == 0), shape(NF, slots + extra, TILE),
                   plan + (stats, sent, ex), [SMEM] * 3 + [VMEM] * 3,
                   [by_block, pltpu.VMEM((slots + extra, TILE), F32)], 8)
        far = lax.all_to_all(use, "far", 0, 0)
        rows = far[:, :slots].reshape(NF * slots, TILE)
        if step == 0:
            rows = jnp.concatenate([rows, far[:, slots]])
        got = lax.all_to_all(jnp.broadcast_to(rows[None], (NN,) + rows.shape), NEAR, 0, 0)
    price, usage, unused = call(
        last_body, (full_shape, full_shape, shape(MB, TILE)), (got, ids, price, allow, stats), [VMEM] * 5, [parts], 16)
    return (price.reshape(-1), usage.reshape(-1), unused.reshape(-1))


def solution(mesh):
    grid = Mesh(mesh.devices.reshape(NF, NP, NX, NY, NC), ("far", "pair", "x", "y", "core"))
    mem = ("far", "pair", "x")
    return jax.shard_map(
        local,
        mesh=grid,
        in_specs=(
            P(mem, None, CAMP),
            P(mem, None, CAMP),
            P(mem, CAMP),
            P(mem, CAMP),
            P(mem, CAMP),
            P(CAMP),
            P(CAMP),
        ),
        out_specs=(P(CAMP), P(CAMP), P(mem)),
        check_vma=False,
    )
```

time: 185 us -> 181 us (0.978)
  the two profiles are of different devices: /device:TPU:8 before, /device:TPU:64 now
where the time goes in v5:
time: 181 us; the launch traced here: 180 us
  blocking collectives  162 us (90%)
  Pallas kernels  15.3 us (8%)
  local copies, waits for them, and re-layouts  2 us (1%)
    all_to_all x3, blocking collectives, local(): far = lax.all_to_all(use, 'far', 0, 0)  71.4 us
    all_to_all x3, blocking collectives, local(): lax.all_to_all(jnp.broadcast_to(rows[None], (NN,) + rows.shape), NEAR, 0, 0)  65.1 us
    all_to_all x3, blocking collectives, local(): stats = lax.all_to_all(sent, CAMP, 0, 0)  25.2 us
    pallas_call x8, Pallas kernels, call(): pl.pallas_call(body, out_shape=out_shape, in_specs=specs, out_specs=jax.t...  15.3 us

profile of v5, /device:TPU:64, one launch (start us, length us, event | category | flops | bytes accessed | tf_op | source)
XLA Modules:
  0.0 180.4 jit_solution(5802700181404858230)
XLA Ops:
  1.3 0.1 shard_map.94.live
  1.4 1.2 copy-done
  2.6 0.4 copy-done.1
  3.0 0.1 copy-done.3
  3.1 2.0 %shard_map.95 = (f32[8,16,128]{2,1,0:T(8,128)S(1)}, f32[40,128,128]{2,1,0:T(8,128)S(1)}) custom-call(s32[40]{0:T(128)S(1)} %bitcast.16, s32[40]{0:T(128)S(1)} %bitcast.22, s32[8,128]{1,0:T(8,128)S(1)} %shard_map.94.live, bf16[40,128,128]{2,1,0:T(8,128)(2,1)S(1)} %copy-done, bf16[40,128,128]{2,1,0:T(8,128)(2,1)S(1)} %copy-done.1, f32[1024,128]{1,0:T(8,128)S(1)} %bitcast.14), custom_call_target="tpu_custom_call" | custom-call | tf_op jit(solution)/shard_map/pallas_call | solution.py:31
  5.1 9.2 %all_to_all.45.got_ref = f32[8,16,128]{2,1,0:T(8,128)S(1)} all-to-all(f32[8,16,128]{2,1,0:T(8,128)S(1)} %get-tuple-element.15.sent_ref), channel_id=1, replica_groups=mesh['far'=8,'pair'=2,'x'=4,'y'=4,'core'=2] {'y','core'}, dimensions={0} | all-to-all | bytes 131072 | tf_op jit(solution)/shard_map/all_to_all | solution.py:208
  14.3 1.2 shard_map.96
  15.5 32.0 %all_to_all.46 = f32[8,48,128]{2,1,0:T(8,128)S(1)} all-to-all(f32[8,48,128]{2,1,0:T(8,128)S(1)} %shard_map.96), channel_id=1, replica_groups=mesh['far'=8,'pair'=2,'x'=4,'y'=4,'core'=2] {'far'}, dimensions={0} | all-to-all | bytes 393216 | tf_op jit(solution)/shard_map/all_to_all | solution.py:213
  47.5 0.1 broadcast_in_dim.20
  47.6 0.0 copy-start.2
  47.7 23.9 %all_to_all.47.got_ref = f32[8,328,128]{2,1,0:T(8,128)S(1)} all-to-all(f32[8,328,128]{2,1,0:T(8,128)S(1)} %broadcast_in_dim.20), channel_id=1, replica_groups=mesh['far'=8,'pair'=2,'x'=4,'y'=4,'core'=2] {'pair','x'}, dimensions={0} | all-to-all | bytes 2686976 | tf_op jit(solution)/shard_map/all_to_all | solution.py:217
  71.5 3.5 %shard_map.97 = (f32[1024,128]{1,0:T(8,128)S(1)}, f32[8,16,128]{2,1,0:T(8,128)S(1)}, f32[40,128,128]{2,1,0:T(8,128)S(1)}, s32[1,2560]{1,0:T(1,128)S(1)}) custom-call(s32[40]{0:T(128)S(1)} %bitcast.18, s32[40]{0:T(128)S(1)} %bitcast.24, s32[8,128]{1,0:T(8,128)S(1)} %shard_map.94.live, bf16[40,128,128]{2,1,0:T(8,128)(2,1)S(1)} %copy-done, ...), custom_call_target="tpu_custom_call" | custom-call | tf_op jit(solution)/shard_map/pallas_call | solution.py:31
  75.1 8.0 %all_to_all.48.got_ref = f32[8,16,128]{2,1,0:T(8,128)S(1)} all-to-all(f32[8,16,128]{2,1,0:T(8,128)S(1)} %get-tuple-element.17.sent_ref), channel_id=1, replica_groups=mesh['far'=8,'pair'=2,'x'=4,'y'=4,'core'=2] {'y','core'}, dimensions={0} | all-to-all | bytes 131072 | tf_op jit(solution)/shard_map/all_to_all | solution.py:208
  83.1 1.2 shard_map.98
  84.3 19.3 %all_to_all.49 = f32[8,40,128]{2,1,0:T(8,128)S(1)} all-to-all(f32[8,40,128]{2,1,0:T(8,128)S(1)} %shard_map.98), channel_id=1, replica_groups=mesh['far'=8,'pair'=2,'x'=4,'y'=4,'core'=2] {'far'}, dimensions={0} | all-to-all | bytes 327680 | tf_op jit(solution)/shard_map/all_to_all | solution.py:213
  103.6 0.1 broadcast_in_dim.22
  103.7 20.0 %all_to_all.50.got_ref = f32[8,320,128]{2,1,0:T(8,128)S(1)} all-to-all(f32[8,320,128]{2,1,0:T(8,128)S(1)} %broadcast_in_dim.22), channel_id=1, replica_groups=mesh['far'=8,'pair'=2,'x'=4,'y'=4,'core'=2] {'pair','x'}, dimensions={0} | all-to-all | bytes 2621440 | tf_op jit(solution)/shard_map/all_to_all | solution.py:217
  123.7 3.5 %shard_map.99 = (f32[1024,128]{1,0:T(8,128)S(1)}, f32[8,16,128]{2,1,0:T(8,128)S(1)}, f32[40,128,128]{2,1,0:T(8,128)S(1)}) custom-call(s32[40]{0:T(128)S(1)} %bitcast.20, s32[40]{0:T(128)S(1)} %bitcast.26, s32[8,128]{1,0:T(8,128)S(1)} %shard_map.94.live, bf16[40,128,128]{2,1,0:T(8,128)(2,1)S(1)} %copy-done, bf16[40,128,128]{2,1,0:T(8,128)(2,1)S(1)} %copy-done.1, ...), custom_call_target="tpu_custom_call" | custom-call | tf_op jit(solution)/shard_map/pallas_call | solution.py:31
  127.2 8.1 %all_to_all.51.got_ref.stats_ref = f32[8,16,128]{2,1,0:T(8,128)S(1)} all-to-all(f32[8,16,128]{2,1,0:T(8,128)S(1)} %get-tuple-element.21.sent_ref), channel_id=1, replica_groups=mesh['far'=8,'pair'=2,'x'=4,'y'=4,'core'=2] {'y','core'}, dimensions={0} | all-to-all | bytes 131072 | tf_op jit(solution)/shard_map/all_to_all | solution.py:208
  135.2 1.2 shard_map.100
  136.5 20.1 %all_to_all.52 = f32[8,40,128]{2,1,0:T(8,128)S(1)} all-to-all(f32[8,40,128]{2,1,0:T(8,128)S(1)} %shard_map.100), channel_id=1, replica_groups=mesh['far'=8,'pair'=2,'x'=4,'y'=4,'core'=2] {'far'}, dimensions={0} | all-to-all | bytes 327680 | tf_op jit(solution)/shard_map/all_to_all | solution.py:213
  156.6 0.1 broadcast_in_dim.24
  156.7 21.2 %all_to_all.53.got_ref = f32[8,320,128]{2,1,0:T(8,128)S(1)} all-to-all(f32[8,320,128]{2,1,0:T(8,128)S(1)} %broadcast_in_dim.24), channel_id=1, replica_groups=mesh['far'=8,'pair'=2,'x'=4,'y'=4,'core'=2] {'pair','x'}, dimensions={0} | all-to-all | bytes 2621440 | tf_op jit(solution)/shard_map/all_to_all | solution.py:217
  177.9 2.5 %shard_map.101 = (f32[1024,128]{1,0:T(8,128)}, f32[1024,128]{1,0:T(8,128)}, f32[8,128]{1,0:T(8,128)}) custom-call(f32[8,320,128]{2,1,0:T(8,128)S(1)} %all_to_all.53.got_ref, s32[1,2560]{1,0:T(1,128)S(1)} %get-tuple-element.19.ids_ref, f32[1024,128]{1,0:T(8,128)S(1)} %get-tuple-element.23.price_ref, f32[1024,128]{1,0:T(8,128)S(1)} %bitcast.13, ...), custom_call_target="tpu_custom_call" | custom-call | tf_op jit(solution)/shard_map/pallas_call | solution.py:31
  (11 shorter events, 0.0 us)
Async XLA Ops:
  1.3 1.3 copy-start
  1.3 1.7 copy-start.1
  1.3 1.8 %copy-start.3 = (f32[131072]{0:T(1024)S(1)}, f32[131072]{0:T(1024)}, u32[]{:S(2)}) copy-start(f32[131072]{0:T(1024)} %param.12) | copy-start | bytes 1572868
  1.3 1.8 copy-start.4
  1.3 1.8 copy-start.5
  47.6 23.9 %copy-start.2 = (f32[131072]{0:T(1024)S(1)}, f32[131072]{0:T(1024)}, u32[]{:S(2)}) copy-start(f32[131072]{0:T(1024)} %param.13) | copy-start | bytes 1572868

commit v6 on v5

v6 whole, which is shorter than its diff:
```python
import functools
import math

import jax
import jax.numpy as jnp
from jax import lax
from jax.experimental import pallas as pl
from jax.experimental.pallas import tpu as pltpu
from jax.sharding import Mesh, PartitionSpec as P

MB = 8
SMOOTHING = 0.05
STEP_SIZE = 0.2
SCALE = math.log2(math.e) / SMOOTHING
NF, NP, NX, NY, NC = 8, 2, 4, 4, 2
CAMP = ("y", "core")
NEAR = ("pair", "x")
NN = NP * NX
N_CAMP = NY * NC
TILE = 128
CHUNK = 256
GROUP = 4
USE_GROUP = 8
OWN = 16
F32 = jnp.float32
VMEM = pl.BlockSpec(memory_space=pltpu.VMEM)
SMEM = pl.BlockSpec(memory_space=pltpu.SMEM)


def call(body, out_shape, operands, specs, scratch, grant, flops=0):
    return pl.pallas_call(
        body,
        out_shape=out_shape,
        in_specs=specs,
        out_specs=jax.tree.map(lambda _: VMEM, out_shape),
        scratch_shapes=scratch,
        compiler_params=pltpu.CompilerParams(vmem_limit_bytes=grant * 1024 * 1024),
        cost_estimate=pl.CostEstimate(flops=flops, bytes_accessed=0, transcendentals=0),
    )(*operands)


def dense_step(ids_ref, price_ref, allow_ref, new_ref, usage_ref, parts):
    ids = ids_ref[...]
    for at in range(0, price_ref.shape[0], CHUNK):
        index = lax.broadcasted_iota(jnp.int32, (CHUNK, 1), 0) + at
        place = jnp.where(ids == index, 1.0, 0.0).astype(jnp.bfloat16)
        both = jnp.dot(place, parts[...], preferred_element_type=F32)
        usage = both[:, :TILE] + both[:, TILE:]
        rows = slice(at, at + CHUNK)
        if usage_ref is not None:
            usage_ref[rows, :] = usage
        new_ref[rows, :] = jnp.maximum(price_ref[rows, :] + STEP_SIZE * (usage - allow_ref[rows, :]), 0.0)


def score_step(rows, live, gain_ref, cost_ref, price_of, sent_ref, ex_ref, top, total):
    top[...] = jnp.zeros_like(top)
    total[...] = jnp.zeros_like(total)
    number = live[0, 0]
    groups = lax.div(number + GROUP - 1, GROUP)

    @pl.loop(0, groups)
    def _(g):
        for k in range(GROUP):
            s = g * GROUP + k
            block = rows[s]
            price = price_of(s) * SCALE
            value = gain_ref[s].astype(F32) * SCALE - cost_ref[s].astype(F32) * price
            ex_ref[s] = value
            top[block] = jnp.maximum(top[block], jnp.where(s < number, value, 0.0))

    lane = lax.broadcasted_iota(jnp.int32, (TILE, TILE), 1)
    stats = jnp.zeros((TILE, TILE), F32)
    for b in range(MB):
        best = jnp.broadcast_to(jnp.max(top[b], axis=1, keepdims=True), (TILE, TILE))
        top[b] = best
        stats = jnp.where(lane == b, best, stats)

    @pl.loop(0, groups)
    def _(g):
        for k in range(GROUP):
            s = g * GROUP + k
            block = rows[s]
            e = jnp.where(s < number, jnp.exp2(ex_ref[s] - top[block]), 0.0)
            total[block] = total[block] + e
            ex_ref[s] = cost_ref[s].astype(F32) * e

    for b in range(MB):
        stats = jnp.where(lane == MB + b, jnp.sum(total[b], axis=1, keepdims=True), stats)
    packed = jnp.transpose(stats)[: 2 * MB, :]
    for k in range(N_CAMP):
        sent_ref[k] = packed


def plan_body(count_ref, live_ref):
    live_ref[...] = jnp.broadcast_to(count_ref[...], live_ref.shape)


def row_of(ref, cols):
    return lambda s: ref[pl.ds(cols[s], 1), :]


def first_body(rows, cols, live, gain_ref, cost_ref, price_ref, sent_ref, ex_ref, top, total):
    score_step(rows, live, gain_ref, cost_ref, row_of(price_ref, cols), sent_ref, ex_ref, top, total)


def line_up(lines, slots, width):
    lane = lax.broadcasted_iota(jnp.int32, (1, TILE), 1)
    out = [jnp.zeros((1, TILE), F32)] * (width // TILE + 1)
    for source, line in enumerate(lines):
        at, shift = divmod(source * slots, TILE)
        line = pltpu.roll(line, shift, 1) if shift else line
        out[at] = out[at] + jnp.where(lane >= shift, line, 0.0)
        if shift + slots > TILE:
            out[at + 1] = out[at + 1] + jnp.where(lane < shift + slots - TILE, line, 0.0)
    at, shift = divmod(len(lines) * slots, TILE)
    if shift:
        out[at] = jnp.where(lane < shift, out[at], -1.0)
    return [x.astype(jnp.int32) for x in out[: width // TILE]]


def near_index():
    return lax.axis_index("pair") * NX + lax.axis_index("x")


def want(got_ref, wanted_ref, slots):
    near, far = near_index(), lax.axis_index("far")
    first = NF * slots
    width = wanted_ref.shape[1]
    ids = line_up([got_ref[k, pl.ds(first + far, 1), :] for k in range(NN)], slots, width)
    ids = jnp.concatenate(ids, axis=1)
    asked = jnp.transpose(jnp.concatenate([got_ref[near, first : first + NF, :]] * (TILE // NF), axis=0))
    index = lax.broadcasted_iota(jnp.int32, (OWN, 1), 0)
    names = []
    for k in range(NF):
        names.append(asked[:slots, k : k + 1].astype(jnp.int32))
        names.append(index + (near * NF + k) * OWN)
    names = jnp.concatenate(names, axis=0)
    wanted_ref[...] = jnp.where(names == ids, 1.0, 0.0).astype(jnp.bfloat16)


def split_into(parts, rows, values):
    high = values.astype(jnp.bfloat16)
    parts[rows, :TILE] = high
    parts[rows, TILE:] = (values - high.astype(F32)).astype(jnp.bfloat16)


def pull_body(wanted_ref, got_ref, asked_ref, parts):
    slots = got_ref.shape[1]
    count = NN * slots
    split_into(parts, slice(0, count), got_ref[...].reshape(count, TILE))
    parts[count:, :] = jnp.zeros((parts.shape[0] - count, 2 * TILE), jnp.bfloat16)
    both = jnp.dot(wanted_ref[...], parts[...], preferred_element_type=F32)
    asked_ref[...] = (both[:, :TILE] + both[:, TILE:]).reshape(asked_ref.shape)


def second_body(rows, cols, live, gain_ref, cost_ref, got_ref, price_ref, allow_ref,
                new_ref, sent_ref, ex_ref, ids_ref, wanted_ref, top, total, parts):
    slots = ex_ref.shape[0]
    lines = [got_ref[near, NF * slots + far : NF * slots + far + 1, :] for near in range(NN) for far in range(NF)]
    for at, line in enumerate(line_up(lines, slots, ids_ref.shape[1])):
        ids_ref[:, at * TILE : (at + 1) * TILE] = line
    want(got_ref, wanted_ref, slots)
    for near in range(NN):
        split_into(parts, slice(near * NF * slots, (near + 1) * NF * slots), got_ref[near, : NF * slots, :])
    dense_step(ids_ref, price_ref, allow_ref, new_ref, None, parts)
    score_step(rows, live, gain_ref, cost_ref, row_of(new_ref, cols), sent_ref, ex_ref, top, total)


def third_body(rows, cols, live, gain_ref, cost_ref, got_ref, price_ref, allow_ref,
               sent_ref, ex_ref, own_ref, top, total, use):
    slots = ex_ref.shape[0]
    use[...] = jnp.sum(got_ref[...], axis=0)

    def step(price, usage, allow):
        return jnp.maximum(price + STEP_SIZE * (usage - allow), 0.0)

    first = pl.multiple_of((near_index() * NF + lax.axis_index("far")) * OWN, OWN)
    own = pl.ds(first, OWN)
    own_ref[...] = step(price_ref[own, :], use[slots:, :], allow_ref[own, :])
    price, allow = row_of(price_ref, cols), row_of(allow_ref, cols)
    price_of = lambda s: step(price(s), use[pl.ds(s, 1), :], allow(s))
    score_step(rows, live, gain_ref, cost_ref, price_of, sent_ref, ex_ref, top, total)


def merge(got_ref):
    tops = got_ref[:, :MB, :]
    row_top = jnp.max(tops, axis=0)
    spare = jnp.exp2(-row_top)
    return row_top, spare, spare + jnp.sum(got_ref[:, MB:, :] * jnp.exp2(tops - row_top), axis=0)


def last_body(got_ref, ids_ref, allow_ref, stats_ref, new_ref, usage_ref, unused_ref, parts, price):
    _, spare, denom = merge(stats_ref)
    unused_ref[...] = spare / denom
    per = got_ref.shape[1] // NF
    slots = per - OWN
    for near in range(NN):
        rows = []
        for far in range(NF):
            first = far * per
            rows.append(got_ref[near, first : first + slots, :])
            block = (near * NF + far) * OWN
            price[block : block + OWN, :] = got_ref[near, first + slots : first + per, :]
        split_into(parts, slice(near * NF * slots, (near + 1) * NF * slots), jnp.concatenate(rows, axis=0))
    dense_step(ids_ref, price, allow_ref, new_ref, usage_ref, parts)


def use_body(rows, cols, live, got_ref, sent_ref, ex_ref, *rest, step):
    own_ref = rest[0] if step == 2 else None
    use_ref, weights, use = rest[-3:]
    slots = ex_ref.shape[0]
    row_top, _, denom = merge(got_ref)
    weight = jnp.exp2(sent_ref[0, :MB, :] - row_top) / denom
    turned = jnp.transpose(jnp.concatenate([weight] * (TILE // MB), axis=0))
    for b in range(MB):
        weights[b] = jnp.broadcast_to(turned[:, b : b + 1], (TILE, TILE))
    use[...] = jnp.zeros_like(use)

    number = live[0, 0]

    @pl.loop(0, lax.div(number + USE_GROUP - 1, USE_GROUP))
    def _(g):
        first = pl.multiple_of(g * USE_GROUP, USE_GROUP)
        lines = [
            jnp.sum(ex_ref[first + k] * weights[rows[first + k]], axis=0, keepdims=True) for k in range(USE_GROUP)
        ]
        index = lax.broadcasted_iota(jnp.int32, (USE_GROUP, 1), 0) + first
        use[pl.ds(first, USE_GROUP), :] = jnp.where(index < number, jnp.concatenate(lines, axis=0), 0.0)

    if step == 0:
        lane = lax.broadcasted_iota(jnp.int32, (MB, TILE), 1)
        ids = jnp.zeros((MB, TILE), F32)
        for s in range(slots):
            ids = jnp.where(lane == s, cols[s].astype(F32), ids)
        use[slots:, :] = ids
    elif step == 2:
        use[slots:, :] = own_ref[...]
    for k in range(NF):
        use_ref[k] = use[...]


def local(gains, costs, tile_rows, tile_cols, tile_count, duals, allowances):
    slots = gains.shape[0]
    blocks = duals.shape[0] // TILE
    price = duals.reshape(blocks, TILE)
    allow = allowances.reshape(blocks, TILE)
    live = call(plan_body, jax.ShapeDtypeStruct((MB, TILE), jnp.int32), (tile_count,), [VMEM], [], 4, flops=20000000000)
    plan = (tile_rows[:, 0], tile_cols[:, 0], live)
    shape = lambda *s: jax.ShapeDtypeStruct(s, F32)
    sent_shape, ex_shape, full_shape = shape(N_CAMP, 2 * MB, TILE), shape(slots, TILE, TILE), shape(blocks, TILE)
    by_block = pltpu.VMEM((MB, TILE, TILE), F32)
    parts = pltpu.VMEM((NF * NN * slots, 2 * TILE), jnp.bfloat16)
    ids_shape = jax.ShapeDtypeStruct((1, NF * NN * slots), jnp.int32)
    width = -(-NN * slots // TILE) * TILE
    wanted_shape = jax.ShapeDtypeStruct((NF * (slots + OWN), width), jnp.bfloat16)

    def usage_rows(step, stats, sent, ex, own=()):
        extra = {0: MB, 1: 0, 2: OWN}[step]
        return call(functools.partial(use_body, step=step), shape(NF, slots + extra, TILE),
                    plan + (stats, sent, ex) + own, [SMEM] * 3 + [VMEM] * (3 + len(own)),
                    [by_block, pltpu.VMEM((slots + extra, TILE), F32)], 8)

    def to_near(rows):
        return lax.all_to_all(jnp.broadcast_to(rows[None], (NN,) + rows.shape), NEAR, 0, 0)

    sent, ex = call(first_body, (sent_shape, ex_shape), plan + (gains, costs, price),
                    [SMEM] * 3 + [VMEM] * 3, [by_block, by_block], 12)
    stats = lax.all_to_all(sent, CAMP, 0, 0)
    far = lax.all_to_all(usage_rows(0, stats, sent, ex), "far", 0, 0)
    got = to_near(jnp.concatenate([far[:, :slots].reshape(NF * slots, TILE), far[:, slots]]))

    price, sent, ex, ids, wanted = call(
        second_body, (full_shape, sent_shape, ex_shape, ids_shape, wanted_shape),
        plan + (gains, costs, got, price, allow), [SMEM] * 3 + [VMEM] * 5, [by_block, by_block, parts], 16)
    stats = lax.all_to_all(sent, CAMP, 0, 0)
    got = lax.all_to_all(usage_rows(1, stats, sent, ex), NEAR, 0, 0)
    asked = call(pull_body, shape(NF, slots + OWN, TILE), (wanted, got), [VMEM] * 2,
                 [pltpu.VMEM((width, 2 * TILE), jnp.bfloat16)], 8)
    got = lax.all_to_all(asked, "far", 0, 0)

    sent, ex, own = call(
        third_body, (sent_shape, ex_shape, shape(OWN, TILE)), plan + (gains, costs, got, price, allow),
        [SMEM] * 3 + [VMEM] * 5, [by_block, by_block, pltpu.VMEM((slots + OWN, TILE), F32)], 12)
    stats = lax.all_to_all(sent, CAMP, 0, 0)
    far = lax.all_to_all(usage_rows(2, stats, sent, ex, (own,)), "far", 0, 0)
    got = to_near(far.reshape(NF * (slots + OWN), TILE))
    price, usage, unused = call(
        last_body, (full_shape, full_shape, shape(MB, TILE)), (got, ids, allow, stats), [VMEM] * 4,
        [parts, pltpu.VMEM((blocks, TILE), F32)], 16)
    return (price.reshape(-1), usage.reshape(-1), unused.reshape(-1))


def solution(mesh):
    grid = Mesh(mesh.devices.reshape(NF, NP, NX, NY, NC), ("far", "pair", "x", "y", "core"))
    mem = ("far", "pair", "x")
    return jax.shard_map(
        local,
        mesh=grid,
        in_specs=(
            P(mem, None, CAMP),
            P(mem, None, CAMP),
            P(mem, CAMP),
            P(mem, CAMP),
            P(mem, CAMP),
            P(CAMP),
            P(CAMP),
        ),
        out_specs=(P(CAMP), P(CAMP), P(mem)),
        check_vma=False,
    )
```

time: 181 us -> 178 us (0.983)
  the two profiles are of different devices: /device:TPU:64 before, /device:TPU:8 now
where the time goes in v6:
time: 178 us
  blocking collectives  163 us (92%)
  Pallas kernels  11.6 us (7%)
  local copies, waits for them, and re-layouts  1.95 us (1%)
    all_to_all x2, blocking collectives, to_near(): lax.all_to_all(jnp.broadcast_to(rows[None], (NN,) + rows.shape), NEAR, 0, 0)  46.5 us
    all_to_all x1, blocking collectives, local(): far = lax.all_to_all(usage_rows(0, stats, sent, ex), 'far', 0, 0)  30 us
    all_to_all x3, blocking collectives, local(): stats = lax.all_to_all(sent, CAMP, 0, 0)  29.5 us
    all_to_all x1, blocking collectives, local(): got = lax.all_to_all(asked, 'far', 0, 0)  24.8 us
    all_to_all x1, blocking collectives, local(): far = lax.all_to_all(usage_rows(2, stats, sent, ex, (own,)), 'far', 0, 0)  22.1 us
    pallas_call x9, Pallas kernels, call(): pl.pallas_call(body, out_shape=out_shape, in_specs=specs, out_specs=jax.t...  11.6 us
    all_to_all x1, blocking collectives, local(): got = lax.all_to_all(usage_rows(1, stats, sent, ex), NEAR, 0, 0)  9.74 us

profile of v6, /device:TPU:8, one launch (start us, length us, event | category | flops | bytes accessed | tf_op | source)
XLA Modules:
  0.0 177.5 jit_solution(17117068294681734640)
XLA Ops:
  1.3 0.1 shard_map.94.live
  1.4 1.2 copy-done
  2.6 0.4 copy-done.1
  3.0 0.1 copy-done.3
  3.1 1.3 shard_map.95
  4.4 12.8 %all_to_all.45.got_ref = f32[8,16,128]{2,1,0:T(8,128)S(1)} all-to-all(f32[8,16,128]{2,1,0:T(8,128)S(1)} %get-tuple-element.16.sent_ref), channel_id=1, replica_groups=mesh['far'=8,'pair'=2,'x'=4,'y'=4,'core'=2] {'y','core'}, dimensions={0} | all-to-all | bytes 131072 | tf_op jit(solution)/shard_map/all_to_all | solution.py:268
  17.2 1.1 shard_map.96
  18.2 30.0 %all_to_all.46 = f32[8,48,128]{2,1,0:T(8,128)S(1)} all-to-all(f32[8,48,128]{2,1,0:T(8,128)S(1)} %shard_map.96), channel_id=1, replica_groups=mesh['far'=8,'pair'=2,'x'=4,'y'=4,'core'=2] {'far'}, dimensions={0} | all-to-all | bytes 393216 | tf_op jit(solution)/shard_map/all_to_all | solution.py:269
  48.3 0.0 copy-start.2
  48.3 0.1 broadcast_in_dim.6
  48.4 20.3 %all_to_all.47.got_ref = f32[8,328,128]{2,1,0:T(8,128)S(1)} all-to-all(f32[8,328,128]{2,1,0:T(8,128)S(1)} %broadcast_in_dim.6), channel_id=1, replica_groups=mesh['far'=8,'pair'=2,'x'=4,'y'=4,'core'=2] {'pair','x'}, dimensions={0} | all-to-all | bytes 2686976 | tf_op jit(solution)/shard_map/all_to_all | solution.py:264
  68.6 2.9 %shard_map.97 = (f32[1024,128]{1,0:T(8,128)S(1)}, f32[8,16,128]{2,1,0:T(8,128)S(1)}, f32[40,128,128]{2,1,0:T(8,128)S(1)}, s32[1,2560]{1,0:T(1,128)S(1)}, bf16[448,384]{1,0:T(8,128)(2,1)S(1)}) custom-call(s32[40]{0:T(128)S(1)} %bitcast.17, s32[40]{0:T(128)S(1)} %bitcast.23, s32[8,128]{1,0:T(8,128)S(1)} %shard_map.94.live, bf16[40,128,128]{2,1,0:T(8,128)(2,1)S(1)} %copy-done, ...), custom_call_target="tpu_custom_call" | custom-call | tf_op jit(solution)/shard_map/pallas_call | solution.py:31
  71.5 8.5 %all_to_all.48.got_ref = f32[8,16,128]{2,1,0:T(8,128)S(1)} all-to-all(f32[8,16,128]{2,1,0:T(8,128)S(1)} %get-tuple-element.19.sent_ref), channel_id=1, replica_groups=mesh['far'=8,'pair'=2,'x'=4,'y'=4,'core'=2] {'y','core'}, dimensions={0} | all-to-all | bytes 131072 | tf_op jit(solution)/shard_map/all_to_all | solution.py:275
  80.0 1.1 shard_map.98
  81.1 9.7 %all_to_all.49.got_ref = f32[8,40,128]{2,1,0:T(8,128)S(1)} all-to-all(f32[8,40,128]{2,1,0:T(8,128)S(1)} %shard_map.98), channel_id=1, replica_groups=mesh['far'=8,'pair'=2,'x'=4,'y'=4,'core'=2] {'pair','x'}, dimensions={0} | all-to-all | bytes 327680 | tf_op jit(solution)/shard_map/all_to_all | solution.py:276
  90.8 0.3 shard_map.99
  91.1 24.8 %all_to_all.50.got_ref = f32[8,56,128]{2,1,0:T(8,128)S(1)} all-to-all(f32[8,56,128]{2,1,0:T(8,128)S(1)} %shard_map.99), channel_id=1, replica_groups=mesh['far'=8,'pair'=2,'x'=4,'y'=4,'core'=2] {'far'}, dimensions={0} | all-to-all | bytes 458752 | tf_op jit(solution)/shard_map/all_to_all | solution.py:279
  115.9 1.3 shard_map.100
  117.2 8.2 %all_to_all.51.got_ref.stats_ref = f32[8,16,128]{2,1,0:T(8,128)S(1)} all-to-all(f32[8,16,128]{2,1,0:T(8,128)S(1)} %get-tuple-element.22.sent_ref), channel_id=1, replica_groups=mesh['far'=8,'pair'=2,'x'=4,'y'=4,'core'=2] {'y','core'}, dimensions={0} | all-to-all | bytes 131072 | tf_op jit(solution)/shard_map/all_to_all | solution.py:284
  125.4 1.1 shard_map.101
  126.5 22.1 %all_to_all.52 = f32[8,56,128]{2,1,0:T(8,128)S(1)} all-to-all(f32[8,56,128]{2,1,0:T(8,128)S(1)} %shard_map.101), channel_id=1, replica_groups=mesh['far'=8,'pair'=2,'x'=4,'y'=4,'core'=2] {'far'}, dimensions={0} | all-to-all | bytes 458752 | tf_op jit(solution)/shard_map/all_to_all | solution.py:285
  148.6 0.1 broadcast_in_dim.15
  148.8 26.2 %all_to_all.53.got_ref = f32[8,448,128]{2,1,0:T(8,128)S(1)} all-to-all(f32[8,448,128]{2,1,0:T(8,128)S(1)} %broadcast_in_dim.15), channel_id=1, replica_groups=mesh['far'=8,'pair'=2,'x'=4,'y'=4,'core'=2] {'pair','x'}, dimensions={0} | all-to-all | bytes 3670016 | tf_op jit(solution)/shard_map/all_to_all | solution.py:264
  175.0 2.5 %shard_map.102 = (f32[1024,128]{1,0:T(8,128)}, f32[1024,128]{1,0:T(8,128)}, f32[8,128]{1,0:T(8,128)}) custom-call(f32[8,448,128]{2,1,0:T(8,128)S(1)} %all_to_all.53.got_ref, s32[1,2560]{1,0:T(1,128)S(1)} %get-tuple-element.25.ids_ref, f32[1024,128]{1,0:T(8,128)S(1)} %bitcast.12, f32[8,16,128]{2,1,0:T(8,128)S(1)} %all_to_all.51.got_ref.stats_ref), custom_call_target="tpu_custom_call" | custom-call | tf_op jit(solution)/shard_map/pallas_call | solution.py:31
  (11 shorter events, 0.0 us)
Async XLA Ops:
  1.3 1.3 copy-start
  1.3 1.7 copy-start.1
  1.3 1.8 %copy-start.3 = (f32[131072]{0:T(1024)S(1)}, f32[131072]{0:T(1024)}, u32[]{:S(2)}) copy-start(f32[131072]{0:T(1024)} %param.12) | copy-start | bytes 1572868
  1.3 1.8 %copy-start.4 = (s32[40,1]{0,1:T(1,128)S(1)}, s32[40,1]{0,1:T(1,128)}, u32[]{:S(2)}) copy-start(s32[40,1]{0,1:T(1,128)} %param.9) | copy-start | bytes 484
  1.3 1.8 %copy-start.5 = (s32[40,1]{0,1:T(1,128)S(1)}, s32[40,1]{0,1:T(1,128)}, u32[]{:S(2)}) copy-start(s32[40,1]{0,1:T(1,128)} %param.10) | copy-start | bytes 484
  48.3 20.4 %copy-start.2 = (f32[131072]{0:T(1024)S(1)}, f32[131072]{0:T(1024)}, u32[]{:S(2)}) copy-start(f32[131072]{0:T(1024)} %param.13) | copy-start | bytes 1572868

commit v7 on v6

v7 whole, which is shorter than its diff:
```python
import functools
import math

import jax
import jax.numpy as jnp
from jax import lax
from jax.experimental import pallas as pl
from jax.experimental.pallas import tpu as pltpu
from jax.sharding import Mesh, PartitionSpec as P

MB = 8
SMOOTHING = 0.05
STEP_SIZE = 0.2
SCALE = math.log2(math.e) / SMOOTHING
NF, NP, NX, NY, NC = 8, 2, 4, 4, 2
CAMP = ("y", "core")
NEAR = ("pair", "x")
NN = NP * NX
N_CAMP = NY * NC
TILE = 128
CHUNK = 256
GROUP = 4
SHIFT = 16
STRIDE = 1 << SHIFT
USE_GROUP = 8
OWN = 16
F32 = jnp.float32
VMEM = pl.BlockSpec(memory_space=pltpu.VMEM)


def call(body, out_shape, operands, scratch, grant, flops=0):
    return pl.pallas_call(
        body,
        out_shape=out_shape,
        in_specs=[VMEM] * len(operands),
        out_specs=jax.tree.map(lambda _: VMEM, out_shape),
        scratch_shapes=scratch,
        compiler_params=pltpu.CompilerParams(vmem_limit_bytes=grant * 1024 * 1024),
        cost_estimate=pl.CostEstimate(flops=flops, bytes_accessed=0, transcendentals=0),
    )(*operands)


def score_step(member, number, gain_ref, cost_ref, price_of, sent_ref, ex_ref, top, total):
    top[...] = jnp.zeros_like(top)
    total[...] = jnp.zeros_like(total)
    groups = lax.div(number + GROUP - 1, GROUP)

    @pl.loop(0, groups)
    def _(g):
        for k in range(GROUP):
            s = g * GROUP + k
            block = member(s)
            price = price_of(s) * SCALE
            value = gain_ref[s].astype(F32) * SCALE - cost_ref[s].astype(F32) * price
            ex_ref[s] = value
            top[block] = jnp.maximum(top[block], jnp.where(s < number, value, 0.0))

    lane = lax.broadcasted_iota(jnp.int32, (TILE, TILE), 1)
    stats = jnp.zeros((TILE, TILE), F32)
    for b in range(MB):
        best = jnp.broadcast_to(jnp.max(top[b], axis=1, keepdims=True), (TILE, TILE))
        top[b] = best
        stats = jnp.where(lane == b, best, stats)

    @pl.loop(0, groups)
    def _(g):
        for k in range(GROUP):
            s = g * GROUP + k
            block = member(s)
            e = jnp.where(s < number, jnp.exp2(ex_ref[s] - top[block]), 0.0)
            total[block] = total[block] + e
            ex_ref[s] = cost_ref[s].astype(F32) * e

    for b in range(MB):
        stats = jnp.where(lane == MB + b, jnp.sum(total[b], axis=1, keepdims=True), stats)
    packed = jnp.transpose(stats)[: 2 * MB, :]
    for k in range(N_CAMP):
        sent_ref[k] = packed


def count_body(count_ref, live_ref):
    live_ref[...] = jnp.broadcast_to(count_ref[...], live_ref.shape)


def write_plan(rows_ref, cols_ref, live_ref, plan_ref):
    plan_ref[...] = live_ref[...]
    plan_ref[0:1, : rows_ref.shape[1]] = rows_ref[...] * STRIDE + cols_ref[...]


def read_plan(plan_ref, table, slots):
    line = plan_ref[0:1, :]
    for s in range(slots):
        table[s] = line[0, s]
    number = plan_ref[1:2, :][0, 0]
    member = lambda s: lax.shift_right_logical(table[s], SHIFT)
    camp = lambda s: table[s] & (STRIDE - 1)
    return member, camp, number


def row_of(ref, camp):
    return lambda s: ref[pl.ds(camp(s), 1), :]


def first_body(rows_ref, cols_ref, live_ref, gain_ref, cost_ref, price_ref,
               plan_ref, sent_ref, ex_ref, table, top, total):
    write_plan(rows_ref, cols_ref, live_ref, plan_ref)
    member, camp, number = read_plan(plan_ref, table, ex_ref.shape[0])
    score_step(member, number, gain_ref, cost_ref, row_of(price_ref, camp), sent_ref, ex_ref, top, total)


def line_up(lines, slots, width):
    lane = lax.broadcasted_iota(jnp.int32, (1, TILE), 1)
    out = [jnp.zeros((1, TILE), F32)] * (width // TILE + 1)
    for source, line in enumerate(lines):
        at, shift = divmod(source * slots, TILE)
        line = pltpu.roll(line, shift, 1) if shift else line
        out[at] = out[at] + jnp.where(lane >= shift, line, 0.0)
        if shift + slots > TILE:
            out[at + 1] = out[at + 1] + jnp.where(lane < shift + slots - TILE, line, 0.0)
    at, shift = divmod(len(lines) * slots, TILE)
    if shift:
        out[at] = jnp.where(lane < shift, out[at], -1.0)
    return [x.astype(jnp.int32) for x in out[: width // TILE]]


def near_index():
    return lax.axis_index("pair") * NX + lax.axis_index("x")


def want(got_ref, ids, slots):
    near, far = near_index(), lax.axis_index("far")
    first = NF * slots
    asked = jnp.transpose(jnp.concatenate([got_ref[near, first : first + NF, :]] * (TILE // NF), axis=0))
    index = lax.broadcasted_iota(jnp.int32, (OWN, 1), 0)
    names = []
    for k in range(NF):
        names.append(asked[:slots, k : k + 1].astype(jnp.int32))
        names.append(index + (near * NF + k) * OWN)
    names = jnp.concatenate(names, axis=0)
    return jnp.where(names == ids, 1.0, 0.0).astype(jnp.bfloat16)


def split_into(parts, rows, values):
    high = values.astype(jnp.bfloat16)
    parts[rows, :TILE] = high
    parts[rows, TILE:] = (values - high.astype(F32)).astype(jnp.bfloat16)


def pull_body(wanted_ref, got_ref, asked_ref, parts):
    slots = got_ref.shape[1]
    count = NN * slots
    split_into(parts, slice(0, count), got_ref[...].reshape(count, TILE))
    parts[count:, :] = jnp.zeros((parts.shape[0] - count, 2 * TILE), jnp.bfloat16)
    both = jnp.dot(wanted_ref[...], parts[...], preferred_element_type=F32)
    asked_ref[...] = (both[:, :TILE] + both[:, TILE:]).reshape(asked_ref.shape)


def second_body(plan_ref, gain_ref, cost_ref, got_ref, price_ref, allow_ref,
                held_ref, sent_ref, ex_ref, ids_ref, wanted_ref, table, top, total, parts, names):
    slots = ex_ref.shape[0]
    far = lax.axis_index("far")
    first = NF * slots
    member, camp, number = read_plan(plan_ref, table, slots)
    lines = [got_ref[k, first + f : first + f + 1, :] for k in range(NN) for f in range(NF)]
    for at, line in enumerate(line_up(lines, slots, ids_ref.shape[1])):
        ids_ref[:, at * TILE : (at + 1) * TILE] = line
    lines = [got_ref[k, pl.ds(first + far, 1), :] for k in range(NN)]
    wanted_ref[...] = want(got_ref, jnp.concatenate(line_up(lines, slots, wanted_ref.shape[1]), axis=1), slots)
    for near in range(NN):
        split_into(parts, slice(near * first, (near + 1) * first), got_ref[near, :first, :])
    own = pl.multiple_of((near_index() * NF + far) * OWN, OWN)

    @pl.loop(0, slots)
    def _(s):
        block = camp(s)
        names[pl.ds(s, 1), :] = jnp.full((1, TILE), block, jnp.int32)
        held_ref[pl.ds(s, 1), :] = price_ref[pl.ds(block, 1), :] - STEP_SIZE * allow_ref[pl.ds(block, 1), :]

    index = lax.broadcasted_iota(jnp.int32, (OWN, TILE), 0)
    names[slots:, :] = index + own
    held_ref[slots:, :] = price_ref[pl.ds(own, OWN), :] - STEP_SIZE * allow_ref[pl.ds(own, OWN), :]
    place = jnp.where(names[:, 0:1] == ids_ref[...], 1.0, 0.0).astype(jnp.bfloat16)
    both = jnp.dot(place, parts[...], preferred_element_type=F32)
    held_ref[...] = jnp.maximum(held_ref[...] + STEP_SIZE * (both[:, :TILE] + both[:, TILE:]), 0.0)
    price_of = lambda s: held_ref[pl.ds(s, 1), :]
    score_step(member, number, gain_ref, cost_ref, price_of, sent_ref, ex_ref, top, total)


def third_body(plan_ref, gain_ref, cost_ref, got_ref, held_ref, allow_ref,
               sent_ref, ex_ref, own_ref, table, top, total, price):
    slots = ex_ref.shape[0]
    member, camp, number = read_plan(plan_ref, table, slots)
    usage = jnp.sum(got_ref[...], axis=0)
    price[...] = held_ref[...] + STEP_SIZE * usage
    own = pl.multiple_of((near_index() * NF + lax.axis_index("far")) * OWN, OWN)
    own_ref[...] = jnp.maximum(price[slots:, :] - STEP_SIZE * allow_ref[pl.ds(own, OWN), :], 0.0)
    allow = row_of(allow_ref, camp)
    price_of = lambda s: jnp.maximum(price[pl.ds(s, 1), :] - STEP_SIZE * allow(s), 0.0)
    score_step(member, number, gain_ref, cost_ref, price_of, sent_ref, ex_ref, top, total)


def merge(got_ref):
    tops = got_ref[:, :MB, :]
    row_top = jnp.max(tops, axis=0)
    spare = jnp.exp2(-row_top)
    return row_top, spare, spare + jnp.sum(got_ref[:, MB:, :] * jnp.exp2(tops - row_top), axis=0)


def last_body(got_ref, ids_ref, allow_ref, stats_ref, new_ref, usage_ref, unused_ref, parts):
    _, spare, denom = merge(stats_ref)
    unused_ref[...] = spare / denom
    per = got_ref.shape[1] // NF
    slots = per - OWN
    for near in range(NN):
        rows = []
        for far in range(NF):
            first = far * per
            rows.append(got_ref[near, first : first + slots, :])
            block = (near * NF + far) * OWN
            own = slice(block, block + OWN)
            new_ref[own, :] = got_ref[near, first + slots : first + per, :] - STEP_SIZE * allow_ref[own, :]
        split_into(parts, slice(near * NF * slots, (near + 1) * NF * slots), jnp.concatenate(rows, axis=0))
    ids = ids_ref[...]
    for at in range(0, new_ref.shape[0], CHUNK):
        rows = slice(at, at + CHUNK)
        index = lax.broadcasted_iota(jnp.int32, (CHUNK, 1), 0) + at
        place = jnp.where(ids == index, 1.0, 0.0).astype(jnp.bfloat16)
        both = jnp.dot(place, parts[...], preferred_element_type=F32)
        usage = both[:, :TILE] + both[:, TILE:]
        usage_ref[rows, :] = usage
        new_ref[rows, :] = jnp.maximum(new_ref[rows, :] + STEP_SIZE * usage, 0.0)


def use_body(plan_ref, got_ref, sent_ref, ex_ref, *rest, step):
    own_ref = rest[0] if step == 2 else None
    use_ref, table, weights, use = rest[-4:]
    slots = ex_ref.shape[0]
    member, camp, number = read_plan(plan_ref, table, slots)
    row_top, _, denom = merge(got_ref)
    weight = jnp.exp2(sent_ref[0, :MB, :] - row_top) / denom
    turned = jnp.transpose(jnp.concatenate([weight] * (TILE // MB), axis=0))
    for b in range(MB):
        weights[b] = jnp.broadcast_to(turned[:, b : b + 1], (TILE, TILE))
    use[...] = jnp.zeros_like(use)

    @pl.loop(0, lax.div(number + USE_GROUP - 1, USE_GROUP))
    def _(g):
        first = pl.multiple_of(g * USE_GROUP, USE_GROUP)
        lines = [
            jnp.sum(ex_ref[first + k] * weights[member(first + k)], axis=0, keepdims=True) for k in range(USE_GROUP)
        ]
        index = lax.broadcasted_iota(jnp.int32, (USE_GROUP, 1), 0) + first
        use[pl.ds(first, USE_GROUP), :] = jnp.where(index < number, jnp.concatenate(lines, axis=0), 0.0)

    if step == 0:
        lane = lax.broadcasted_iota(jnp.int32, (MB, TILE), 1)
        ids = jnp.zeros((MB, TILE), F32)
        for s in range(slots):
            ids = jnp.where(lane == s, camp(s).astype(F32), ids)
        use[slots:, :] = ids
    elif step == 2:
        use[slots:, :] = own_ref[...]
    for k in range(NF):
        use_ref[k] = use[...]


def local(gains, costs, tile_rows, tile_cols, tile_count, duals, allowances):
    slots = gains.shape[0]
    blocks = duals.shape[0] // TILE
    price = duals.reshape(blocks, TILE)
    allow = allowances.reshape(blocks, TILE)
    whole = lambda x: jax.ShapeDtypeStruct((MB, TILE), x)
    plan_shape = whole(jnp.int32)
    live = call(count_body, plan_shape, (tile_count,), [], 4, flops=20000000000)
    shape = lambda *s: jax.ShapeDtypeStruct(s, F32)
    sent_shape, ex_shape = shape(N_CAMP, 2 * MB, TILE), shape(slots, TILE, TILE)
    table = pltpu.SMEM((slots,), jnp.int32)
    by_block = pltpu.VMEM((MB, TILE, TILE), F32)
    parts = pltpu.VMEM((NF * NN * slots, 2 * TILE), jnp.bfloat16)
    ids_shape = jax.ShapeDtypeStruct((1, NF * NN * slots), jnp.int32)
    width = -(-NN * slots // TILE) * TILE
    wanted_shape = jax.ShapeDtypeStruct((NF * (slots + OWN), width), jnp.bfloat16)

    def usage_rows(step, stats, sent, ex, own=()):
        extra = {0: MB, 1: 0, 2: OWN}[step]
        return call(functools.partial(use_body, step=step), shape(NF, slots + extra, TILE),
                    (plan, stats, sent, ex) + own, [table, by_block, pltpu.VMEM((slots + extra, TILE), F32)], 8)

    def to_near(rows):
        return lax.all_to_all(jnp.broadcast_to(rows[None], (NN,) + rows.shape), NEAR, 0, 0)

    plan, sent, ex = call(
        first_body, (plan_shape, sent_shape, ex_shape),
        (tile_rows.reshape(1, slots), tile_cols.reshape(1, slots), live, gains, costs, price),
        [table, by_block, by_block], 12)
    stats = lax.all_to_all(sent, CAMP, 0, 0)
    far = lax.all_to_all(usage_rows(0, stats, sent, ex), "far", 0, 0)
    got = to_near(jnp.concatenate([far[:, :slots].reshape(NF * slots, TILE), far[:, slots]]))

    held, sent, ex, ids, wanted = call(
        second_body, (shape(slots + OWN, TILE), sent_shape, ex_shape, ids_shape, wanted_shape),
        (plan, gains, costs, got, price, allow),
        [table, by_block, by_block, parts, pltpu.VMEM((slots + OWN, TILE), jnp.int32)], 16)
    stats = lax.all_to_all(sent, CAMP, 0, 0)
    got = lax.all_to_all(usage_rows(1, stats, sent, ex), NEAR, 0, 0)
    asked = call(pull_body, shape(NF, slots + OWN, TILE), (wanted, got),
                 [pltpu.VMEM((width, 2 * TILE), jnp.bfloat16)], 8)
    got = lax.all_to_all(asked, "far", 0, 0)

    sent, ex, own = call(
        third_body, (sent_shape, ex_shape, shape(OWN, TILE)), (plan, gains, costs, got, held, allow),
        [table, by_block, by_block, pltpu.VMEM((slots + OWN, TILE), F32)], 12)
    stats = lax.all_to_all(sent, CAMP, 0, 0)
    far = lax.all_to_all(usage_rows(2, stats, sent, ex, (own,)), "far", 0, 0)
    got = to_near(far.reshape(NF * (slots + OWN), TILE))
    price, usage, unused = call(
        last_body, (shape(blocks, TILE), shape(blocks, TILE), whole(F32)), (got, ids, allow, stats), [parts], 16)
    return (price.reshape(-1), usage.reshape(-1), unused.reshape(-1))


def solution(mesh):
    grid = Mesh(mesh.devices.reshape(NF, NP, NX, NY, NC), ("far", "pair", "x", "y", "core"))
    mem = ("far", "pair", "x")
    return jax.shard_map(
        local,
        mesh=grid,
        in_specs=(
            P(mem, None, CAMP),
            P(mem, None, CAMP),
            P(mem, CAMP),
            P(mem, CAMP),
            P(mem, CAMP),
            P(CAMP),
            P(CAMP),
        ),
        out_specs=(P(CAMP), P(CAMP), P(mem)),
        check_vma=False,
    )
```

time: 178 us -> 174 us (0.978)
  the two profiles are of different devices: /device:TPU:8 before, /device:TPU:64 now
where the time goes in v7:
time: 174 us
  blocking collectives  161 us (93%)
  Pallas kernels  9.21 us (5%)
  local copies, waits for them, and re-layouts  1.95 us (1%)
    all_to_all x2, blocking collectives, to_near(): lax.all_to_all(jnp.broadcast_to(rows[None], (NN,) + rows.shape), NEAR, 0, 0)  51.1 us
    all_to_all x1, blocking collectives, local(): far = lax.all_to_all(usage_rows(0, stats, sent, ex), 'far', 0, 0)  31 us
    all_to_all x3, blocking collectives, local(): stats = lax.all_to_all(sent, CAMP, 0, 0)  26.2 us
    all_to_all x1, blocking collectives, local(): far = lax.all_to_all(usage_rows(2, stats, sent, ex, (own,)), 'far', 0, 0)  22.9 us
    all_to_all x1, blocking collectives, local(): got = lax.all_to_all(asked, 'far', 0, 0)  20.7 us
    pallas_call x9, Pallas kernels, call(): pl.pallas_call(body, out_shape=out_shape, in_specs=[VMEM] * len(operands)...  9.21 us
    all_to_all x1, blocking collectives, local(): got = lax.all_to_all(usage_rows(1, stats, sent, ex), NEAR, 0, 0)  9.19 us

profile of v7, /device:TPU:64, one launch (start us, length us, event | category | flops | bytes accessed | tf_op | source)
XLA Modules:
  0.0 173.6 jit_solution(12060559226522261685)
XLA Ops:
  1.3 0.1 shard_map.94.live_ref
  1.4 1.2 copy-done
  2.6 0.4 copy-done.1
  3.0 0.1 copy-done.3
  3.1 1.2 shard_map.95
  4.3 10.2 %all_to_all.45.got_ref = f32[8,16,128]{2,1,0:T(8,128)S(1)} all-to-all(f32[8,16,128]{2,1,0:T(8,128)S(1)} %get-tuple-element.18.sent_ref), channel_id=1, replica_groups=mesh['far'=8,'pair'=2,'x'=4,'y'=4,'core'=2] {'y','core'}, dimensions={0} | all-to-all | bytes 131072 | tf_op jit(solution)/shard_map/all_to_all | solution.py:296
  14.5 0.6 shard_map.96
  15.1 31.0 %all_to_all.46 = f32[8,48,128]{2,1,0:T(8,128)S(1)} all-to-all(f32[8,48,128]{2,1,0:T(8,128)S(1)} %shard_map.96), channel_id=1, replica_groups=mesh['far'=8,'pair'=2,'x'=4,'y'=4,'core'=2] {'far'}, dimensions={0} | all-to-all | bytes 393216 | tf_op jit(solution)/shard_map/all_to_all | solution.py:297
  46.1 0.0 copy-start.2
  46.1 0.1 broadcast_in_dim.6
  46.2 24.1 %all_to_all.47.got_ref = f32[8,328,128]{2,1,0:T(8,128)S(1)} all-to-all(f32[8,328,128]{2,1,0:T(8,128)S(1)} %broadcast_in_dim.6), channel_id=1, replica_groups=mesh['far'=8,'pair'=2,'x'=4,'y'=4,'core'=2] {'pair','x'}, dimensions={0} | all-to-all | bytes 2686976 | tf_op jit(solution)/shard_map/all_to_all | solution.py:290
  70.3 2.4 %shard_map.97 = (f32[56,128]{1,0:T(8,128)S(1)}, f32[8,16,128]{2,1,0:T(8,128)S(1)}, f32[40,128,128]{2,1,0:T(8,128)S(1)}, s32[1,2560]{1,0:T(1,128)S(1)}, bf16[448,384]{1,0:T(8,128)(2,1)S(1)}) custom-call(s32[8,128]{1,0:T(8,128)S(1)} %get-tuple-element.17.plan_ref, bf16[40,128,128]{2,1,0:T(8,128)(2,1)S(1)} %copy-done, bf16[40,128,128]{2,1,0:T(8,128)(2,1)S(1)} %copy-done.1, ...), custom_call_target="tpu_custom_call" | custom-call | tf_op jit(solution)/shard_map/pallas_call | solution.py:32
  72.7 8.0 %all_to_all.48.got_ref = f32[8,16,128]{2,1,0:T(8,128)S(1)} all-to-all(f32[8,16,128]{2,1,0:T(8,128)S(1)} %get-tuple-element.21.sent_ref), channel_id=1, replica_groups=mesh['far'=8,'pair'=2,'x'=4,'y'=4,'core'=2] {'y','core'}, dimensions={0} | all-to-all | bytes 131072 | tf_op jit(solution)/shard_map/all_to_all | solution.py:304
  80.7 0.5 shard_map.98
  81.2 9.2 %all_to_all.49.got_ref = f32[8,40,128]{2,1,0:T(8,128)S(1)} all-to-all(f32[8,40,128]{2,1,0:T(8,128)S(1)} %shard_map.98), channel_id=1, replica_groups=mesh['far'=8,'pair'=2,'x'=4,'y'=4,'core'=2] {'pair','x'}, dimensions={0} | all-to-all | bytes 327680 | tf_op jit(solution)/shard_map/all_to_all | solution.py:305
  90.4 0.3 shard_map.99
  90.7 20.7 %all_to_all.50.got_ref = f32[8,56,128]{2,1,0:T(8,128)S(1)} all-to-all(f32[8,56,128]{2,1,0:T(8,128)S(1)} %shard_map.99), channel_id=1, replica_groups=mesh['far'=8,'pair'=2,'x'=4,'y'=4,'core'=2] {'far'}, dimensions={0} | all-to-all | bytes 458752 | tf_op jit(solution)/shard_map/all_to_all | solution.py:308
  111.4 1.2 shard_map.100
  112.6 8.0 %all_to_all.51.got_ref.stats_ref = f32[8,16,128]{2,1,0:T(8,128)S(1)} all-to-all(f32[8,16,128]{2,1,0:T(8,128)S(1)} %get-tuple-element.24.sent_ref), channel_id=1, replica_groups=mesh['far'=8,'pair'=2,'x'=4,'y'=4,'core'=2] {'y','core'}, dimensions={0} | all-to-all | bytes 131072 | tf_op jit(solution)/shard_map/all_to_all | solution.py:313
  120.6 0.5 shard_map.101
  121.1 22.9 %all_to_all.52 = f32[8,56,128]{2,1,0:T(8,128)S(1)} all-to-all(f32[8,56,128]{2,1,0:T(8,128)S(1)} %shard_map.101), channel_id=1, replica_groups=mesh['far'=8,'pair'=2,'x'=4,'y'=4,'core'=2] {'far'}, dimensions={0} | all-to-all | bytes 458752 | tf_op jit(solution)/shard_map/all_to_all | solution.py:314
  144.0 0.1 broadcast_in_dim.15
  144.1 27.0 %all_to_all.53.got_ref = f32[8,448,128]{2,1,0:T(8,128)S(1)} all-to-all(f32[8,448,128]{2,1,0:T(8,128)S(1)} %broadcast_in_dim.15), channel_id=1, replica_groups=mesh['far'=8,'pair'=2,'x'=4,'y'=4,'core'=2] {'pair','x'}, dimensions={0} | all-to-all | bytes 3670016 | tf_op jit(solution)/shard_map/all_to_all | solution.py:290
  171.1 2.5 %shard_map.102 = (f32[1024,128]{1,0:T(8,128)}, f32[1024,128]{1,0:T(8,128)}, f32[8,128]{1,0:T(8,128)}) custom-call(f32[8,448,128]{2,1,0:T(8,128)S(1)} %all_to_all.53.got_ref, s32[1,2560]{1,0:T(1,128)S(1)} %get-tuple-element.27.ids_ref, f32[1024,128]{1,0:T(8,128)S(1)} %bitcast.12, f32[8,16,128]{2,1,0:T(8,128)S(1)} %all_to_all.51.got_ref.stats_ref), custom_call_target="tpu_custom_call" | custom-call | tf_op jit(solution)/shard_map/pallas_call | solution.py:32
  (11 shorter events, 0.0 us)
Async XLA Ops:
  1.3 1.3 copy-start
  1.3 1.7 copy-start.1
  1.3 1.8 %copy-start.3 = (f32[131072]{0:T(1024)S(1)}, f32[131072]{0:T(1024)}, u32[]{:S(2)}) copy-start(f32[131072]{0:T(1024)} %param.12) | copy-start | bytes 1572868
  1.3 1.8 %copy-start.4 = (s32[40,1]{0,1:T(1,128)S(1)}, s32[40,1]{0,1:T(1,128)}, u32[]{:S(2)}) copy-start(s32[40,1]{0,1:T(1,128)} %param.9) | copy-start | bytes 484
  1.3 1.8 %copy-start.5 = (s32[40,1]{0,1:T(1,128)S(1)}, s32[40,1]{0,1:T(1,128)}, u32[]{:S(2)}) copy-start(s32[40,1]{0,1:T(1,128)} %param.10) | copy-start | bytes 484
  46.1 24.2 %copy-start.2 = (f32[131072]{0:T(1024)S(1)}, f32[131072]{0:T(1024)}, u32[]{:S(2)}) copy-start(f32[131072]{0:T(1024)} %param.13) | copy-start | bytes 1572868

commit v8 on v7

--- a/solution.py
+++ b/solution.py
@@ -24,6 +24,7 @@
 STRIDE = 1 << SHIFT
 USE_GROUP = 8
 OWN = 16
+WAIT = 20000000000
 F32 = jnp.float32
 VMEM = pl.BlockSpec(memory_space=pltpu.VMEM)
 
@@ -78,8 +79,11 @@
         sent_ref[k] = packed
 
 
-def count_body(count_ref, live_ref):
+def start_body(count_ref, cols_ref, live_ref, ids_ref):
     live_ref[...] = jnp.broadcast_to(count_ref[...], live_ref.shape)
+    line = jnp.concatenate([cols_ref[...].astype(F32), jnp.zeros((1, TILE - cols_ref.shape[1]), F32)], axis=1)
+    for k in range(NN):
+        ids_ref[k] = jnp.broadcast_to(line, (MB, TILE))
 
 
 def write_plan(rows_ref, cols_ref, live_ref, plan_ref):
@@ -127,17 +131,17 @@
     return lax.axis_index("pair") * NX + lax.axis_index("x")
 
 
-def want(got_ref, ids, slots):
-    near, far = near_index(), lax.axis_index("far")
-    first = NF * slots
-    asked = jnp.transpose(jnp.concatenate([got_ref[near, first : first + NF, :]] * (TILE // NF), axis=0))
-    index = lax.broadcasted_iota(jnp.int32, (OWN, 1), 0)
+def want(far_ref, near_ref, slots, width):
+    ids = line_up([far_ref[k, slots : slots + 1, :] for k in range(NF)], slots, width)
+    lines = jnp.concatenate([near_ref[k, 0:1, :] for k in range(NN)] * (TILE // NN), axis=0)
+    asked = jnp.transpose(lines)
+    index = lax.broadcasted_iota(jnp.int32, (OWN, 1), 0) + lax.axis_index("far") * OWN
     names = []
-    for k in range(NF):
+    for k in range(NN):
         names.append(asked[:slots, k : k + 1].astype(jnp.int32))
-        names.append(index + (near * NF + k) * OWN)
+        names.append(index + k * NF * OWN)
     names = jnp.concatenate(names, axis=0)
-    return jnp.where(names == ids, 1.0, 0.0).astype(jnp.bfloat16)
+    return jnp.where(names == jnp.concatenate(ids, axis=1), 1.0, 0.0).astype(jnp.bfloat16)
 
 
 def split_into(parts, rows, values):
@@ -146,56 +150,59 @@
     parts[rows, TILE:] = (values - high.astype(F32)).astype(jnp.bfloat16)
 
 
-def pull_body(wanted_ref, got_ref, asked_ref, parts):
-    slots = got_ref.shape[1]
-    count = NN * slots
-    split_into(parts, slice(0, count), got_ref[...].reshape(count, TILE))
+def pull(wanted, got_ref, asked_ref, parts):
+    slots = asked_ref.shape[1] - OWN
+    count = NF * slots
+    rows = jnp.concatenate([got_ref[k, :slots, :] for k in range(NF)], axis=0)
+    split_into(parts, slice(0, count), rows)
     parts[count:, :] = jnp.zeros((parts.shape[0] - count, 2 * TILE), jnp.bfloat16)
-    both = jnp.dot(wanted_ref[...], parts[...], preferred_element_type=F32)
+    both = jnp.dot(wanted, parts[...], preferred_element_type=F32)
     asked_ref[...] = (both[:, :TILE] + both[:, TILE:]).reshape(asked_ref.shape)
 
 
+def first_pull_body(got_ref, near_ref, asked_ref, wanted_ref, lines_ref, parts):
+    slots = asked_ref.shape[1] - OWN
+    for k in range(NF):
+        lines_ref[k : k + 1, :] = got_ref[k, slots : slots + 1, :]
+    wanted = want(got_ref, near_ref, asked_ref.shape[1] - OWN, wanted_ref.shape[1])
+    wanted_ref[...] = wanted
+    pull(wanted, got_ref, asked_ref, parts)
+
+
+def pull_body(got_ref, wanted_ref, asked_ref, parts):
+    pull(wanted_ref[...], got_ref, asked_ref, parts)
+
+
 def second_body(plan_ref, gain_ref, cost_ref, got_ref, price_ref, allow_ref,
-                held_ref, sent_ref, ex_ref, ids_ref, wanted_ref, table, top, total, parts, names):
+                held_ref, drop_ref, sent_ref, ex_ref, table, top, total):
     slots = ex_ref.shape[0]
-    far = lax.axis_index("far")
-    first = NF * slots
     member, camp, number = read_plan(plan_ref, table, slots)
-    lines = [got_ref[k, first + f : first + f + 1, :] for k in range(NN) for f in range(NF)]
-    for at, line in enumerate(line_up(lines, slots, ids_ref.shape[1])):
-        ids_ref[:, at * TILE : (at + 1) * TILE] = line
-    lines = [got_ref[k, pl.ds(first + far, 1), :] for k in range(NN)]
-    wanted_ref[...] = want(got_ref, jnp.concatenate(line_up(lines, slots, wanted_ref.shape[1]), axis=1), slots)
-    for near in range(NN):
-        split_into(parts, slice(near * first, (near + 1) * first), got_ref[near, :first, :])
-    own = pl.multiple_of((near_index() * NF + far) * OWN, OWN)
-
-    @pl.loop(0, slots)
-    def _(s):
-        block = camp(s)
-        names[pl.ds(s, 1), :] = jnp.full((1, TILE), block, jnp.int32)
-        held_ref[pl.ds(s, 1), :] = price_ref[pl.ds(block, 1), :] - STEP_SIZE * allow_ref[pl.ds(block, 1), :]
-
-    index = lax.broadcasted_iota(jnp.int32, (OWN, TILE), 0)
-    names[slots:, :] = index + own
-    held_ref[slots:, :] = price_ref[pl.ds(own, OWN), :] - STEP_SIZE * allow_ref[pl.ds(own, OWN), :]
-    place = jnp.where(names[:, 0:1] == ids_ref[...], 1.0, 0.0).astype(jnp.bfloat16)
-    both = jnp.dot(place, parts[...], preferred_element_type=F32)
-    held_ref[...] = jnp.maximum(held_ref[...] + STEP_SIZE * (both[:, :TILE] + both[:, TILE:]), 0.0)
+    usage = jnp.sum(got_ref[...], axis=0)
+
+    @pl.loop(0, slots // GROUP)
+    def _(g):
+        for k in range(GROUP):
+            s = g * GROUP + k
+            block = camp(s)
+            held_ref[pl.ds(s, 1), :] = price_ref[pl.ds(block, 1), :]
+            drop_ref[pl.ds(s, 1), :] = allow_ref[pl.ds(block, 1), :]
+
+    own = pl.ds(pl.multiple_of((near_index() * NF + lax.axis_index("far")) * OWN, OWN), OWN)
+    held_ref[slots:, :] = price_ref[own, :]
+    drop_ref[slots:, :] = allow_ref[own, :]
+    held_ref[...] = jnp.maximum(held_ref[...] + STEP_SIZE * (usage - drop_ref[...]), 0.0)
     price_of = lambda s: held_ref[pl.ds(s, 1), :]
     score_step(member, number, gain_ref, cost_ref, price_of, sent_ref, ex_ref, top, total)
 
 
-def third_body(plan_ref, gain_ref, cost_ref, got_ref, held_ref, allow_ref,
+def third_body(plan_ref, gain_ref, cost_ref, got_ref, held_ref, drop_ref,
                sent_ref, ex_ref, own_ref, table, top, total, price):
     slots = ex_ref.shape[0]
     member, camp, number = read_plan(plan_ref, table, slots)
     usage = jnp.sum(got_ref[...], axis=0)
-    price[...] = held_ref[...] + STEP_SIZE * usage
-    own = pl.multiple_of((near_index() * NF + lax.axis_index("far")) * OWN, OWN)
-    own_ref[...] = jnp.maximum(price[slots:, :] - STEP_SIZE * allow_ref[pl.ds(own, OWN), :], 0.0)
-    allow = row_of(allow_ref, camp)
-    price_of = lambda s: jnp.maximum(price[pl.ds(s, 1), :] - STEP_SIZE * allow(s), 0.0)
+    price[...] = jnp.maximum(held_ref[...] + STEP_SIZE * (usage - drop_ref[...]), 0.0)
+    own_ref[...] = price[slots:, :]
+    price_of = lambda s: price[pl.ds(s, 1), :]
     score_step(member, number, gain_ref, cost_ref, price_of, sent_ref, ex_ref, top, total)
 
 
@@ -206,10 +213,10 @@
     return row_top, spare, spare + jnp.sum(got_ref[:, MB:, :] * jnp.exp2(tops - row_top), axis=0)
 
 
-def last_body(got_ref, ids_ref, allow_ref, stats_ref, new_ref, usage_ref, unused_ref, parts):
+def last_body(got_ref, allow_ref, stats_ref, new_ref, usage_ref, unused_ref, parts):
     _, spare, denom = merge(stats_ref)
     unused_ref[...] = spare / denom
-    per = got_ref.shape[1] // NF
+    per = got_ref.shape[1] // NF - 1
     slots = per - OWN
     for near in range(NN):
         rows = []
@@ -220,7 +227,8 @@
             own = slice(block, block + OWN)
             new_ref[own, :] = got_ref[near, first + slots : first + per, :] - STEP_SIZE * allow_ref[own, :]
         split_into(parts, slice(near * NF * slots, (near + 1) * NF * slots), jnp.concatenate(rows, axis=0))
-    ids = ids_ref[...]
+    lines = [got_ref[k, NF * per + f : NF * per + f + 1, :] for k in range(NN) for f in range(NF)]
+    ids = jnp.concatenate(line_up(lines, slots, NN * NF * slots), axis=1)
     for at in range(0, new_ref.shape[0], CHUNK):
         rows = slice(at, at + CHUNK)
         index = lax.broadcasted_iota(jnp.int32, (CHUNK, 1), 0) + at
@@ -270,51 +278,52 @@
     price = duals.reshape(blocks, TILE)
     allow = allowances.reshape(blocks, TILE)
     whole = lambda x: jax.ShapeDtypeStruct((MB, TILE), x)
-    plan_shape = whole(jnp.int32)
-    live = call(count_body, plan_shape, (tile_count,), [], 4, flops=20000000000)
     shape = lambda *s: jax.ShapeDtypeStruct(s, F32)
     sent_shape, ex_shape = shape(N_CAMP, 2 * MB, TILE), shape(slots, TILE, TILE)
+    kept = slots + OWN
+    kept_shape, asked_shape = shape(kept, TILE), shape(NN, kept, TILE)
     table = pltpu.SMEM((slots,), jnp.int32)
     by_block = pltpu.VMEM((MB, TILE, TILE), F32)
-    parts = pltpu.VMEM((NF * NN * slots, 2 * TILE), jnp.bfloat16)
-    ids_shape = jax.ShapeDtypeStruct((1, NF * NN * slots), jnp.int32)
-    width = -(-NN * slots // TILE) * TILE
-    wanted_shape = jax.ShapeDtypeStruct((NF * (slots + OWN), width), jnp.bfloat16)
+    width = -(-NF * slots // TILE) * TILE
+    wanted_shape = jax.ShapeDtypeStruct((NN * kept, width), jnp.bfloat16)
+    column = pltpu.VMEM((width, 2 * TILE), jnp.bfloat16)
 
     def usage_rows(step, stats, sent, ex, own=()):
         extra = {0: MB, 1: 0, 2: OWN}[step]
         return call(functools.partial(use_body, step=step), shape(NF, slots + extra, TILE),
                     (plan, stats, sent, ex) + own, [table, by_block, pltpu.VMEM((slots + extra, TILE), F32)], 8)
 
-    def to_near(rows):
-        return lax.all_to_all(jnp.broadcast_to(rows[None], (NN,) + rows.shape), NEAR, 0, 0)
+    cols = tile_cols.reshape(1, slots)
+    live, ids = call(start_body, (whole(jnp.int32), shape(NN, MB, TILE)), (tile_count, cols), [], 4, flops=WAIT)
+    live, near_ids = lax.optimization_barrier((live, lax.all_to_all(ids, NEAR, 0, 0)))
 
     plan, sent, ex = call(
-        first_body, (plan_shape, sent_shape, ex_shape),
-        (tile_rows.reshape(1, slots), tile_cols.reshape(1, slots), live, gains, costs, price),
+        first_body, (whole(jnp.int32), sent_shape, ex_shape),
+        (tile_rows.reshape(1, slots), cols, live, gains, costs, price), [table, by_block, by_block], 12, flops=WAIT)
+    stats = lax.all_to_all(sent, CAMP, 0, 0)
+    far = lax.all_to_all(usage_rows(0, stats, sent, ex), "far", 0, 0)
+    asked, wanted, lines = call(
+        first_pull_body, (asked_shape, wanted_shape, whole(F32)), (far, near_ids), [column], 8)
+    got = lax.all_to_all(asked, NEAR, 0, 0)
+
+    held, drop, sent, ex = call(
+        second_body, (kept_shape, kept_shape, sent_shape, ex_shape), (plan, gains, costs, got, price, allow),
         [table, by_block, by_block], 12)
     stats = lax.all_to_all(sent, CAMP, 0, 0)
-    far = lax.all_to_all(usage_rows(0, stats, sent, ex), "far", 0, 0)
-    got = to_near(jnp.concatenate([far[:, :slots].reshape(NF * slots, TILE), far[:, slots]]))
-
-    held, sent, ex, ids, wanted = call(
-        second_body, (shape(slots + OWN, TILE), sent_shape, ex_shape, ids_shape, wanted_shape),
-        (plan, gains, costs, got, price, allow),
-        [table, by_block, by_block, parts, pltpu.VMEM((slots + OWN, TILE), jnp.int32)], 16)
-    stats = lax.all_to_all(sent, CAMP, 0, 0)
-    got = lax.all_to_all(usage_rows(1, stats, sent, ex), NEAR, 0, 0)
-    asked = call(pull_body, shape(NF, slots + OWN, TILE), (wanted, got),
-                 [pltpu.VMEM((width, 2 * TILE), jnp.bfloat16)], 8)
-    got = lax.all_to_all(asked, "far", 0, 0)
+    far = lax.all_to_all(usage_rows(1, stats, sent, ex), "far", 0, 0)
+    asked = call(pull_body, asked_shape, (far, wanted), [column], 8)
+    got = lax.all_to_all(asked, NEAR, 0, 0)
 
     sent, ex, own = call(
-        third_body, (sent_shape, ex_shape, shape(OWN, TILE)), (plan, gains, costs, got, held, allow),
-        [table, by_block, by_block, pltpu.VMEM((slots + OWN, TILE), F32)], 12)
+        third_body, (sent_shape, ex_shape, shape(OWN, TILE)), (plan, gains, costs, got, held, drop),
+        [table, by_block, by_block, pltpu.VMEM((kept, TILE), F32)], 12)
     stats = lax.all_to_all(sent, CAMP, 0, 0)
     far = lax.all_to_all(usage_rows(2, stats, sent, ex, (own,)), "far", 0, 0)
-    got = to_near(far.reshape(NF * (slots + OWN), TILE))
+    rows = jnp.concatenate([far.reshape(NF * kept, TILE), lines])
+    got = lax.all_to_all(jnp.broadcast_to(rows[None], (NN,) + rows.shape), NEAR, 0, 0)
     price, usage, unused = call(
-        last_body, (shape(blocks, TILE), shape(blocks, TILE), whole(F32)), (got, ids, allow, stats), [parts], 16)
+        last_body, (shape(blocks, TILE), shape(blocks, TILE), whole(F32)), (got, allow, stats),
+        [pltpu.VMEM((NN * NF * slots, 2 * TILE), jnp.bfloat16)], 16)
     return (price.reshape(-1), usage.reshape(-1), unused.reshape(-1))
 
 

time: 174 us -> 170 us (0.977)
  blocking collectives: 161 us -> 158 us
    all_to_all x4 -> x5, blocking collectives: 81 us -> 78.9 us  [the longest x1 27.5 us: local(): lax.all_to_all(jnp.broadcast_to(rows[None], (NN,) + rows.shape), NEAR, 0, 0)]
    pallas_call x9 -> x10, Pallas kernels: 9.21 us -> 9.78 us  [call(): pl.pallas_call(body, out_shape=out_shape, in_specs=[VMEM] * len(operands)...]
where the time goes in v8:
time: 170 us
  blocking collectives  158 us (93%)
  Pallas kernels  9.78 us (6%)
    all_to_all x1, blocking collectives, local(): far = lax.all_to_all(usage_rows(0, stats, sent, ex), 'far', 0, 0)  31.1 us
    all_to_all x1, blocking collectives, local(): lax.all_to_all(jnp.broadcast_to(rows[None], (NN,) + rows.shape), NEAR, 0, 0)  27.5 us
    all_to_all x3, blocking collectives, local(): stats = lax.all_to_all(sent, CAMP, 0, 0)  25.2 us
    all_to_all x1, blocking collectives, local(): far = lax.all_to_all(usage_rows(2, stats, sent, ex, (own,)), 'far', 0, 0)  22.5 us
    all_to_all x1, blocking collectives, local(): far = lax.all_to_all(usage_rows(1, stats, sent, ex), 'far', 0, 0)  20.1 us
    all_to_all x2, blocking collectives, local(): got = lax.all_to_all(asked, NEAR, 0, 0)  19.3 us
    all_to_all x1, blocking collectives, local(): lax.all_to_all(ids, NEAR, 0, 0)  12 us
    pallas_call x10, Pallas kernels, call(): pl.pallas_call(body, out_shape=out_shape, in_specs=[VMEM] * len(operands)...  9.78 us

profile of v8, /device:TPU:64, one launch (start us, length us, event | category | flops | bytes accessed | tf_op | source)
XLA Modules:
  0.0 169.6 jit_solution(4195087565949500481)
XLA Ops:
  1.3 0.6 copy-done.5
  2.0 0.1 shard_map.94
  2.0 12.0 %all_to_all.50.near_ref = f32[8,8,128]{2,1,0:T(8,128)S(1)} all-to-all(f32[8,8,128]{2,1,0:T(8,128)S(1)} %get-tuple-element.24), channel_id=1, replica_groups=mesh['far'=8,'pair'=2,'x'=4,'y'=4,'core'=2] {'pair','x'}, dimensions={0} | all-to-all | bytes 65536 | tf_op jit(solution)/shard_map/all_to_all | solution.py:298
  14.0 0.0 copy-done
  14.0 0.0 copy-done.3
  14.0 1.5 shard_map.95
  15.5 9.2 %all_to_all.51.got_ref = f32[8,16,128]{2,1,0:T(8,128)S(1)} all-to-all(f32[8,16,128]{2,1,0:T(8,128)S(1)} %get-tuple-element.27.sent_ref), channel_id=1, replica_groups=mesh['far'=8,'pair'=2,'x'=4,'y'=4,'core'=2] {'y','core'}, dimensions={0} | all-to-all | bytes 131072 | tf_op jit(solution)/shard_map/all_to_all | solution.py:303
  24.7 0.7 shard_map.96
  25.4 31.1 %all_to_all.52.got_ref = f32[8,48,128]{2,1,0:T(8,128)S(1)} all-to-all(f32[8,48,128]{2,1,0:T(8,128)S(1)} %shard_map.96), channel_id=1, replica_groups=mesh['far'=8,'pair'=2,'x'=4,'y'=4,'core'=2] {'far'}, dimensions={0} | all-to-all | bytes 393216 | tf_op jit(solution)/shard_map/all_to_all | solution.py:304
  56.5 0.5 shard_map.97
  57.0 9.8 %all_to_all.53.got_ref = f32[8,56,128]{2,1,0:T(8,128)S(1)} all-to-all(f32[8,56,128]{2,1,0:T(8,128)S(1)} %get-tuple-element.30), channel_id=1, replica_groups=mesh['far'=8,'pair'=2,'x'=4,'y'=4,'core'=2] {'pair','x'}, dimensions={0} | all-to-all | bytes 458752 | tf_op jit(solution)/shard_map/all_to_all | solution.py:307
  66.8 1.6 shard_map.98
  68.4 8.0 %all_to_all.54.got_ref = f32[8,16,128]{2,1,0:T(8,128)S(1)} all-to-all(f32[8,16,128]{2,1,0:T(8,128)S(1)} %get-tuple-element.31.sent_ref), channel_id=1, replica_groups=mesh['far'=8,'pair'=2,'x'=4,'y'=4,'core'=2] {'y','core'}, dimensions={0} | all-to-all | bytes 131072 | tf_op jit(solution)/shard_map/all_to_all | solution.py:312
  76.4 0.6 shard_map.99
  77.0 20.1 %all_to_all.55.got_ref = f32[8,40,128]{2,1,0:T(8,128)S(1)} all-to-all(f32[8,40,128]{2,1,0:T(8,128)S(1)} %shard_map.99), channel_id=1, replica_groups=mesh['far'=8,'pair'=2,'x'=4,'y'=4,'core'=2] {'far'}, dimensions={0} | all-to-all | bytes 327680 | tf_op jit(solution)/shard_map/all_to_all | solution.py:313
  97.1 0.3 shard_map.100
  97.4 9.5 %all_to_all.56.got_ref = f32[8,56,128]{2,1,0:T(8,128)S(1)} all-to-all(f32[8,56,128]{2,1,0:T(8,128)S(1)} %shard_map.100), channel_id=1, replica_groups=mesh['far'=8,'pair'=2,'x'=4,'y'=4,'core'=2] {'pair','x'}, dimensions={0} | all-to-all | bytes 458752 | tf_op jit(solution)/shard_map/all_to_all | solution.py:315
  106.9 1.4 shard_map.101
  108.3 8.0 %all_to_all.57.got_ref.stats_ref = f32[8,16,128]{2,1,0:T(8,128)S(1)} all-to-all(f32[8,16,128]{2,1,0:T(8,128)S(1)} %get-tuple-element.36.sent_ref), channel_id=1, replica_groups=mesh['far'=8,'pair'=2,'x'=4,'y'=4,'core'=2] {'y','core'}, dimensions={0} | all-to-all | bytes 131072 | tf_op jit(solution)/shard_map/all_to_all | solution.py:320
  116.3 0.6 shard_map.102
  116.9 22.5 %all_to_all.58 = f32[8,56,128]{2,1,0:T(8,128)S(1)} all-to-all(f32[8,56,128]{2,1,0:T(8,128)S(1)} %shard_map.102), channel_id=1, replica_groups=mesh['far'=8,'pair'=2,'x'=4,'y'=4,'core'=2] {'far'}, dimensions={0} | all-to-all | bytes 458752 | tf_op jit(solution)/shard_map/all_to_all | solution.py:321
  139.4 0.1 broadcast_in_dim.2
  139.5 27.5 %all_to_all.59.got_ref = f32[8,456,128]{2,1,0:T(8,128)S(1)} all-to-all(f32[8,456,128]{2,1,0:T(8,128)S(1)} %broadcast_in_dim.2), channel_id=1, replica_groups=mesh['far'=8,'pair'=2,'x'=4,'y'=4,'core'=2] {'pair','x'}, dimensions={0} | all-to-all | bytes 3735552 | tf_op jit(solution)/shard_map/all_to_all | solution.py:323
  167.0 2.6 %shard_map.103 = (f32[1024,128]{1,0:T(8,128)}, f32[1024,128]{1,0:T(8,128)}, f32[8,128]{1,0:T(8,128)}) custom-call(f32[8,456,128]{2,1,0:T(8,128)S(1)} %all_to_all.59.got_ref, f32[1024,128]{1,0:T(8,128)S(1)} %bitcast.9, f32[8,16,128]{2,1,0:T(8,128)S(1)} %all_to_all.57.got_ref.stats_ref), custom_call_target="tpu_custom_call" | custom-call | tf_op jit(solution)/shard_map/pallas_call | solution.py:33
  (12 shorter events, 0.0 us)
Async XLA Ops:
  1.3 0.7 copy-start.5
  1.9 12.1 %copy-start = (bf16[40,128,128]{2,1,0:T(8,128)(2,1)S(1)}, bf16[40,128,128]{2,1,0:T(8,128)(2,1)}, u32[]{:S(2)}) copy-start(bf16[40,128,128]{2,1,0:T(8,128)(2,1)} %gain_ref.5) | copy-start | bytes 3932164
  1.9 12.1 %copy-start.1 = (bf16[40,128,128]{2,1,0:T(8,128)(2,1)S(1)}, bf16[40,128,128]{2,1,0:T(8,128)(2,1)}, u32[]{:S(2)}) copy-start(bf16[40,128,128]{2,1,0:T(8,128)(2,1)} %cost_ref.5) | copy-start | bytes 3932164
  1.9 12.1 %copy-start.3 = (f32[131072]{0:T(1024)S(1)}, f32[131072]{0:T(1024)}, u32[]{:S(2)}) copy-start(f32[131072]{0:T(1024)} %param.12) | copy-start | bytes 1572868
  1.9 12.1 %copy-start.4 = (s32[40,1]{0,1:T(1,128)S(1)}, s32[40,1]{0,1:T(1,128)}, u32[]{:S(2)}) copy-start(s32[40,1]{0,1:T(1,128)} %param.9) | copy-start | bytes 484
  1.9 12.1 %copy-start.6 = (s32[40,1]{0,1:T(1,128)S(1)}, s32[40,1]{0,1:T(1,128)}, u32[]{:S(2)}) copy-start(s32[40,1]{0,1:T(1,128)} %param.10) | copy-start | bytes 484
  24.7 42.1 %copy-start.2 = (f32[131072]{0:T(1024)S(1)}, f32[131072]{0:T(1024)}, u32[]{:S(2)}) copy-start(f32[131072]{0:T(1024)} %param.13) | copy-start | bytes 1572868

commit v9 on v8

--- a/solution.py
+++ b/solution.py
@@ -19,12 +19,13 @@
 N_CAMP = NY * NC
 TILE = 128
 CHUNK = 256
-GROUP = 4
+GROUP = 8
 SHIFT = 16
 STRIDE = 1 << SHIFT
 USE_GROUP = 8
 OWN = 16
 WAIT = 20000000000
+NOTHING = -1e30
 F32 = jnp.float32
 VMEM = pl.BlockSpec(memory_space=pltpu.VMEM)
 
@@ -41,7 +42,7 @@
     )(*operands)
 
 
-def score_step(member, number, gain_ref, cost_ref, price_of, sent_ref, ex_ref, top, total):
+def score_step(member, number, gain_ref, cost_ref, price_of, sent_ref, best_ref, ex_ref, top, total):
     top[...] = jnp.zeros_like(top)
     total[...] = jnp.zeros_like(total)
     groups = lax.div(number + GROUP - 1, GROUP)
@@ -74,9 +75,12 @@
 
     for b in range(MB):
         stats = jnp.where(lane == MB + b, jnp.sum(total[b], axis=1, keepdims=True), stats)
-    packed = jnp.transpose(stats)[: 2 * MB, :]
+    packed = jnp.transpose(stats)
+    best, summed = packed[:MB, :], packed[MB : 2 * MB, :]
+    best_ref[...] = best
+    share = jnp.where(summed > 0.0, best + jnp.log2(jnp.where(summed > 0.0, summed, 1.0)), NOTHING)
     for k in range(N_CAMP):
-        sent_ref[k] = packed
+        sent_ref[k] = share
 
 
 def start_body(count_ref, cols_ref, live_ref, ids_ref):
@@ -106,10 +110,10 @@
 
 
 def first_body(rows_ref, cols_ref, live_ref, gain_ref, cost_ref, price_ref,
-               plan_ref, sent_ref, ex_ref, table, top, total):
+               plan_ref, sent_ref, best_ref, ex_ref, table, top, total):
     write_plan(rows_ref, cols_ref, live_ref, plan_ref)
     member, camp, number = read_plan(plan_ref, table, ex_ref.shape[0])
-    score_step(member, number, gain_ref, cost_ref, row_of(price_ref, camp), sent_ref, ex_ref, top, total)
+    score_step(member, number, gain_ref, cost_ref, row_of(price_ref, camp), sent_ref, best_ref, ex_ref, top, total)
 
 
 def line_up(lines, slots, width):
@@ -174,7 +178,7 @@
 
 
 def second_body(plan_ref, gain_ref, cost_ref, got_ref, price_ref, allow_ref,
-                held_ref, drop_ref, sent_ref, ex_ref, table, top, total):
+                held_ref, drop_ref, sent_ref, best_ref, ex_ref, table, top, total):
     slots = ex_ref.shape[0]
     member, camp, number = read_plan(plan_ref, table, slots)
     usage = jnp.sum(got_ref[...], axis=0)
@@ -192,25 +196,25 @@
     drop_ref[slots:, :] = allow_ref[own, :]
     held_ref[...] = jnp.maximum(held_ref[...] + STEP_SIZE * (usage - drop_ref[...]), 0.0)
     price_of = lambda s: held_ref[pl.ds(s, 1), :]
-    score_step(member, number, gain_ref, cost_ref, price_of, sent_ref, ex_ref, top, total)
+    score_step(member, number, gain_ref, cost_ref, price_of, sent_ref, best_ref, ex_ref, top, total)
 
 
 def third_body(plan_ref, gain_ref, cost_ref, got_ref, held_ref, drop_ref,
-               sent_ref, ex_ref, own_ref, table, top, total, price):
+               sent_ref, best_ref, ex_ref, own_ref, table, top, total, price):
     slots = ex_ref.shape[0]
     member, camp, number = read_plan(plan_ref, table, slots)
     usage = jnp.sum(got_ref[...], axis=0)
     price[...] = jnp.maximum(held_ref[...] + STEP_SIZE * (usage - drop_ref[...]), 0.0)
     own_ref[...] = price[slots:, :]
     price_of = lambda s: price[pl.ds(s, 1), :]
-    score_step(member, number, gain_ref, cost_ref, price_of, sent_ref, ex_ref, top, total)
+    score_step(member, number, gain_ref, cost_ref, price_of, sent_ref, best_ref, ex_ref, top, total)
 
 
 def merge(got_ref):
-    tops = got_ref[:, :MB, :]
-    row_top = jnp.max(tops, axis=0)
+    sums = got_ref[...]
+    row_top = jnp.maximum(jnp.max(sums, axis=0), 0.0)
     spare = jnp.exp2(-row_top)
-    return row_top, spare, spare + jnp.sum(got_ref[:, MB:, :] * jnp.exp2(tops - row_top), axis=0)
+    return row_top, spare, spare + jnp.sum(jnp.exp2(sums - row_top), axis=0)
 
 
 def last_body(got_ref, allow_ref, stats_ref, new_ref, usage_ref, unused_ref, parts):
@@ -239,13 +243,13 @@
         new_ref[rows, :] = jnp.maximum(new_ref[rows, :] + STEP_SIZE * usage, 0.0)
 
 
-def use_body(plan_ref, got_ref, sent_ref, ex_ref, *rest, step):
+def use_body(plan_ref, got_ref, best_ref, ex_ref, *rest, step):
     own_ref = rest[0] if step == 2 else None
     use_ref, table, weights, use = rest[-4:]
     slots = ex_ref.shape[0]
     member, camp, number = read_plan(plan_ref, table, slots)
     row_top, _, denom = merge(got_ref)
-    weight = jnp.exp2(sent_ref[0, :MB, :] - row_top) / denom
+    weight = jnp.exp2(best_ref[...] - row_top) / denom
     turned = jnp.transpose(jnp.concatenate([weight] * (TILE // MB), axis=0))
     for b in range(MB):
         weights[b] = jnp.broadcast_to(turned[:, b : b + 1], (TILE, TILE))
@@ -279,7 +283,7 @@
     allow = allowances.reshape(blocks, TILE)
     whole = lambda x: jax.ShapeDtypeStruct((MB, TILE), x)
     shape = lambda *s: jax.ShapeDtypeStruct(s, F32)
-    sent_shape, ex_shape = shape(N_CAMP, 2 * MB, TILE), shape(slots, TILE, TILE)
+    sent_shape, best_shape, ex_shape = shape(N_CAMP, MB, TILE), whole(F32), shape(slots, TILE, TILE)
     kept = slots + OWN
     kept_shape, asked_shape = shape(kept, TILE), shape(NN, kept, TILE)
     table = pltpu.SMEM((slots,), jnp.int32)
@@ -288,37 +292,37 @@
     wanted_shape = jax.ShapeDtypeStruct((NN * kept, width), jnp.bfloat16)
     column = pltpu.VMEM((width, 2 * TILE), jnp.bfloat16)
 
-    def usage_rows(step, stats, sent, ex, own=()):
+    def usage_rows(step, stats, best, ex, own=()):
         extra = {0: MB, 1: 0, 2: OWN}[step]
         return call(functools.partial(use_body, step=step), shape(NF, slots + extra, TILE),
-                    (plan, stats, sent, ex) + own, [table, by_block, pltpu.VMEM((slots + extra, TILE), F32)], 8)
+                    (plan, stats, best, ex) + own, [table, by_block, pltpu.VMEM((slots + extra, TILE), F32)], 8)
 
     cols = tile_cols.reshape(1, slots)
     live, ids = call(start_body, (whole(jnp.int32), shape(NN, MB, TILE)), (tile_count, cols), [], 4, flops=WAIT)
     live, near_ids = lax.optimization_barrier((live, lax.all_to_all(ids, NEAR, 0, 0)))
 
-    plan, sent, ex = call(
-        first_body, (whole(jnp.int32), sent_shape, ex_shape),
+    plan, sent, best, ex = call(
+        first_body, (whole(jnp.int32), sent_shape, best_shape, ex_shape),
         (tile_rows.reshape(1, slots), cols, live, gains, costs, price), [table, by_block, by_block], 12, flops=WAIT)
     stats = lax.all_to_all(sent, CAMP, 0, 0)
-    far = lax.all_to_all(usage_rows(0, stats, sent, ex), "far", 0, 0)
+    far = lax.all_to_all(usage_rows(0, stats, best, ex), "far", 0, 0)
     asked, wanted, lines = call(
         first_pull_body, (asked_shape, wanted_shape, whole(F32)), (far, near_ids), [column], 8)
     got = lax.all_to_all(asked, NEAR, 0, 0)
 
-    held, drop, sent, ex = call(
-        second_body, (kept_shape, kept_shape, sent_shape, ex_shape), (plan, gains, costs, got, price, allow),
+    held, drop, sent, best, ex = call(
+        second_body, (kept_shape, kept_shape, sent_shape, best_shape, ex_shape), (plan, gains, costs, got, price, allow),
         [table, by_block, by_block], 12)
     stats = lax.all_to_all(sent, CAMP, 0, 0)
-    far = lax.all_to_all(usage_rows(1, stats, sent, ex), "far", 0, 0)
+    far = lax.all_to_all(usage_rows(1, stats, best, ex), "far", 0, 0)
     asked = call(pull_body, asked_shape, (far, wanted), [column], 8)
     got = lax.all_to_all(asked, NEAR, 0, 0)
 
-    sent, ex, own = call(
-        third_body, (sent_shape, ex_shape, shape(OWN, TILE)), (plan, gains, costs, got, held, drop),
+    sent, best, ex, own = call(
+        third_body, (sent_shape, best_shape, ex_shape, shape(OWN, TILE)), (plan, gains, costs, got, held, drop),
         [table, by_block, by_block, pltpu.VMEM((kept, TILE), F32)], 12)
     stats = lax.all_to_all(sent, CAMP, 0, 0)
-    far = lax.all_to_all(usage_rows(2, stats, sent, ex, (own,)), "far", 0, 0)
+    far = lax.all_to_all(usage_rows(2, stats, best, ex, (own,)), "far", 0, 0)
     rows = jnp.concatenate([far.reshape(NF * kept, TILE), lines])
     got = lax.all_to_all(jnp.broadcast_to(rows[None], (NN,) + rows.shape), NEAR, 0, 0)
     price, usage, unused = call(

time: 170 us -> 169 us (level)
  no operation moved by 1% of the time
where the time goes in v9:
time: 169 us
  blocking collectives  157 us (93%)
  Pallas kernels  9.61 us (6%)
    all_to_all x1, blocking collectives, local(): far = lax.all_to_all(usage_rows(0, stats, best, ex), 'far', 0, 0)  29.5 us
    all_to_all x1, blocking collectives, local(): lax.all_to_all(jnp.broadcast_to(rows[None], (NN,) + rows.shape), NEAR, 0, 0)  27.6 us
    all_to_all x3, blocking collectives, local(): stats = lax.all_to_all(sent, CAMP, 0, 0)  25.9 us
    all_to_all x1, blocking collectives, local(): far = lax.all_to_all(usage_rows(2, stats, best, ex, (own,)), 'far', 0, 0)  22.9 us
    all_to_all x1, blocking collectives, local(): far = lax.all_to_all(usage_rows(1, stats, best, ex), 'far', 0, 0)  19.7 us
    all_to_all x2, blocking collectives, local(): got = lax.all_to_all(asked, NEAR, 0, 0)  19.6 us
    all_to_all x1, blocking collectives, local(): lax.all_to_all(ids, NEAR, 0, 0)  12 us
    pallas_call x10, Pallas kernels, call(): pl.pallas_call(body, out_shape=out_shape, in_specs=[VMEM] * len(operands)...  9.61 us

profile of v9, /device:TPU:64, one launch (start us, length us, event | category | flops | bytes accessed | tf_op | source)
XLA Modules:
  0.0 169.0 jit_solution(9913190687711874856)
XLA Ops:
  1.3 0.6 copy-done.5
  2.0 0.1 shard_map.94
  2.0 12.0 %all_to_all.50.near_ref = f32[8,8,128]{2,1,0:T(8,128)S(1)} all-to-all(f32[8,8,128]{2,1,0:T(8,128)S(1)} %get-tuple-element.27), channel_id=1, replica_groups=mesh['far'=8,'pair'=2,'x'=4,'y'=4,'core'=2] {'pair','x'}, dimensions={0} | all-to-all | bytes 65536 | tf_op jit(solution)/shard_map/all_to_all | solution.py:302
  14.0 0.0 copy-done
  14.0 0.0 copy-done.3
  14.0 1.4 shard_map.95
  15.5 10.0 %all_to_all.51.got_ref = f32[8,8,128]{2,1,0:T(8,128)S(1)} all-to-all(f32[8,8,128]{2,1,0:T(8,128)S(1)} %get-tuple-element.30), channel_id=1, replica_groups=mesh['far'=8,'pair'=2,'x'=4,'y'=4,'core'=2] {'y','core'}, dimensions={0} | all-to-all | bytes 65536 | tf_op jit(solution)/shard_map/all_to_all | solution.py:307
  25.5 0.7 shard_map.96
  26.1 29.5 %all_to_all.52.got_ref = f32[8,48,128]{2,1,0:T(8,128)S(1)} all-to-all(f32[8,48,128]{2,1,0:T(8,128)S(1)} %shard_map.96), channel_id=1, replica_groups=mesh['far'=8,'pair'=2,'x'=4,'y'=4,'core'=2] {'far'}, dimensions={0} | all-to-all | bytes 393216 | tf_op jit(solution)/shard_map/all_to_all | solution.py:308
  55.6 0.5 shard_map.97
  56.2 9.7 %all_to_all.53.got_ref = f32[8,56,128]{2,1,0:T(8,128)S(1)} all-to-all(f32[8,56,128]{2,1,0:T(8,128)S(1)} %get-tuple-element.34), channel_id=1, replica_groups=mesh['far'=8,'pair'=2,'x'=4,'y'=4,'core'=2] {'pair','x'}, dimensions={0} | all-to-all | bytes 458752 | tf_op jit(solution)/shard_map/all_to_all | solution.py:311
  65.9 1.5 shard_map.98
  67.4 8.1 %all_to_all.54.got_ref = f32[8,8,128]{2,1,0:T(8,128)S(1)} all-to-all(f32[8,8,128]{2,1,0:T(8,128)S(1)} %get-tuple-element.35), channel_id=1, replica_groups=mesh['far'=8,'pair'=2,'x'=4,'y'=4,'core'=2] {'y','core'}, dimensions={0} | all-to-all | bytes 65536 | tf_op jit(solution)/shard_map/all_to_all | solution.py:316
  75.5 0.6 shard_map.99
  76.1 19.7 %all_to_all.55.got_ref = f32[8,40,128]{2,1,0:T(8,128)S(1)} all-to-all(f32[8,40,128]{2,1,0:T(8,128)S(1)} %shard_map.99), channel_id=1, replica_groups=mesh['far'=8,'pair'=2,'x'=4,'y'=4,'core'=2] {'far'}, dimensions={0} | all-to-all | bytes 327680 | tf_op jit(solution)/shard_map/all_to_all | solution.py:317
  95.8 0.3 shard_map.100
  96.1 10.0 %all_to_all.56.got_ref = f32[8,56,128]{2,1,0:T(8,128)S(1)} all-to-all(f32[8,56,128]{2,1,0:T(8,128)S(1)} %shard_map.100), channel_id=1, replica_groups=mesh['far'=8,'pair'=2,'x'=4,'y'=4,'core'=2] {'pair','x'}, dimensions={0} | all-to-all | bytes 458752 | tf_op jit(solution)/shard_map/all_to_all | solution.py:319
  106.0 1.4 shard_map.101
  107.4 7.8 %all_to_all.57.got_ref.stats_ref = f32[8,8,128]{2,1,0:T(8,128)S(1)} all-to-all(f32[8,8,128]{2,1,0:T(8,128)S(1)} %get-tuple-element.41), channel_id=1, replica_groups=mesh['far'=8,'pair'=2,'x'=4,'y'=4,'core'=2] {'y','core'}, dimensions={0} | all-to-all | bytes 65536 | tf_op jit(solution)/shard_map/all_to_all | solution.py:324
  115.2 0.6 shard_map.102
  115.8 22.9 %all_to_all.58 = f32[8,56,128]{2,1,0:T(8,128)S(1)} all-to-all(f32[8,56,128]{2,1,0:T(8,128)S(1)} %shard_map.102), channel_id=1, replica_groups=mesh['far'=8,'pair'=2,'x'=4,'y'=4,'core'=2] {'far'}, dimensions={0} | all-to-all | bytes 458752 | tf_op jit(solution)/shard_map/all_to_all | solution.py:325
  138.7 0.1 broadcast_in_dim.2
  138.9 27.6 %all_to_all.59.got_ref = f32[8,456,128]{2,1,0:T(8,128)S(1)} all-to-all(f32[8,456,128]{2,1,0:T(8,128)S(1)} %broadcast_in_dim.2), channel_id=1, replica_groups=mesh['far'=8,'pair'=2,'x'=4,'y'=4,'core'=2] {'pair','x'}, dimensions={0} | all-to-all | bytes 3735552 | tf_op jit(solution)/shard_map/all_to_all | solution.py:327
  166.4 2.5 %shard_map.103 = (f32[1024,128]{1,0:T(8,128)}, f32[1024,128]{1,0:T(8,128)}, f32[8,128]{1,0:T(8,128)}) custom-call(f32[8,456,128]{2,1,0:T(8,128)S(1)} %all_to_all.59.got_ref, f32[1024,128]{1,0:T(8,128)S(1)} %bitcast.9, f32[8,8,128]{2,1,0:T(8,128)S(1)} %all_to_all.57.got_ref.stats_ref), custom_call_target="tpu_custom_call" | custom-call | tf_op jit(solution)/shard_map/pallas_call | solution.py:34
  (12 shorter events, 0.0 us)
Async XLA Ops:
  1.3 0.7 copy-start.5
  1.9 12.1 %copy-start = (bf16[40,128,128]{2,1,0:T(8,128)(2,1)S(1)}, bf16[40,128,128]{2,1,0:T(8,128)(2,1)}, u32[]{:S(2)}) copy-start(bf16[40,128,128]{2,1,0:T(8,128)(2,1)} %gain_ref.5) | copy-start | bytes 3932164
  1.9 12.1 %copy-start.1 = (bf16[40,128,128]{2,1,0:T(8,128)(2,1)S(1)}, bf16[40,128,128]{2,1,0:T(8,128)(2,1)}, u32[]{:S(2)}) copy-start(bf16[40,128,128]{2,1,0:T(8,128)(2,1)} %cost_ref.5) | copy-start | bytes 3932164
  1.9 12.1 %copy-start.3 = (f32[131072]{0:T(1024)S(1)}, f32[131072]{0:T(1024)}, u32[]{:S(2)}) copy-start(f32[131072]{0:T(1024)} %param.12) | copy-start | bytes 1572868
  1.9 12.1 %copy-start.4 = (s32[40,1]{0,1:T(1,128)S(1)}, s32[40,1]{0,1:T(1,128)}, u32[]{:S(2)}) copy-start(s32[40,1]{0,1:T(1,128)} %param.9) | copy-start | bytes 484
  1.9 12.1 %copy-start.6 = (s32[40,1]{0,1:T(1,128)S(1)}, s32[40,1]{0,1:T(1,128)}, u32[]{:S(2)}) copy-start(s32[40,1]{0,1:T(1,128)} %param.10) | copy-start | bytes 484
  25.5 40.4 %copy-start.2 = (f32[131072]{0:T(1024)S(1)}, f32[131072]{0:T(1024)}, u32[]{:S(2)}) copy-start(f32[131072]{0:T(1024)} %param.13) | copy-start | bytes 1572868

commit v10 on v9

--- a/solution.py
+++ b/solution.py
@@ -26,6 +26,7 @@
 OWN = 16
 WAIT = 20000000000
 NOTHING = -1e30
+DEAD = 1e6
 F32 = jnp.float32
 VMEM = pl.BlockSpec(memory_space=pltpu.VMEM)
 
@@ -42,7 +43,7 @@
     )(*operands)
 
 
-def score_step(member, number, gain_ref, cost_ref, price_of, sent_ref, best_ref, ex_ref, top, total):
+def score_step(member, number, gain_ref, cost_ref, price_of, sent_ref, best_ref, ex_ref, top, total, keep=True):
     top[...] = jnp.zeros_like(top)
     total[...] = jnp.zeros_like(total)
     groups = lax.div(number + GROUP - 1, GROUP)
@@ -52,10 +53,10 @@
         for k in range(GROUP):
             s = g * GROUP + k
             block = member(s)
-            price = price_of(s) * SCALE
+            price = jnp.where(s < number, price_of(s) * SCALE, DEAD)
             value = gain_ref[s].astype(F32) * SCALE - cost_ref[s].astype(F32) * price
             ex_ref[s] = value
-            top[block] = jnp.maximum(top[block], jnp.where(s < number, value, 0.0))
+            top[block] = jnp.maximum(top[block], value)
 
     lane = lax.broadcasted_iota(jnp.int32, (TILE, TILE), 1)
     stats = jnp.zeros((TILE, TILE), F32)
@@ -69,9 +70,10 @@
         for k in range(GROUP):
             s = g * GROUP + k
             block = member(s)
-            e = jnp.where(s < number, jnp.exp2(ex_ref[s] - top[block]), 0.0)
+            e = jnp.exp2(ex_ref[s] - top[block])
             total[block] = total[block] + e
-            ex_ref[s] = cost_ref[s].astype(F32) * e
+            if keep:
+                ex_ref[s] = cost_ref[s].astype(F32) * e
 
     for b in range(MB):
         stats = jnp.where(lane == MB + b, jnp.sum(total[b], axis=1, keepdims=True), stats)
@@ -110,10 +112,10 @@
 
 
 def first_body(rows_ref, cols_ref, live_ref, gain_ref, cost_ref, price_ref,
-               plan_ref, sent_ref, best_ref, ex_ref, table, top, total):
+               plan_ref, sent_ref, best_ref, table, top, total, score):
     write_plan(rows_ref, cols_ref, live_ref, plan_ref)
-    member, camp, number = read_plan(plan_ref, table, ex_ref.shape[0])
-    score_step(member, number, gain_ref, cost_ref, row_of(price_ref, camp), sent_ref, best_ref, ex_ref, top, total)
+    member, camp, number = read_plan(plan_ref, table, score.shape[0])
+    score_step(member, number, gain_ref, cost_ref, row_of(price_ref, camp), sent_ref, best_ref, score, top, total, False)
 
 
 def line_up(lines, slots, width):
@@ -243,35 +245,56 @@
         new_ref[rows, :] = jnp.maximum(new_ref[rows, :] + STEP_SIZE * usage, 0.0)
 
 
-def use_body(plan_ref, got_ref, best_ref, ex_ref, *rest, step):
-    own_ref = rest[0] if step == 2 else None
+def columns(lines, target):
+    turned = jnp.transpose(jnp.concatenate([lines] * (TILE // MB), axis=0))
+    for b in range(MB):
+        target[b] = jnp.broadcast_to(turned[:, b : b + 1], (TILE, TILE))
+
+
+def add_up(number, use, tile):
+    use[...] = jnp.zeros_like(use)
+
+    @pl.loop(0, lax.div(number + USE_GROUP - 1, USE_GROUP))
+    def _(g):
+        first = pl.multiple_of(g * USE_GROUP, USE_GROUP)
+        lines = [jnp.sum(tile(first + k), axis=0, keepdims=True) for k in range(USE_GROUP)]
+        index = lax.broadcasted_iota(jnp.int32, (USE_GROUP, 1), 0) + first
+        use[pl.ds(first, USE_GROUP), :] = jnp.where(index < number, jnp.concatenate(lines, axis=0), 0.0)
+
+
+def first_use_body(plan_ref, got_ref, gain_ref, cost_ref, price_ref, use_ref, table, weights, tops, use):
+    slots = gain_ref.shape[0]
+    member, camp, number = read_plan(plan_ref, table, slots)
+    row_top, _, denom = merge(got_ref)
+    columns(1.0 / denom, weights)
+    columns(row_top, tops)
+    price_of = row_of(price_ref, camp)
+
+    def tile(s):
+        price = jnp.where(s < number, price_of(s) * SCALE, DEAD)
+        cost = cost_ref[s].astype(F32)
+        score = gain_ref[s].astype(F32) * SCALE - cost * price
+        return cost * jnp.exp2(score - tops[member(s)]) * weights[member(s)]
+
+    add_up(number, use, tile)
+    lane = lax.broadcasted_iota(jnp.int32, (MB, TILE), 1)
+    ids = jnp.zeros((MB, TILE), F32)
+    for s in range(slots):
+        ids = jnp.where(lane == s, camp(s).astype(F32), ids)
+    use[slots:, :] = ids
+    for k in range(NF):
+        use_ref[k] = use[...]
+
+
+def use_body(plan_ref, got_ref, best_ref, ex_ref, *rest):
     use_ref, table, weights, use = rest[-4:]
     slots = ex_ref.shape[0]
     member, camp, number = read_plan(plan_ref, table, slots)
     row_top, _, denom = merge(got_ref)
-    weight = jnp.exp2(best_ref[...] - row_top) / denom
-    turned = jnp.transpose(jnp.concatenate([weight] * (TILE // MB), axis=0))
-    for b in range(MB):
-        weights[b] = jnp.broadcast_to(turned[:, b : b + 1], (TILE, TILE))
-    use[...] = jnp.zeros_like(use)
-
-    @pl.loop(0, lax.div(number + USE_GROUP - 1, USE_GROUP))
-    def _(g):
-        first = pl.multiple_of(g * USE_GROUP, USE_GROUP)
-        lines = [
-            jnp.sum(ex_ref[first + k] * weights[member(first + k)], axis=0, keepdims=True) for k in range(USE_GROUP)
-        ]
-        index = lax.broadcasted_iota(jnp.int32, (USE_GROUP, 1), 0) + first
-        use[pl.ds(first, USE_GROUP), :] = jnp.where(index < number, jnp.concatenate(lines, axis=0), 0.0)
-
-    if step == 0:
-        lane = lax.broadcasted_iota(jnp.int32, (MB, TILE), 1)
-        ids = jnp.zeros((MB, TILE), F32)
-        for s in range(slots):
-            ids = jnp.where(lane == s, camp(s).astype(F32), ids)
-        use[slots:, :] = ids
-    elif step == 2:
-        use[slots:, :] = own_ref[...]
+    columns(jnp.exp2(best_ref[...] - row_top) / denom, weights)
+    add_up(number, use, lambda s: ex_ref[s] * weights[member(s)])
+    if use.shape[0] > slots:
+        use[slots:, :] = rest[0][...]
     for k in range(NF):
         use_ref[k] = use[...]
 
@@ -292,20 +315,24 @@
     wanted_shape = jax.ShapeDtypeStruct((NN * kept, width), jnp.bfloat16)
     column = pltpu.VMEM((width, 2 * TILE), jnp.bfloat16)
 
-    def usage_rows(step, stats, best, ex, own=()):
-        extra = {0: MB, 1: 0, 2: OWN}[step]
-        return call(functools.partial(use_body, step=step), shape(NF, slots + extra, TILE),
-                    (plan, stats, best, ex) + own, [table, by_block, pltpu.VMEM((slots + extra, TILE), F32)], 8)
+    def usage_rows(stats, best, ex, own=()):
+        count = kept if own else slots
+        return call(use_body, shape(NF, count, TILE), (plan, stats, best, ex) + own,
+                    [table, by_block, pltpu.VMEM((count, TILE), F32)], 8)
 
     cols = tile_cols.reshape(1, slots)
     live, ids = call(start_body, (whole(jnp.int32), shape(NN, MB, TILE)), (tile_count, cols), [], 4, flops=WAIT)
-    live, near_ids = lax.optimization_barrier((live, lax.all_to_all(ids, NEAR, 0, 0)))
-
-    plan, sent, best, ex = call(
-        first_body, (whole(jnp.int32), sent_shape, best_shape, ex_shape),
-        (tile_rows.reshape(1, slots), cols, live, gains, costs, price), [table, by_block, by_block], 12, flops=WAIT)
+    near_ids = lax.all_to_all(ids, NEAR, 0, 0)
+
+    plan, sent, best = call(
+        first_body, (whole(jnp.int32), sent_shape, best_shape),
+        (tile_rows.reshape(1, slots), cols, live, gains, costs, price),
+        [table, by_block, by_block, pltpu.VMEM((slots, TILE, TILE), F32)], 12, flops=WAIT)
+    sent, near_ids = lax.optimization_barrier((sent, near_ids))
     stats = lax.all_to_all(sent, CAMP, 0, 0)
-    far = lax.all_to_all(usage_rows(0, stats, best, ex), "far", 0, 0)
+    use = call(first_use_body, shape(NF, slots + MB, TILE), (plan, stats, gains, costs, price),
+               [table, by_block, by_block, pltpu.VMEM((slots + MB, TILE), F32)], 8)
+    far = lax.all_to_all(use, "far", 0, 0)
     asked, wanted, lines = call(
         first_pull_body, (asked_shape, wanted_shape, whole(F32)), (far, near_ids), [column], 8)
     got = lax.all_to_all(asked, NEAR, 0, 0)
@@ -314,7 +341,7 @@
         second_body, (kept_shape, kept_shape, sent_shape, best_shape, ex_shape), (plan, gains, costs, got, price, allow),
         [table, by_block, by_block], 12)
     stats = lax.all_to_all(sent, CAMP, 0, 0)
-    far = lax.all_to_all(usage_rows(1, stats, best, ex), "far", 0, 0)
+    far = lax.all_to_all(usage_rows(stats, best, ex), "far", 0, 0)
     asked = call(pull_body, asked_shape, (far, wanted), [column], 8)
     got = lax.all_to_all(asked, NEAR, 0, 0)
 
@@ -322,7 +349,7 @@
         third_body, (sent_shape, best_shape, ex_shape, shape(OWN, TILE)), (plan, gains, costs, got, held, drop),
         [table, by_block, by_block, pltpu.VMEM((kept, TILE), F32)], 12)
     stats = lax.all_to_all(sent, CAMP, 0, 0)
-    far = lax.all_to_all(usage_rows(2, stats, best, ex, (own,)), "far", 0, 0)
+    far = lax.all_to_all(usage_rows(stats, best, ex, (own,)), "far", 0, 0)
     rows = jnp.concatenate([far.reshape(NF * kept, TILE), lines])
     got = lax.all_to_all(jnp.broadcast_to(rows[None], (NN,) + rows.shape), NEAR, 0, 0)
     price, usage, unused = call(

time: 169 us -> 168 us (level)
  blocking collectives: 157 us -> 145 us
  starting transfers between devices: 0 us -> 5.79 us
  waiting for transfers between devices: 0 us -> 4.38 us
    all_to_all x4 -> x3, blocking collectives: 84.1 us -> 72.4 us  [the longest x1 30.1 us: local(): far = lax.all_to_all(use, 'far', 0, 0)]
    all_to_all x0 -> x1, starting transfers between devices: none -> 5.79 us  [local(): near_ids = lax.all_to_all(ids, NEAR, 0, 0)]
    all_to_all x0 -> x1, waiting for transfers between devices: none -> 4.38 us  [local(): near_ids = lax.all_to_all(ids, NEAR, 0, 0)]
  transfers between devices with their start and end apart: 0 -> 1, of which waited for: 0 -> 1; matrix products, arithmetic and copies ran while one was open for 0% -> 0% of each run, Pallas kernels for 0% -> 1%
where the time goes in v10:
time: 168 us
  blocking collectives  145 us (86%)
  Pallas kernels  10.8 us (6%)
  starting transfers between devices  5.79 us (3%)
  waiting for transfers between devices  4.38 us (3%)
    all_to_all x1, blocking collectives, local(): far = lax.all_to_all(use, 'far', 0, 0)  30.1 us
    all_to_all x1, blocking collectives, local(): lax.all_to_all(jnp.broadcast_to(rows[None], (NN,) + rows.shape), NEAR, 0, 0)  27.5 us
    all_to_all x3, blocking collectives, local(): stats = lax.all_to_all(sent, CAMP, 0, 0)  25.7 us
    all_to_all x1, blocking collectives, local(): far = lax.all_to_all(usage_rows(stats, best, ex, (own,)), 'far', 0, 0)  22.6 us
    all_to_all x1, blocking collectives, local(): far = lax.all_to_all(usage_rows(stats, best, ex), 'far', 0, 0)  19.8 us
    all_to_all x2, blocking collectives, local(): got = lax.all_to_all(asked, NEAR, 0, 0)  19.1 us
    pallas_call x10, Pallas kernels, call(): pl.pallas_call(body, out_shape=out_shape, in_specs=[VMEM] * len(operands)...  10.8 us
    all_to_all x1, starting transfers between devices, local(): near_ids = lax.all_to_all(ids, NEAR, 0, 0)  5.79 us
  transfers between devices with their start and end apart: 1, of which 1 were waited for; matrix products, arithmetic and copies ran while one was open for 0% of the time, Pallas kernels for 1%

profile of v10, /device:TPU:64, one launch (start us, length us, event | category | flops | bytes accessed | tf_op | source)
XLA Modules:
  0.0 167.9 jit_solution(3893934506847389143)
XLA Ops:
  1.3 0.0 copy-start.5
  1.3 0.6 copy-done.5
  2.0 0.6 shard_map.94
  2.6 5.8 %all-to-all-start = ((f32[8,8,128]{2,1,0:T(8,128)}), f32[8,8,128]{2,1,0:T(8,128)S(1)}, u32[]{:S(2)}, u32[]{:S(2)}) async-start(f32[8,8,128]{2,1,0:T(8,128)} %get-tuple-element.27), calls=%async_computation | async-start | bytes 65536 | tf_op jit(solution)/shard_map/all_to_all | solution.py:325
  8.4 1.8 %shard_map.95 = (s32[8,128]{1,0:T(8,128)S(1)}, f32[8,8,128]{2,1,0:T(8,128)S(1)}, f32[8,128]{1,0:T(8,128)}) custom-call(s32[1,40]{1,0:T(1,128)S(1)} %bitcast.13, s32[1,40]{1,0:T(1,128)S(1)} %bitcast.15, s32[8,128]{1,0:T(8,128)S(1)} %get-tuple-element.24.live_ref, bf16[40,128,128]{2,1,0:T(8,128)(2,1)S(1)} %copy-done, bf16[40,128,128]{2,1,0:T(8,128)(2,1)S(1)} %copy-done.1, ...), custom_call_target="tpu_custom_call" | custom-call | flops 20000000000 | tf_op jit(solution)/shard_map/pallas_call | solution.py:35
  10.2 4.4 %all-to-all-done.near_ref = f32[8,8,128]{2,1,0:T(8,128)S(1)} async-done(((f32[8,8,128]{2,1,0:T(8,128)}), f32[8,8,128]{2,1,0:T(8,128)S(1)}, u32[]{:S(2)}, u32[]{:S(2)}) %all-to-all-start) | async-done | bytes 32800 | tf_op jit(solution)/shard_map/all_to_all | solution.py:325
  14.6 9.7 %all_to_all.50.got_ref = f32[8,8,128]{2,1,0:T(8,128)S(1)} all-to-all(f32[8,8,128]{2,1,0:T(8,128)S(1)} %get-tuple-element.28), channel_id=1, replica_groups=mesh['far'=8,'pair'=2,'x'=4,'y'=4,'core'=2] {'y','core'}, dimensions={0} | all-to-all | bytes 65536 | tf_op jit(solution)/shard_map/all_to_all | solution.py:332
  24.3 1.1 shard_map.96
  25.5 30.1 %all_to_all.51.got_ref = f32[8,48,128]{2,1,0:T(8,128)S(1)} all-to-all(f32[8,48,128]{2,1,0:T(8,128)S(1)} %shard_map.96), channel_id=1, replica_groups=mesh['far'=8,'pair'=2,'x'=4,'y'=4,'core'=2] {'far'}, dimensions={0} | all-to-all | bytes 393216 | tf_op jit(solution)/shard_map/all_to_all | solution.py:335
  55.5 0.5 shard_map.97
  56.1 9.5 %all_to_all.52.got_ref = f32[8,56,128]{2,1,0:T(8,128)S(1)} all-to-all(f32[8,56,128]{2,1,0:T(8,128)S(1)} %get-tuple-element.30), channel_id=1, replica_groups=mesh['far'=8,'pair'=2,'x'=4,'y'=4,'core'=2] {'pair','x'}, dimensions={0} | all-to-all | bytes 458752 | tf_op jit(solution)/shard_map/all_to_all | solution.py:338
  65.6 1.4 shard_map.98
  67.0 8.2 %all_to_all.53.got_ref = f32[8,8,128]{2,1,0:T(8,128)S(1)} all-to-all(f32[8,8,128]{2,1,0:T(8,128)S(1)} %get-tuple-element.31), channel_id=1, replica_groups=mesh['far'=8,'pair'=2,'x'=4,'y'=4,'core'=2] {'y','core'}, dimensions={0} | all-to-all | bytes 65536 | tf_op jit(solution)/shard_map/all_to_all | solution.py:343
  75.2 0.6 shard_map.99
  75.8 19.8 %all_to_all.54.got_ref = f32[8,40,128]{2,1,0:T(8,128)S(1)} all-to-all(f32[8,40,128]{2,1,0:T(8,128)S(1)} %shard_map.99), channel_id=1, replica_groups=mesh['far'=8,'pair'=2,'x'=4,'y'=4,'core'=2] {'far'}, dimensions={0} | all-to-all | bytes 327680 | tf_op jit(solution)/shard_map/all_to_all | solution.py:344
  95.5 0.3 shard_map.100
  95.9 9.6 %all_to_all.55.got_ref = f32[8,56,128]{2,1,0:T(8,128)S(1)} all-to-all(f32[8,56,128]{2,1,0:T(8,128)S(1)} %shard_map.100), channel_id=1, replica_groups=mesh['far'=8,'pair'=2,'x'=4,'y'=4,'core'=2] {'pair','x'}, dimensions={0} | all-to-all | bytes 458752 | tf_op jit(solution)/shard_map/all_to_all | solution.py:346
  105.5 1.3 shard_map.101
  106.7 7.8 %all_to_all.56.got_ref.stats_ref = f32[8,8,128]{2,1,0:T(8,128)S(1)} all-to-all(f32[8,8,128]{2,1,0:T(8,128)S(1)} %get-tuple-element.37), channel_id=1, replica_groups=mesh['far'=8,'pair'=2,'x'=4,'y'=4,'core'=2] {'y','core'}, dimensions={0} | all-to-all | bytes 65536 | tf_op jit(solution)/shard_map/all_to_all | solution.py:351
  114.6 0.6 shard_map.102
  115.1 22.6 %all_to_all.57 = f32[8,56,128]{2,1,0:T(8,128)S(1)} all-to-all(f32[8,56,128]{2,1,0:T(8,128)S(1)} %shard_map.102), channel_id=1, replica_groups=mesh['far'=8,'pair'=2,'x'=4,'y'=4,'core'=2] {'far'}, dimensions={0} | all-to-all | bytes 458752 | tf_op jit(solution)/shard_map/all_to_all | solution.py:352
  137.7 0.1 broadcast_in_dim.2
  137.9 27.5 %all_to_all.58.got_ref = f32[8,456,128]{2,1,0:T(8,128)S(1)} all-to-all(f32[8,456,128]{2,1,0:T(8,128)S(1)} %broadcast_in_dim.2), channel_id=1, replica_groups=mesh['far'=8,'pair'=2,'x'=4,'y'=4,'core'=2] {'pair','x'}, dimensions={0} | all-to-all | bytes 3735552 | tf_op jit(solution)/shard_map/all_to_all | solution.py:354
  165.4 2.5 %shard_map.103 = (f32[1024,128]{1,0:T(8,128)}, f32[1024,128]{1,0:T(8,128)}, f32[8,128]{1,0:T(8,128)}) custom-call(f32[8,456,128]{2,1,0:T(8,128)S(1)} %all_to_all.58.got_ref, f32[1024,128]{1,0:T(8,128)S(1)} %bitcast.12, f32[8,8,128]{2,1,0:T(8,128)S(1)} %all_to_all.56.got_ref.stats_ref), custom_call_target="tpu_custom_call" | custom-call | tf_op jit(solution)/shard_map/pallas_call | solution.py:35
  (13 shorter events, 0.0 us)
Async XLA Ops:
  1.3 0.7 copy-start.5
  1.9 6.4 %copy-start = (bf16[40,128,128]{2,1,0:T(8,128)(2,1)S(1)}, bf16[40,128,128]{2,1,0:T(8,128)(2,1)}, u32[]{:S(2)}) copy-start(bf16[40,128,128]{2,1,0:T(8,128)(2,1)} %gain_ref.7) | copy-start | bytes 3932164
  1.9 6.4 %copy-start.1 = (bf16[40,128,128]{2,1,0:T(8,128)(2,1)S(1)}, bf16[40,128,128]{2,1,0:T(8,128)(2,1)}, u32[]{:S(2)}) copy-start(bf16[40,128,128]{2,1,0:T(8,128)(2,1)} %cost_ref.7) | copy-start | bytes 3932164
  1.9 6.4 %copy-start.2 = (f32[131072]{0:T(1024)S(1)}, f32[131072]{0:T(1024)}, u32[]{:S(2)}) copy-start(f32[131072]{0:T(1024)} %param.12) | copy-start | bytes 1572868
  1.9 6.5 %copy-start.4 = (s32[40,1]{0,1:T(1,128)S(1)}, s32[40,1]{0,1:T(1,128)}, u32[]{:S(2)}) copy-start(s32[40,1]{0,1:T(1,128)} %param.9) | copy-start | bytes 484
  1.9 6.5 %copy-start.6 = (s32[40,1]{0,1:T(1,128)S(1)}, s32[40,1]{0,1:T(1,128)}, u32[]{:S(2)}) copy-start(s32[40,1]{0,1:T(1,128)} %param.10) | copy-start | bytes 484
  2.6 12.0 %all-to-all-start = ((f32[8,8,128]{2,1,0:T(8,128)}), f32[8,8,128]{2,1,0:T(8,128)S(1)}, u32[]{:S(2)}, u32[]{:S(2)}) async-start(f32[8,8,128]{2,1,0:T(8,128)} %get-tuple-element.27), calls=%async_computation | async-start | bytes 65536 | tf_op jit(solution)/shard_map/all_to_all | solution.py:325
  24.3 41.2 %copy-start.3 = (f32[131072]{0:T(1024)S(1)}, f32[131072]{0:T(1024)}, u32[]{:S(2)}) copy-start(f32[131072]{0:T(1024)} %param.13) | copy-start | bytes 1572868

commit v11 on v10

--- a/solution.py
+++ b/solution.py
@@ -137,8 +137,8 @@
     return lax.axis_index("pair") * NX + lax.axis_index("x")
 
 
-def want(far_ref, near_ref, slots, width):
-    ids = line_up([far_ref[k, slots : slots + 1, :] for k in range(NF)], slots, width)
+def want(far_lines, near_ref, slots, width):
+    ids = line_up(far_lines, slots, width)
     lines = jnp.concatenate([near_ref[k, 0:1, :] for k in range(NN)] * (TILE // NN), axis=0)
     asked = jnp.transpose(lines)
     index = lax.broadcasted_iota(jnp.int32, (OWN, 1), 0) + lax.axis_index("far") * OWN
@@ -156,10 +156,8 @@
     parts[rows, TILE:] = (values - high.astype(F32)).astype(jnp.bfloat16)
 
 
-def pull(wanted, got_ref, asked_ref, parts):
-    slots = asked_ref.shape[1] - OWN
-    count = NF * slots
-    rows = jnp.concatenate([got_ref[k, :slots, :] for k in range(NF)], axis=0)
+def pull(wanted, rows, asked_ref, parts):
+    count = rows.shape[0]
     split_into(parts, slice(0, count), rows)
     parts[count:, :] = jnp.zeros((parts.shape[0] - count, 2 * TILE), jnp.bfloat16)
     both = jnp.dot(wanted, parts[...], preferred_element_type=F32)
@@ -168,15 +166,16 @@
 
 def first_pull_body(got_ref, near_ref, asked_ref, wanted_ref, lines_ref, parts):
     slots = asked_ref.shape[1] - OWN
-    for k in range(NF):
-        lines_ref[k : k + 1, :] = got_ref[k, slots : slots + 1, :]
-    wanted = want(got_ref, near_ref, asked_ref.shape[1] - OWN, wanted_ref.shape[1])
+    first = [k * (slots + 1) for k in range(NF)]
+    lines = [got_ref[at + slots : at + slots + 1, :] for at in first]
+    lines_ref[...] = jnp.concatenate(lines, axis=0)
+    wanted = want(lines, near_ref, slots, wanted_ref.shape[1])
     wanted_ref[...] = wanted
-    pull(wanted, got_ref, asked_ref, parts)
+    pull(wanted, jnp.concatenate([got_ref[at : at + slots, :] for at in first], axis=0), asked_ref, parts)
 
 
 def pull_body(got_ref, wanted_ref, asked_ref, parts):
-    pull(wanted_ref[...], got_ref, asked_ref, parts)
+    pull(wanted_ref[...], got_ref[...].reshape(-1, TILE), asked_ref, parts)
 
 
 def second_body(plan_ref, gain_ref, cost_ref, got_ref, price_ref, allow_ref,
@@ -283,7 +282,7 @@
         ids = jnp.where(lane == s, camp(s).astype(F32), ids)
     use[slots:, :] = ids
     for k in range(NF):
-        use_ref[k] = use[...]
+        use_ref[k * (slots + 1) : (k + 1) * (slots + 1), :] = use[: slots + 1, :]
 
 
 def use_body(plan_ref, got_ref, best_ref, ex_ref, *rest):
@@ -330,9 +329,9 @@
         [table, by_block, by_block, pltpu.VMEM((slots, TILE, TILE), F32)], 12, flops=WAIT)
     sent, near_ids = lax.optimization_barrier((sent, near_ids))
     stats = lax.all_to_all(sent, CAMP, 0, 0)
-    use = call(first_use_body, shape(NF, slots + MB, TILE), (plan, stats, gains, costs, price),
+    use = call(first_use_body, shape(NF * (slots + 1), TILE), (plan, stats, gains, costs, price),
                [table, by_block, by_block, pltpu.VMEM((slots + MB, TILE), F32)], 8)
-    far = lax.all_to_all(use, "far", 0, 0)
+    far = lax.all_to_all(use.reshape(NF, slots + 1, 1, TILE), "far", 0, 0).reshape(use.shape)
     asked, wanted, lines = call(
         first_pull_body, (asked_shape, wanted_shape, whole(F32)), (far, near_ids), [column], 8)
     got = lax.all_to_all(asked, NEAR, 0, 0)

time: 168 us -> 167 us (level)
  Pallas kernels: 10.8 us -> 8.87 us
    pallas_call x10, Pallas kernels: 10.8 us -> 8.87 us  [call(): pl.pallas_call(body, out_shape=out_shape, in_specs=[VMEM] * len(operands)...]
where the time goes in v11:
time: 167 us; the launch traced here: 166 us
  blocking collectives  145 us (87%)
  Pallas kernels  8.87 us (5%)
  starting transfers between devices  5.79 us (3%)
  waiting for transfers between devices  4.79 us (3%)
    all_to_all x1, blocking collectives, local(): lax.all_to_all(use.reshape(NF, slots + 1, 1, TILE), 'far', 0, 0)  29.3 us
    all_to_all x1, blocking collectives, local(): lax.all_to_all(jnp.broadcast_to(rows[None], (NN,) + rows.shape), NEAR, 0, 0)  27.4 us
    all_to_all x3, blocking collectives, local(): stats = lax.all_to_all(sent, CAMP, 0, 0)  26 us
    all_to_all x1, blocking collectives, local(): far = lax.all_to_all(usage_rows(stats, best, ex, (own,)), 'far', 0, 0)  22.5 us
    all_to_all x1, blocking collectives, local(): far = lax.all_to_all(usage_rows(stats, best, ex), 'far', 0, 0)  20.1 us
    all_to_all x2, blocking collectives, local(): got = lax.all_to_all(asked, NEAR, 0, 0)  19.2 us
    pallas_call x10, Pallas kernels, call(): pl.pallas_call(body, out_shape=out_shape, in_specs=[VMEM] * len(operands)...  8.87 us
    all_to_all x1, starting transfers between devices, local(): near_ids = lax.all_to_all(ids, NEAR, 0, 0)  5.79 us
  transfers between devices with their start and end apart: 1, of which 1 were waited for; matrix products, arithmetic and copies ran while one was open for 0% of the time, Pallas kernels for 1%

profile of v11, /device:TPU:64, one launch (start us, length us, event | category | flops | bytes accessed | tf_op | source)
XLA Modules:
  0.0 166.2 jit_solution(13989487163077170657)
XLA Ops:
  1.3 0.0 copy-start.5
  1.3 0.6 copy-done.5
  2.0 0.6 shard_map.94
  2.6 5.8 %all-to-all-start = ((f32[8,8,128]{2,1,0:T(8,128)}), f32[8,8,128]{2,1,0:T(8,128)S(1)}, u32[]{:S(2)}, u32[]{:S(2)}) async-start(f32[8,8,128]{2,1,0:T(8,128)} %get-tuple-element.27), calls=%async_computation | async-start | bytes 65536 | tf_op jit(solution)/shard_map/all_to_all | solution.py:324
  8.4 1.4 shard_map.95
  9.8 4.8 %all-to-all-done.near_ref = f32[8,8,128]{2,1,0:T(8,128)S(1)} async-done(((f32[8,8,128]{2,1,0:T(8,128)}), f32[8,8,128]{2,1,0:T(8,128)S(1)}, u32[]{:S(2)}, u32[]{:S(2)}) %all-to-all-start) | async-done | bytes 32800 | tf_op jit(solution)/shard_map/all_to_all | solution.py:324
  14.6 9.7 %all_to_all.50.got_ref = f32[8,8,128]{2,1,0:T(8,128)S(1)} all-to-all(f32[8,8,128]{2,1,0:T(8,128)S(1)} %get-tuple-element.28), channel_id=1, replica_groups=mesh['far'=8,'pair'=2,'x'=4,'y'=4,'core'=2] {'y','core'}, dimensions={0} | all-to-all | bytes 65536 | tf_op jit(solution)/shard_map/all_to_all | solution.py:331
  24.3 0.7 shard_map.96
  25.1 29.3 %all_to_all.51 = f32[8,41,1,128]{3,2,1,0:T(1,128)S(1)} all-to-all(f32[8,41,1,128]{3,2,1,0:T(1,128)S(1)} %bitcast.15), channel_id=1, replica_groups=mesh['far'=8,'pair'=2,'x'=4,'y'=4,'core'=2] {'far'}, dimensions={0} | all-to-all | bytes 335872 | tf_op jit(solution)/shard_map/all_to_all | solution.py:334
  54.3 0.5 shard_map.97
  54.9 9.7 %all_to_all.52.got_ref = f32[8,56,128]{2,1,0:T(8,128)S(1)} all-to-all(f32[8,56,128]{2,1,0:T(8,128)S(1)} %get-tuple-element.30), channel_id=1, replica_groups=mesh['far'=8,'pair'=2,'x'=4,'y'=4,'core'=2] {'pair','x'}, dimensions={0} | all-to-all | bytes 458752 | tf_op jit(solution)/shard_map/all_to_all | solution.py:337
  64.6 1.0 shard_map.98
  65.6 7.8 %all_to_all.53.got_ref = f32[8,8,128]{2,1,0:T(8,128)S(1)} all-to-all(f32[8,8,128]{2,1,0:T(8,128)S(1)} %get-tuple-element.31), channel_id=1, replica_groups=mesh['far'=8,'pair'=2,'x'=4,'y'=4,'core'=2] {'y','core'}, dimensions={0} | all-to-all | bytes 65536 | tf_op jit(solution)/shard_map/all_to_all | solution.py:342
  73.4 0.4 shard_map.99
  73.9 20.1 %all_to_all.54.got_ref = f32[8,40,128]{2,1,0:T(8,128)S(1)} all-to-all(f32[8,40,128]{2,1,0:T(8,128)S(1)} %shard_map.99), channel_id=1, replica_groups=mesh['far'=8,'pair'=2,'x'=4,'y'=4,'core'=2] {'far'}, dimensions={0} | all-to-all | bytes 327680 | tf_op jit(solution)/shard_map/all_to_all | solution.py:343
  94.0 0.3 shard_map.100
  94.3 9.5 %all_to_all.55.got_ref = f32[8,56,128]{2,1,0:T(8,128)S(1)} all-to-all(f32[8,56,128]{2,1,0:T(8,128)S(1)} %shard_map.100), channel_id=1, replica_groups=mesh['far'=8,'pair'=2,'x'=4,'y'=4,'core'=2] {'pair','x'}, dimensions={0} | all-to-all | bytes 458752 | tf_op jit(solution)/shard_map/all_to_all | solution.py:345
  103.8 0.8 shard_map.101
  104.6 8.5 %all_to_all.56.got_ref.stats_ref = f32[8,8,128]{2,1,0:T(8,128)S(1)} all-to-all(f32[8,8,128]{2,1,0:T(8,128)S(1)} %get-tuple-element.37), channel_id=1, replica_groups=mesh['far'=8,'pair'=2,'x'=4,'y'=4,'core'=2] {'y','core'}, dimensions={0} | all-to-all | bytes 65536 | tf_op jit(solution)/shard_map/all_to_all | solution.py:350
  113.1 0.4 shard_map.102
  113.6 22.5 %all_to_all.57 = f32[8,56,128]{2,1,0:T(8,128)S(1)} all-to-all(f32[8,56,128]{2,1,0:T(8,128)S(1)} %shard_map.102), channel_id=1, replica_groups=mesh['far'=8,'pair'=2,'x'=4,'y'=4,'core'=2] {'far'}, dimensions={0} | all-to-all | bytes 458752 | tf_op jit(solution)/shard_map/all_to_all | solution.py:351
  136.1 0.1 broadcast_in_dim.2
  136.3 27.4 %all_to_all.58.got_ref = f32[8,456,128]{2,1,0:T(8,128)S(1)} all-to-all(f32[8,456,128]{2,1,0:T(8,128)S(1)} %broadcast_in_dim.2), channel_id=1, replica_groups=mesh['far'=8,'pair'=2,'x'=4,'y'=4,'core'=2] {'pair','x'}, dimensions={0} | all-to-all | bytes 3735552 | tf_op jit(solution)/shard_map/all_to_all | solution.py:353
  163.7 2.5 %shard_map.103 = (f32[1024,128]{1,0:T(8,128)}, f32[1024,128]{1,0:T(8,128)}, f32[8,128]{1,0:T(8,128)}) custom-call(f32[8,456,128]{2,1,0:T(8,128)S(1)} %all_to_all.58.got_ref, f32[1024,128]{1,0:T(8,128)S(1)} %bitcast.14, f32[8,8,128]{2,1,0:T(8,128)S(1)} %all_to_all.56.got_ref.stats_ref), custom_call_target="tpu_custom_call" | custom-call | tf_op jit(solution)/shard_map/pallas_call | solution.py:35
  (13 shorter events, 0.0 us)
Async XLA Ops:
  1.3 0.7 copy-start.5
  1.9 6.4 %copy-start = (bf16[40,128,128]{2,1,0:T(8,128)(2,1)S(1)}, bf16[40,128,128]{2,1,0:T(8,128)(2,1)}, u32[]{:S(2)}) copy-start(bf16[40,128,128]{2,1,0:T(8,128)(2,1)} %gain_ref.7) | copy-start | bytes 3932164
  1.9 6.4 %copy-start.1 = (bf16[40,128,128]{2,1,0:T(8,128)(2,1)S(1)}, bf16[40,128,128]{2,1,0:T(8,128)(2,1)}, u32[]{:S(2)}) copy-start(bf16[40,128,128]{2,1,0:T(8,128)(2,1)} %cost_ref.7) | copy-start | bytes 3932164
  1.9 6.4 %copy-start.2 = (f32[131072]{0:T(1024)S(1)}, f32[131072]{0:T(1024)}, u32[]{:S(2)}) copy-start(f32[131072]{0:T(1024)} %param.12) | copy-start | bytes 1572868
  1.9 6.5 %copy-start.4 = (s32[40,1]{0,1:T(1,128)S(1)}, s32[40,1]{0,1:T(1,128)}, u32[]{:S(2)}) copy-start(s32[40,1]{0,1:T(1,128)} %param.9) | copy-start | bytes 484
  1.9 6.5 %copy-start.6 = (s32[40,1]{0,1:T(1,128)S(1)}, s32[40,1]{0,1:T(1,128)}, u32[]{:S(2)}) copy-start(s32[40,1]{0,1:T(1,128)} %param.10) | copy-start | bytes 484
  2.6 12.0 %all-to-all-start = ((f32[8,8,128]{2,1,0:T(8,128)}), f32[8,8,128]{2,1,0:T(8,128)S(1)}, u32[]{:S(2)}, u32[]{:S(2)}) async-start(f32[8,8,128]{2,1,0:T(8,128)} %get-tuple-element.27), calls=%async_computation | async-start | bytes 65536 | tf_op jit(solution)/shard_map/all_to_all | solution.py:324
  24.3 40.3 %copy-start.3 = (f32[131072]{0:T(1024)S(1)}, f32[131072]{0:T(1024)}, u32[]{:S(2)}) copy-start(f32[131072]{0:T(1024)} %param.13) | copy-start | bytes 1572868

commit v12 on v11

--- a/solution.py
+++ b/solution.py
@@ -19,10 +19,10 @@
 N_CAMP = NY * NC
 TILE = 128
 CHUNK = 256
-GROUP = 8
+GROUP = 40
 SHIFT = 16
 STRIDE = 1 << SHIFT
-USE_GROUP = 8
+USE_GROUP = 40
 OWN = 16
 WAIT = 20000000000
 NOTHING = -1e30
@@ -88,8 +88,7 @@
 def start_body(count_ref, cols_ref, live_ref, ids_ref):
     live_ref[...] = jnp.broadcast_to(count_ref[...], live_ref.shape)
     line = jnp.concatenate([cols_ref[...].astype(F32), jnp.zeros((1, TILE - cols_ref.shape[1]), F32)], axis=1)
-    for k in range(NN):
-        ids_ref[k] = jnp.broadcast_to(line, (MB, TILE))
+    ids_ref[...] = jnp.broadcast_to(line, ids_ref.shape)
 
 
 def write_plan(rows_ref, cols_ref, live_ref, plan_ref):
@@ -139,7 +138,7 @@
 
 def want(far_lines, near_ref, slots, width):
     ids = line_up(far_lines, slots, width)
-    lines = jnp.concatenate([near_ref[k, 0:1, :] for k in range(NN)] * (TILE // NN), axis=0)
+    lines = jnp.concatenate([near_ref[...]] * (TILE // NN), axis=0)
     asked = jnp.transpose(lines)
     index = lax.broadcasted_iota(jnp.int32, (OWN, 1), 0) + lax.axis_index("far") * OWN
     names = []
@@ -320,8 +319,8 @@
                     [table, by_block, pltpu.VMEM((count, TILE), F32)], 8)
 
     cols = tile_cols.reshape(1, slots)
-    live, ids = call(start_body, (whole(jnp.int32), shape(NN, MB, TILE)), (tile_count, cols), [], 4, flops=WAIT)
-    near_ids = lax.all_to_all(ids, NEAR, 0, 0)
+    live, ids = call(start_body, (whole(jnp.int32), shape(NN, TILE)), (tile_count, cols), [], 4, flops=WAIT)
+    near_ids = lax.all_to_all(ids.reshape(NN, 1, TILE), NEAR, 0, 0).reshape(ids.shape)
 
     plan, sent, best = call(
         first_body, (whole(jnp.int32), sent_shape, best_shape),

time: 167 us -> 168 us (level)
  Pallas kernels: 8.87 us -> 12.2 us
  blocking collectives: 145 us -> 143 us
    pallas_call x10, Pallas kernels: 8.87 us -> 12.2 us  [call(): pl.pallas_call(body, out_shape=out_shape, in_specs=[VMEM] * len(operands)...]
where the time goes in v12:
time: 168 us; the launch traced here: 167 us
  blocking collectives  143 us (85%)
  Pallas kernels  12.2 us (7%)
  starting transfers between devices  5.79 us (3%)
  waiting for transfers between devices  3.86 us (2%)
    all_to_all x1, blocking collectives, local(): lax.all_to_all(use.reshape(NF, slots + 1, 1, TILE), 'far', 0, 0)  29.3 us
    all_to_all x1, blocking collectives, local(): lax.all_to_all(jnp.broadcast_to(rows[None], (NN,) + rows.shape), NEAR, 0, 0)  27.5 us
    all_to_all x3, blocking collectives, local(): stats = lax.all_to_all(sent, CAMP, 0, 0)  25.3 us
    all_to_all x1, blocking collectives, local(): far = lax.all_to_all(usage_rows(stats, best, ex, (own,)), 'far', 0, 0)  22.5 us
    all_to_all x1, blocking collectives, local(): far = lax.all_to_all(usage_rows(stats, best, ex), 'far', 0, 0)  19.5 us
    all_to_all x2, blocking collectives, local(): got = lax.all_to_all(asked, NEAR, 0, 0)  19.2 us
    pallas_call x10, Pallas kernels, call(): pl.pallas_call(body, out_shape=out_shape, in_specs=[VMEM] * len(operands)...  12.2 us
    all_to_all x1, starting transfers between devices, local(): lax.all_to_all(ids.reshape(NN, 1, TILE), NEAR, 0, 0).reshape(ids.shape)  5.79 us
  transfers between devices with their start and end apart: 1, of which 1 were waited for; matrix products, arithmetic and copies ran while one was open for 0% of the time, Pallas kernels for 1%

profile of v12, /device:TPU:64, one launch (start us, length us, event | category | flops | bytes accessed | tf_op | source)
XLA Modules:
  0.0 167.4 jit_solution(11998906627086413822)
XLA Ops:
  1.3 0.0 copy-start.5
  1.3 0.6 copy-done.5
  2.0 0.6 shard_map.94
  2.6 5.8 %all-to-all-start = ((f32[8,1,128]{2,1,0:T(1,128)}), f32[8,1,128]{2,1,0:T(1,128)S(1)}, u32[]{:S(2)}, u32[]{:S(2)}) async-start(f32[8,1,128]{2,1,0:T(1,128)} %bitcast.4), calls=%async_computation | async-start | bytes 8192 | tf_op jit(solution)/shard_map/all_to_all | solution.py:323
  8.4 2.2 %shard_map.95 = (s32[8,128]{1,0:T(8,128)S(1)}, f32[8,8,128]{2,1,0:T(8,128)S(1)}, f32[8,128]{1,0:T(8,128)}) custom-call(s32[1,40]{1,0:T(1,128)S(1)} %bitcast.22, s32[1,40]{1,0:T(1,128)S(1)} %bitcast.24, s32[8,128]{1,0:T(8,128)S(1)} %get-tuple-element.24.live_ref, bf16[40,128,128]{2,1,0:T(8,128)(2,1)S(1)} %copy-done, bf16[40,128,128]{2,1,0:T(8,128)(2,1)S(1)} %copy-done.1, ...), custom_call_target="tpu_custom_call" | custom-call | flops 20000000000 | tf_op jit(solution)/shard_map/pallas_call | solution.py:35
  10.6 3.9 %all-to-all-done = f32[8,1,128]{2,1,0:T(1,128)S(1)} async-done(((f32[8,1,128]{2,1,0:T(1,128)}), f32[8,1,128]{2,1,0:T(1,128)S(1)}, u32[]{:S(2)}, u32[]{:S(2)}) %all-to-all-start) | async-done | bytes 4128 | tf_op jit(solution)/shard_map/all_to_all | solution.py:323
  14.4 9.7 %all_to_all.50.got_ref = f32[8,8,128]{2,1,0:T(8,128)S(1)} all-to-all(f32[8,8,128]{2,1,0:T(8,128)S(1)} %get-tuple-element.28), channel_id=1, replica_groups=mesh['far'=8,'pair'=2,'x'=4,'y'=4,'core'=2] {'y','core'}, dimensions={0} | all-to-all | bytes 65536 | tf_op jit(solution)/shard_map/all_to_all | solution.py:330
  24.1 1.5 shard_map.96
  25.6 29.3 %all_to_all.51 = f32[8,41,1,128]{3,2,1,0:T(1,128)S(1)} all-to-all(f32[8,41,1,128]{3,2,1,0:T(1,128)S(1)} %bitcast.19), channel_id=1, replica_groups=mesh['far'=8,'pair'=2,'x'=4,'y'=4,'core'=2] {'far'}, dimensions={0} | all-to-all | bytes 335872 | tf_op jit(solution)/shard_map/all_to_all | solution.py:333
  54.9 0.5 shard_map.97
  55.4 9.7 %all_to_all.52.got_ref = f32[8,56,128]{2,1,0:T(8,128)S(1)} all-to-all(f32[8,56,128]{2,1,0:T(8,128)S(1)} %get-tuple-element.30), channel_id=1, replica_groups=mesh['far'=8,'pair'=2,'x'=4,'y'=4,'core'=2] {'pair','x'}, dimensions={0} | all-to-all | bytes 458752 | tf_op jit(solution)/shard_map/all_to_all | solution.py:336
  65.1 1.7 %shard_map.98 = (f32[56,128]{1,0:T(8,128)S(1)}, f32[56,128]{1,0:T(8,128)S(1)}, f32[8,8,128]{2,1,0:T(8,128)S(1)}, f32[8,128]{1,0:T(8,128)S(1)}, f32[40,128,128]{2,1,0:T(8,128)S(1)}) custom-call(s32[8,128]{1,0:T(8,128)S(1)} %get-tuple-element.25.plan_ref, bf16[40,128,128]{2,1,0:T(8,128)(2,1)S(1)} %copy-done, bf16[40,128,128]{2,1,0:T(8,128)(2,1)S(1)} %copy-done.1, ...), custom_call_target="tpu_custom_call" | custom-call | tf_op jit(solution)/shard_map/pallas_call | solution.py:35
  66.8 7.8 %all_to_all.53.got_ref = f32[8,8,128]{2,1,0:T(8,128)S(1)} all-to-all(f32[8,8,128]{2,1,0:T(8,128)S(1)} %get-tuple-element.31), channel_id=1, replica_groups=mesh['far'=8,'pair'=2,'x'=4,'y'=4,'core'=2] {'y','core'}, dimensions={0} | all-to-all | bytes 65536 | tf_op jit(solution)/shard_map/all_to_all | solution.py:341
  74.6 0.6 shard_map.99
  75.2 19.5 %all_to_all.54.got_ref = f32[8,40,128]{2,1,0:T(8,128)S(1)} all-to-all(f32[8,40,128]{2,1,0:T(8,128)S(1)} %shard_map.99), channel_id=1, replica_groups=mesh['far'=8,'pair'=2,'x'=4,'y'=4,'core'=2] {'far'}, dimensions={0} | all-to-all | bytes 327680 | tf_op jit(solution)/shard_map/all_to_all | solution.py:342
  94.8 0.3 shard_map.100
  95.1 9.5 %all_to_all.55.got_ref = f32[8,56,128]{2,1,0:T(8,128)S(1)} all-to-all(f32[8,56,128]{2,1,0:T(8,128)S(1)} %shard_map.100), channel_id=1, replica_groups=mesh['far'=8,'pair'=2,'x'=4,'y'=4,'core'=2] {'pair','x'}, dimensions={0} | all-to-all | bytes 458752 | tf_op jit(solution)/shard_map/all_to_all | solution.py:344
  104.6 1.7 shard_map.101
  106.2 7.8 %all_to_all.56.got_ref.stats_ref = f32[8,8,128]{2,1,0:T(8,128)S(1)} all-to-all(f32[8,8,128]{2,1,0:T(8,128)S(1)} %get-tuple-element.37), channel_id=1, replica_groups=mesh['far'=8,'pair'=2,'x'=4,'y'=4,'core'=2] {'y','core'}, dimensions={0} | all-to-all | bytes 65536 | tf_op jit(solution)/shard_map/all_to_all | solution.py:349
  114.1 0.6 shard_map.102
  114.7 22.5 %all_to_all.57 = f32[8,56,128]{2,1,0:T(8,128)S(1)} all-to-all(f32[8,56,128]{2,1,0:T(8,128)S(1)} %shard_map.102), channel_id=1, replica_groups=mesh['far'=8,'pair'=2,'x'=4,'y'=4,'core'=2] {'far'}, dimensions={0} | all-to-all | bytes 458752 | tf_op jit(solution)/shard_map/all_to_all | solution.py:350
  137.2 0.1 broadcast_in_dim.2
  137.4 27.5 %all_to_all.58.got_ref = f32[8,456,128]{2,1,0:T(8,128)S(1)} all-to-all(f32[8,456,128]{2,1,0:T(8,128)S(1)} %broadcast_in_dim.2), channel_id=1, replica_groups=mesh['far'=8,'pair'=2,'x'=4,'y'=4,'core'=2] {'pair','x'}, dimensions={0} | all-to-all | bytes 3735552 | tf_op jit(solution)/shard_map/all_to_all | solution.py:352
  164.9 2.5 %shard_map.103 = (f32[1024,128]{1,0:T(8,128)}, f32[1024,128]{1,0:T(8,128)}, f32[8,128]{1,0:T(8,128)}) custom-call(f32[8,456,128]{2,1,0:T(8,128)S(1)} %all_to_all.58.got_ref, f32[1024,128]{1,0:T(8,128)S(1)} %bitcast.18, f32[8,8,128]{2,1,0:T(8,128)S(1)} %all_to_all.56.got_ref.stats_ref), custom_call_target="tpu_custom_call" | custom-call | tf_op jit(solution)/shard_map/pallas_call | solution.py:35
  (13 shorter events, 0.0 us)
Async XLA Ops:
  1.3 0.7 copy-start.5
  1.9 6.4 %copy-start = (bf16[40,128,128]{2,1,0:T(8,128)(2,1)S(1)}, bf16[40,128,128]{2,1,0:T(8,128)(2,1)}, u32[]{:S(2)}) copy-start(bf16[40,128,128]{2,1,0:T(8,128)(2,1)} %gain_ref.7) | copy-start | bytes 3932164
  1.9 6.4 %copy-start.1 = (bf16[40,128,128]{2,1,0:T(8,128)(2,1)S(1)}, bf16[40,128,128]{2,1,0:T(8,128)(2,1)}, u32[]{:S(2)}) copy-start(bf16[40,128,128]{2,1,0:T(8,128)(2,1)} %cost_ref.7) | copy-start | bytes 3932164
  1.9 6.4 %copy-start.2 = (f32[131072]{0:T(1024)S(1)}, f32[131072]{0:T(1024)}, u32[]{:S(2)}) copy-start(f32[131072]{0:T(1024)} %param.12) | copy-start | bytes 1572868
  1.9 6.4 %copy-start.4 = (s32[40,1]{0,1:T(1,128)S(1)}, s32[40,1]{0,1:T(1,128)}, u32[]{:S(2)}) copy-start(s32[40,1]{0,1:T(1,128)} %param.9) | copy-start | bytes 484
  1.9 6.4 %copy-start.6 = (s32[40,1]{0,1:T(1,128)S(1)}, s32[40,1]{0,1:T(1,128)}, u32[]{:S(2)}) copy-start(s32[40,1]{0,1:T(1,128)} %param.10) | copy-start | bytes 484
  2.6 11.9 %all-to-all-start = ((f32[8,1,128]{2,1,0:T(1,128)}), f32[8,1,128]{2,1,0:T(1,128)S(1)}, u32[]{:S(2)}, u32[]{:S(2)}) async-start(f32[8,1,128]{2,1,0:T(1,128)} %bitcast.4), calls=%async_computation | async-start | bytes 8192 | tf_op jit(solution)/shard_map/all_to_all | solution.py:323
  24.1 41.0 %copy-start.3 = (f32[131072]{0:T(1024)S(1)}, f32[131072]{0:T(1024)}, u32[]{:S(2)}) copy-start(f32[131072]{0:T(1024)} %param.13) | copy-start | bytes 1572868

commit v13 on v12

--- a/solution.py
+++ b/solution.py
@@ -19,10 +19,10 @@
 N_CAMP = NY * NC
 TILE = 128
 CHUNK = 256
-GROUP = 40
+GROUP = 8
 SHIFT = 16
 STRIDE = 1 << SHIFT
-USE_GROUP = 40
+USE_GROUP = 8
 OWN = 16
 WAIT = 20000000000
 NOTHING = -1e30

time: 168 us -> 167 us (level)
  Pallas kernels: 12.2 us -> 8.84 us
  blocking collectives: 143 us -> 145 us
    pallas_call x10, Pallas kernels: 12.2 us -> 8.84 us  [call(): pl.pallas_call(body, out_shape=out_shape, in_specs=[VMEM] * len(operands)...]
where the time goes in v13:
time: 167 us
  blocking collectives  145 us (87%)
  Pallas kernels  8.84 us (5%)
  starting transfers between devices  5.79 us (3%)
  waiting for transfers between devices  4.61 us (3%)
    all_to_all x1, blocking collectives, local(): lax.all_to_all(use.reshape(NF, slots + 1, 1, TILE), 'far', 0, 0)  29.2 us
    all_to_all x1, blocking collectives, local(): lax.all_to_all(jnp.broadcast_to(rows[None], (NN,) + rows.shape), NEAR, 0, 0)  27.6 us
    all_to_all x3, blocking collectives, local(): stats = lax.all_to_all(sent, CAMP, 0, 0)  26.8 us
    all_to_all x1, blocking collectives, local(): far = lax.all_to_all(usage_rows(stats, best, ex, (own,)), 'far', 0, 0)  22.8 us
    all_to_all x1, blocking collectives, local(): far = lax.all_to_all(usage_rows(stats, best, ex), 'far', 0, 0)  20 us
    all_to_all x2, blocking collectives, local(): got = lax.all_to_all(asked, NEAR, 0, 0)  19 us
    pallas_call x10, Pallas kernels, call(): pl.pallas_call(body, out_shape=out_shape, in_specs=[VMEM] * len(operands)...  8.84 us
    all_to_all x1, starting transfers between devices, local(): lax.all_to_all(ids.reshape(NN, 1, TILE), NEAR, 0, 0).reshape(ids.shape)  5.79 us
  transfers between devices with their start and end apart: 1, of which 1 were waited for; matrix products, arithmetic and copies ran while one was open for 0% of the time, Pallas kernels for 1%

profile of v13, /device:TPU:64, one launch (start us, length us, event | category | flops | bytes accessed | tf_op | source)
XLA Modules:
  0.0 166.8 jit_solution(6463897540046773651)
XLA Ops:
  1.3 0.0 copy-start.5
  1.3 0.6 copy-done.5
  2.0 0.6 shard_map.94
  2.6 5.8 %all-to-all-start = ((f32[8,1,128]{2,1,0:T(1,128)}), f32[8,1,128]{2,1,0:T(1,128)S(1)}, u32[]{:S(2)}, u32[]{:S(2)}) async-start(f32[8,1,128]{2,1,0:T(1,128)} %bitcast.4), calls=%async_computation | async-start | bytes 8192 | tf_op jit(solution)/shard_map/all_to_all | solution.py:323
  8.4 1.4 shard_map.95
  9.8 4.6 %all-to-all-done = f32[8,1,128]{2,1,0:T(1,128)S(1)} async-done(((f32[8,1,128]{2,1,0:T(1,128)}), f32[8,1,128]{2,1,0:T(1,128)S(1)}, u32[]{:S(2)}, u32[]{:S(2)}) %all-to-all-start) | async-done | bytes 4128 | tf_op jit(solution)/shard_map/all_to_all | solution.py:323
  14.4 9.7 %all_to_all.50.got_ref = f32[8,8,128]{2,1,0:T(8,128)S(1)} all-to-all(f32[8,8,128]{2,1,0:T(8,128)S(1)} %get-tuple-element.28), channel_id=1, replica_groups=mesh['far'=8,'pair'=2,'x'=4,'y'=4,'core'=2] {'y','core'}, dimensions={0} | all-to-all | bytes 65536 | tf_op jit(solution)/shard_map/all_to_all | solution.py:330
  24.1 0.7 shard_map.96
  24.9 29.2 %all_to_all.51 = f32[8,41,1,128]{3,2,1,0:T(1,128)S(1)} all-to-all(f32[8,41,1,128]{3,2,1,0:T(1,128)S(1)} %bitcast.19), channel_id=1, replica_groups=mesh['far'=8,'pair'=2,'x'=4,'y'=4,'core'=2] {'far'}, dimensions={0} | all-to-all | bytes 335872 | tf_op jit(solution)/shard_map/all_to_all | solution.py:333
  54.1 0.5 shard_map.97
  54.6 9.5 %all_to_all.52.got_ref = f32[8,56,128]{2,1,0:T(8,128)S(1)} all-to-all(f32[8,56,128]{2,1,0:T(8,128)S(1)} %get-tuple-element.30), channel_id=1, replica_groups=mesh['far'=8,'pair'=2,'x'=4,'y'=4,'core'=2] {'pair','x'}, dimensions={0} | all-to-all | bytes 458752 | tf_op jit(solution)/shard_map/all_to_all | solution.py:336
  64.2 1.0 shard_map.98
  65.1 8.5 %all_to_all.53.got_ref = f32[8,8,128]{2,1,0:T(8,128)S(1)} all-to-all(f32[8,8,128]{2,1,0:T(8,128)S(1)} %get-tuple-element.31), channel_id=1, replica_groups=mesh['far'=8,'pair'=2,'x'=4,'y'=4,'core'=2] {'y','core'}, dimensions={0} | all-to-all | bytes 65536 | tf_op jit(solution)/shard_map/all_to_all | solution.py:341
  73.6 0.4 shard_map.99
  74.0 20.0 %all_to_all.54.got_ref = f32[8,40,128]{2,1,0:T(8,128)S(1)} all-to-all(f32[8,40,128]{2,1,0:T(8,128)S(1)} %shard_map.99), channel_id=1, replica_groups=mesh['far'=8,'pair'=2,'x'=4,'y'=4,'core'=2] {'far'}, dimensions={0} | all-to-all | bytes 327680 | tf_op jit(solution)/shard_map/all_to_all | solution.py:342
  94.0 0.3 shard_map.100
  94.4 9.5 %all_to_all.55.got_ref = f32[8,56,128]{2,1,0:T(8,128)S(1)} all-to-all(f32[8,56,128]{2,1,0:T(8,128)S(1)} %shard_map.100), channel_id=1, replica_groups=mesh['far'=8,'pair'=2,'x'=4,'y'=4,'core'=2] {'pair','x'}, dimensions={0} | all-to-all | bytes 458752 | tf_op jit(solution)/shard_map/all_to_all | solution.py:344
  103.9 0.8 shard_map.101
  104.7 8.6 %all_to_all.56.got_ref.stats_ref = f32[8,8,128]{2,1,0:T(8,128)S(1)} all-to-all(f32[8,8,128]{2,1,0:T(8,128)S(1)} %get-tuple-element.37), channel_id=1, replica_groups=mesh['far'=8,'pair'=2,'x'=4,'y'=4,'core'=2] {'y','core'}, dimensions={0} | all-to-all | bytes 65536 | tf_op jit(solution)/shard_map/all_to_all | solution.py:349
  113.3 0.4 shard_map.102
  113.8 22.8 %all_to_all.57 = f32[8,56,128]{2,1,0:T(8,128)S(1)} all-to-all(f32[8,56,128]{2,1,0:T(8,128)S(1)} %shard_map.102), channel_id=1, replica_groups=mesh['far'=8,'pair'=2,'x'=4,'y'=4,'core'=2] {'far'}, dimensions={0} | all-to-all | bytes 458752 | tf_op jit(solution)/shard_map/all_to_all | solution.py:350
  136.6 0.1 broadcast_in_dim.2
  136.7 27.6 %all_to_all.58.got_ref = f32[8,456,128]{2,1,0:T(8,128)S(1)} all-to-all(f32[8,456,128]{2,1,0:T(8,128)S(1)} %broadcast_in_dim.2), channel_id=1, replica_groups=mesh['far'=8,'pair'=2,'x'=4,'y'=4,'core'=2] {'pair','x'}, dimensions={0} | all-to-all | bytes 3735552 | tf_op jit(solution)/shard_map/all_to_all | solution.py:352
  164.3 2.5 %shard_map.103 = (f32[1024,128]{1,0:T(8,128)}, f32[1024,128]{1,0:T(8,128)}, f32[8,128]{1,0:T(8,128)}) custom-call(f32[8,456,128]{2,1,0:T(8,128)S(1)} %all_to_all.58.got_ref, f32[1024,128]{1,0:T(8,128)S(1)} %bitcast.18, f32[8,8,128]{2,1,0:T(8,128)S(1)} %all_to_all.56.got_ref.stats_ref), custom_call_target="tpu_custom_call" | custom-call | tf_op jit(solution)/shard_map/pallas_call | solution.py:35
  (13 shorter events, 0.0 us)
Async XLA Ops:
  1.3 0.7 copy-start.5
  1.9 6.4 %copy-start = (bf16[40,128,128]{2,1,0:T(8,128)(2,1)S(1)}, bf16[40,128,128]{2,1,0:T(8,128)(2,1)}, u32[]{:S(2)}) copy-start(bf16[40,128,128]{2,1,0:T(8,128)(2,1)} %gain_ref.7) | copy-start | bytes 3932164
  1.9 6.4 %copy-start.1 = (bf16[40,128,128]{2,1,0:T(8,128)(2,1)S(1)}, bf16[40,128,128]{2,1,0:T(8,128)(2,1)}, u32[]{:S(2)}) copy-start(bf16[40,128,128]{2,1,0:T(8,128)(2,1)} %cost_ref.7) | copy-start | bytes 3932164
  1.9 6.4 %copy-start.2 = (f32[131072]{0:T(1024)S(1)}, f32[131072]{0:T(1024)}, u32[]{:S(2)}) copy-start(f32[131072]{0:T(1024)} %param.12) | copy-start | bytes 1572868
  1.9 6.4 %copy-start.4 = (s32[40,1]{0,1:T(1,128)S(1)}, s32[40,1]{0,1:T(1,128)}, u32[]{:S(2)}) copy-start(s32[40,1]{0,1:T(1,128)} %param.9) | copy-start | bytes 484
  1.9 6.4 %copy-start.6 = (s32[40,1]{0,1:T(1,128)S(1)}, s32[40,1]{0,1:T(1,128)}, u32[]{:S(2)}) copy-start(s32[40,1]{0,1:T(1,128)} %param.10) | copy-start | bytes 484
  2.6 11.9 %all-to-all-start = ((f32[8,1,128]{2,1,0:T(1,128)}), f32[8,1,128]{2,1,0:T(1,128)S(1)}, u32[]{:S(2)}, u32[]{:S(2)}) async-start(f32[8,1,128]{2,1,0:T(1,128)} %bitcast.4), calls=%async_computation | async-start | bytes 8192 | tf_op jit(solution)/shard_map/all_to_all | solution.py:323
  24.1 40.0 %copy-start.3 = (f32[131072]{0:T(1024)S(1)}, f32[131072]{0:T(1024)}, u32[]{:S(2)}) copy-start(f32[131072]{0:T(1024)} %param.13) | copy-start | bytes 1572868

commit v14 on v13

--- a/solution.py
+++ b/solution.py
@@ -137,7 +137,7 @@
 
 
 def want(far_lines, near_ref, slots, width):
-    ids = line_up(far_lines, slots, width)
+    ids = line_up(far_lines, slots, -(-width // TILE) * TILE)
     lines = jnp.concatenate([near_ref[...]] * (TILE // NN), axis=0)
     asked = jnp.transpose(lines)
     index = lax.broadcasted_iota(jnp.int32, (OWN, 1), 0) + lax.axis_index("far") * OWN
@@ -146,7 +146,7 @@
         names.append(asked[:slots, k : k + 1].astype(jnp.int32))
         names.append(index + k * NF * OWN)
     names = jnp.concatenate(names, axis=0)
-    return jnp.where(names == jnp.concatenate(ids, axis=1), 1.0, 0.0).astype(jnp.bfloat16)
+    return jnp.where(names == jnp.concatenate(ids, axis=1)[:, :width], 1.0, 0.0).astype(jnp.bfloat16)
 
 
 def split_into(parts, rows, values):
@@ -158,7 +158,6 @@
 def pull(wanted, rows, asked_ref, parts):
     count = rows.shape[0]
     split_into(parts, slice(0, count), rows)
-    parts[count:, :] = jnp.zeros((parts.shape[0] - count, 2 * TILE), jnp.bfloat16)
     both = jnp.dot(wanted, parts[...], preferred_element_type=F32)
     asked_ref[...] = (both[:, :TILE] + both[:, TILE:]).reshape(asked_ref.shape)
 
@@ -309,7 +308,7 @@
     kept_shape, asked_shape = shape(kept, TILE), shape(NN, kept, TILE)
     table = pltpu.SMEM((slots,), jnp.int32)
     by_block = pltpu.VMEM((MB, TILE, TILE), F32)
-    width = -(-NF * slots // TILE) * TILE
+    width = NF * slots
     wanted_shape = jax.ShapeDtypeStruct((NN * kept, width), jnp.bfloat16)
     column = pltpu.VMEM((width, 2 * TILE), jnp.bfloat16)
 

time: 167 us -> 167 us (level)
  Pallas kernels: 8.84 us -> 10.8 us
    pallas_call x10, Pallas kernels: 8.84 us -> 10.8 us  [call(): pl.pallas_call(body, out_shape=out_shape, in_specs=[VMEM] * len(operands)...]
where the time goes in v14:
time: 167 us
  blocking collectives  144 us (86%)
  Pallas kernels  10.8 us (6%)
  starting transfers between devices  5.79 us (3%)
  waiting for transfers between devices  4.2 us (3%)
    all_to_all x1, blocking collectives, local(): lax.all_to_all(use.reshape(NF, slots + 1, 1, TILE), 'far', 0, 0)  28.8 us
    all_to_all x1, blocking collectives, local(): lax.all_to_all(jnp.broadcast_to(rows[None], (NN,) + rows.shape), NEAR, 0, 0)  27.6 us
    all_to_all x3, blocking collectives, local(): stats = lax.all_to_all(sent, CAMP, 0, 0)  25.3 us
    all_to_all x1, blocking collectives, local(): far = lax.all_to_all(usage_rows(stats, best, ex, (own,)), 'far', 0, 0)  23.1 us
    all_to_all x1, blocking collectives, local(): far = lax.all_to_all(usage_rows(stats, best, ex), 'far', 0, 0)  19.6 us
    all_to_all x2, blocking collectives, local(): got = lax.all_to_all(asked, NEAR, 0, 0)  19.2 us
    pallas_call x10, Pallas kernels, call(): pl.pallas_call(body, out_shape=out_shape, in_specs=[VMEM] * len(operands)...  10.8 us
    all_to_all x1, starting transfers between devices, local(): lax.all_to_all(ids.reshape(NN, 1, TILE), NEAR, 0, 0).reshape(ids.shape)  5.79 us
  transfers between devices with their start and end apart: 1, of which 1 were waited for; matrix products, arithmetic and copies ran while one was open for 0% of the time, Pallas kernels for 1%

profile of v14, /device:TPU:64, one launch (start us, length us, event | category | flops | bytes accessed | tf_op | source)
XLA Modules:
  0.0 166.6 jit_solution(11516025641515456216)
XLA Ops:
  1.3 0.0 copy-start.5
  1.3 0.6 copy-done.5
  2.0 0.6 shard_map.94
  2.6 5.8 %all-to-all-start = ((f32[8,1,128]{2,1,0:T(1,128)}), f32[8,1,128]{2,1,0:T(1,128)S(1)}, u32[]{:S(2)}, u32[]{:S(2)}) async-start(f32[8,1,128]{2,1,0:T(1,128)} %bitcast.4), calls=%async_computation | async-start | bytes 8192 | tf_op jit(solution)/shard_map/all_to_all | solution.py:322
  8.4 1.8 %shard_map.95 = (s32[8,128]{1,0:T(8,128)S(1)}, f32[8,8,128]{2,1,0:T(8,128)S(1)}, f32[8,128]{1,0:T(8,128)}) custom-call(s32[1,40]{1,0:T(1,128)S(1)} %bitcast.22, s32[1,40]{1,0:T(1,128)S(1)} %bitcast.24, s32[8,128]{1,0:T(8,128)S(1)} %get-tuple-element.24.live_ref, bf16[40,128,128]{2,1,0:T(8,128)(2,1)S(1)} %copy-done, bf16[40,128,128]{2,1,0:T(8,128)(2,1)S(1)} %copy-done.1, ...), custom_call_target="tpu_custom_call" | custom-call | flops 20000000000 | tf_op jit(solution)/shard_map/pallas_call | solution.py:35
  10.2 4.2 %all-to-all-done = f32[8,1,128]{2,1,0:T(1,128)S(1)} async-done(((f32[8,1,128]{2,1,0:T(1,128)}), f32[8,1,128]{2,1,0:T(1,128)S(1)}, u32[]{:S(2)}, u32[]{:S(2)}) %all-to-all-start) | async-done | bytes 4128 | tf_op jit(solution)/shard_map/all_to_all | solution.py:322
  14.4 9.7 %all_to_all.50.got_ref = f32[8,8,128]{2,1,0:T(8,128)S(1)} all-to-all(f32[8,8,128]{2,1,0:T(8,128)S(1)} %get-tuple-element.28), channel_id=1, replica_groups=mesh['far'=8,'pair'=2,'x'=4,'y'=4,'core'=2] {'y','core'}, dimensions={0} | all-to-all | bytes 65536 | tf_op jit(solution)/shard_map/all_to_all | solution.py:329
  24.1 1.1 shard_map.96
  25.3 28.8 %all_to_all.51 = f32[8,41,1,128]{3,2,1,0:T(1,128)S(1)} all-to-all(f32[8,41,1,128]{3,2,1,0:T(1,128)S(1)} %bitcast.19), channel_id=1, replica_groups=mesh['far'=8,'pair'=2,'x'=4,'y'=4,'core'=2] {'far'}, dimensions={0} | all-to-all | bytes 335872 | tf_op jit(solution)/shard_map/all_to_all | solution.py:332
  54.1 0.5 shard_map.97
  54.6 9.7 %all_to_all.52.got_ref = f32[8,56,128]{2,1,0:T(8,128)S(1)} all-to-all(f32[8,56,128]{2,1,0:T(8,128)S(1)} %get-tuple-element.30), channel_id=1, replica_groups=mesh['far'=8,'pair'=2,'x'=4,'y'=4,'core'=2] {'pair','x'}, dimensions={0} | all-to-all | bytes 458752 | tf_op jit(solution)/shard_map/all_to_all | solution.py:335
  64.4 1.4 shard_map.98
  65.8 7.8 %all_to_all.53.got_ref = f32[8,8,128]{2,1,0:T(8,128)S(1)} all-to-all(f32[8,8,128]{2,1,0:T(8,128)S(1)} %get-tuple-element.31), channel_id=1, replica_groups=mesh['far'=8,'pair'=2,'x'=4,'y'=4,'core'=2] {'y','core'}, dimensions={0} | all-to-all | bytes 65536 | tf_op jit(solution)/shard_map/all_to_all | solution.py:340
  73.6 0.6 shard_map.99
  74.2 19.6 %all_to_all.54.got_ref = f32[8,40,128]{2,1,0:T(8,128)S(1)} all-to-all(f32[8,40,128]{2,1,0:T(8,128)S(1)} %shard_map.99), channel_id=1, replica_groups=mesh['far'=8,'pair'=2,'x'=4,'y'=4,'core'=2] {'far'}, dimensions={0} | all-to-all | bytes 327680 | tf_op jit(solution)/shard_map/all_to_all | solution.py:341
  93.8 0.3 shard_map.100
  94.1 9.5 %all_to_all.55.got_ref = f32[8,56,128]{2,1,0:T(8,128)S(1)} all-to-all(f32[8,56,128]{2,1,0:T(8,128)S(1)} %shard_map.100), channel_id=1, replica_groups=mesh['far'=8,'pair'=2,'x'=4,'y'=4,'core'=2] {'pair','x'}, dimensions={0} | all-to-all | bytes 458752 | tf_op jit(solution)/shard_map/all_to_all | solution.py:343
  103.6 1.3 shard_map.101
  104.8 7.8 %all_to_all.56.got_ref.stats_ref = f32[8,8,128]{2,1,0:T(8,128)S(1)} all-to-all(f32[8,8,128]{2,1,0:T(8,128)S(1)} %get-tuple-element.37), channel_id=1, replica_groups=mesh['far'=8,'pair'=2,'x'=4,'y'=4,'core'=2] {'y','core'}, dimensions={0} | all-to-all | bytes 65536 | tf_op jit(solution)/shard_map/all_to_all | solution.py:348
  112.7 0.6 shard_map.102
  113.2 23.1 %all_to_all.57 = f32[8,56,128]{2,1,0:T(8,128)S(1)} all-to-all(f32[8,56,128]{2,1,0:T(8,128)S(1)} %shard_map.102), channel_id=1, replica_groups=mesh['far'=8,'pair'=2,'x'=4,'y'=4,'core'=2] {'far'}, dimensions={0} | all-to-all | bytes 458752 | tf_op jit(solution)/shard_map/all_to_all | solution.py:349
  136.3 0.1 broadcast_in_dim.2
  136.5 27.6 %all_to_all.58.got_ref = f32[8,456,128]{2,1,0:T(8,128)S(1)} all-to-all(f32[8,456,128]{2,1,0:T(8,128)S(1)} %broadcast_in_dim.2), channel_id=1, replica_groups=mesh['far'=8,'pair'=2,'x'=4,'y'=4,'core'=2] {'pair','x'}, dimensions={0} | all-to-all | bytes 3735552 | tf_op jit(solution)/shard_map/all_to_all | solution.py:351
  164.0 2.5 %shard_map.103 = (f32[1024,128]{1,0:T(8,128)}, f32[1024,128]{1,0:T(8,128)}, f32[8,128]{1,0:T(8,128)}) custom-call(f32[8,456,128]{2,1,0:T(8,128)S(1)} %all_to_all.58.got_ref, f32[1024,128]{1,0:T(8,128)S(1)} %bitcast.18, f32[8,8,128]{2,1,0:T(8,128)S(1)} %all_to_all.56.got_ref.stats_ref), custom_call_target="tpu_custom_call" | custom-call | tf_op jit(solution)/shard_map/pallas_call | solution.py:35
  (13 shorter events, 0.0 us)
Async XLA Ops:
  1.3 0.7 copy-start.5
  1.9 6.4 %copy-start = (bf16[40,128,128]{2,1,0:T(8,128)(2,1)S(1)}, bf16[40,128,128]{2,1,0:T(8,128)(2,1)}, u32[]{:S(2)}) copy-start(bf16[40,128,128]{2,1,0:T(8,128)(2,1)} %gain_ref.7) | copy-start | bytes 3932164
  1.9 6.4 %copy-start.1 = (bf16[40,128,128]{2,1,0:T(8,128)(2,1)S(1)}, bf16[40,128,128]{2,1,0:T(8,128)(2,1)}, u32[]{:S(2)}) copy-start(bf16[40,128,128]{2,1,0:T(8,128)(2,1)} %cost_ref.7) | copy-start | bytes 3932164
  1.9 6.4 %copy-start.2 = (f32[131072]{0:T(1024)S(1)}, f32[131072]{0:T(1024)}, u32[]{:S(2)}) copy-start(f32[131072]{0:T(1024)} %param.12) | copy-start | bytes 1572868
  1.9 6.4 %copy-start.4 = (s32[40,1]{0,1:T(1,128)S(1)}, s32[40,1]{0,1:T(1,128)}, u32[]{:S(2)}) copy-start(s32[40,1]{0,1:T(1,128)} %param.9) | copy-start | bytes 484
  1.9 6.4 %copy-start.6 = (s32[40,1]{0,1:T(1,128)S(1)}, s32[40,1]{0,1:T(1,128)}, u32[]{:S(2)}) copy-start(s32[40,1]{0,1:T(1,128)} %param.10) | copy-start | bytes 484
  2.6 11.9 %all-to-all-start = ((f32[8,1,128]{2,1,0:T(1,128)}), f32[8,1,128]{2,1,0:T(1,128)S(1)}, u32[]{:S(2)}, u32[]{:S(2)}) async-start(f32[8,1,128]{2,1,0:T(1,128)} %bitcast.4), calls=%async_computation | async-start | bytes 8192 | tf_op jit(solution)/shard_map/all_to_all | solution.py:322
  24.1 40.2 %copy-start.3 = (f32[131072]{0:T(1024)S(1)}, f32[131072]{0:T(1024)}, u32[]{:S(2)}) copy-start(f32[131072]{0:T(1024)} %param.13) | copy-start | bytes 1572868
